TPU v7x, 32 devices: a whole 2x2x4 slice. The times are simulated.
32 devices in a mesh: row: 4 (over z), wide: 8 (over y, x, core).
Axes of the slice: x: 2, y: 2, z: 4, core: 2. Of those that a mesh axis runs over, the one named last changes fastest.
Arguments:
- hidden: bfloat16 [4096, 2048], P(('row', 'wide')), may hold values from -6 to 6
- modality: int32 [4096], P(('row', 'wide')), may hold values from 0 to 2
- norm_gain: bfloat16 [2048], replicated, may hold values from 0.099609375 to 1.8984375
- in_proj: bfloat16 [3, 2048, 2, 4096], P(None, None, None, 'wide'), may hold values from -0.125 to 0.125
- conv_weight: bfloat16 [4, 4096], P(None, 'wide'), may hold values from -3 to 3
- conv_bias: bfloat16 [4096], P('wide'), may hold values from -3 to 3
- x_proj_dt: bfloat16 [4096, 128], replicated, may hold values from -0.09375 to 0.09375
- x_proj_bc: bfloat16 [4096, 32], replicated, may hold values from -0.09375 to 0.09375
- dt_proj: bfloat16 [128, 4096], replicated, may hold values from -0.5 to 0.5
- dt_bias: float32 [4096], replicated, may hold values from -5 to -3
- a_log: float32 [16, 4096], replicated, may hold values from -8 to 0.2
- skip_weight: float32 [4096], replicated, may hold values from 0.5 to 1.5
- out_proj: bfloat16 [3, 4096, 2048], P(None, 'wide'), may hold values from -0.09375 to 0.09375
- cotangent: bfloat16 [4096, 2048], P(('row', 'wide')), may hold values from -6 to 6
Outputs:
- output: bfloat16 [4096, 2048], P(('row', 'wide'))
- grad_hidden: float32 [4096, 2048], P(('row', 'wide'))
- grad_norm_gain: float32 [2048], P('wide')
- grad_in_proj: float32 [3, 2048, 2, 4096], P(None, None, None, 'wide')
- grad_conv_weight: float32 [4, 4096], P(None, 'wide')
- grad_conv_bias: float32 [4096], P('wide')
- grad_x_proj_dt: float32 [4096, 128], P('wide')
- grad_x_proj_bc: float32 [4096, 32], P('wide')
- grad_dt_proj: float32 [128, 4096], P(None, 'wide')
- grad_dt_bias: float32 [4096], P('wide')
- grad_a_log: float32 [16, 4096], P(None, 'wide')
- grad_skip_weight: float32 [4096], P('wide')
- grad_out_proj: float32 [3, 4096, 2048], P(None, 'wide')
All inputs are finite; a program needn't handle non-finite values.
Results may differ from a plain program's by a relative error of at most 0.02.
Values may be sent and summed in bfloat16 or wider, within the bound.
No kernel may reach another device: no remote copies, remote signals or barrier semaphores. Data moves between devices by JAX's collectives and lax.ppermute only.
A program may use at most 320 MiB of HBM per device.

v0:
```python
import jax
import jax.numpy as jnp
from jax import lax
from jax.sharding import PartitionSpec as P

EPS = 1e-05
LIMIT = 131072


def entering(array, axis, join, neutral, backward):
    count = lax.axis_size(axis)
    place = lax.axis_index(axis)
    ahead = count - 1 - place if backward else place
    gathered = jax.tree.map(
        lambda a, kind: lax.all_gather(a.astype(kind), axis), array, (jnp.bfloat16, jnp.bfloat16)
    )
    state = jax.tree.map(lambda a, e: jnp.zeros_like(a) + jnp.asarray(e, a.dtype), array, neutral)

    def one(lap, state):
        source = count - 1 - lap if backward else lap
        return join(
            state,
            jax.tree.map(
                lambda a, own: lax.dynamic_index_in_dim(a, source, 0, False).astype(own.dtype),
                gathered,
                array,
            ),
        )

    return lax.fori_loop(0, ahead, one, state)


def combine(earlier_pair, later_pair):
    decay_one, state_one = earlier_pair
    decay_two, state_two = later_pair
    return (decay_one * decay_two, decay_two * state_one + state_two)


def contract(left, right, left_dim, right_dim):
    return lax.dot_general(
        left, right, (((left_dim,), (right_dim,)), ((), ())), preferred_element_type=jnp.float32
    )


def block_rows(row_count, chan_count):
    block_size = row_count
    while block_size > 8 and block_size * chan_count > LIMIT:
        block_size = block_size // 2
    while row_count % block_size:
        block_size = block_size // 2
    return block_size


def group_span(row_count):
    span_rows = min(512, row_count)
    while row_count % span_rows:
        span_rows = span_rows // 2
    return span_rows


def modal_order(modal_ids):
    order = jnp.argsort(modal_ids, stable=True)
    inverse = jnp.argsort(order)
    return (order, inverse)


def grouped_apply(rows, modal_ids, weights, right_dim, order, inverse):
    sorted_rows = rows[order]
    sorted_ids = modal_ids[order]
    row_count = rows.shape[0]
    span_rows = group_span(row_count)
    block_count = row_count // span_rows
    out_cols = weights.shape[2 - right_dim]

    def block_product(pieces):
        block, id_block = pieces
        running = jnp.zeros((span_rows, out_cols), jnp.float32)
        for modal_id in range(weights.shape[0]):

            def block_take_block():
                return jnp.where(
                    (id_block == modal_id)[:, None],
                    contract(block, weights[modal_id], 1, right_dim),
                    0.0,
                )

            def block_skip_block():
                return jnp.zeros((span_rows, out_cols), jnp.float32)

            present = (id_block[0] <= modal_id) & (modal_id <= id_block[-1])
            running = running + lax.cond(present, block_take_block, block_skip_block)
        return running

    result = lax.map(
        block_product,
        (
            sorted_rows.reshape(block_count, span_rows, rows.shape[1]),
            sorted_ids.reshape(block_count, span_rows),
        ),
    )
    return result.reshape(row_count, out_cols)[inverse]


def grouped_grad(left, right, modal_ids, order, mod_count):
    sorted_left = left[order]
    sorted_right = right[order]
    sorted_ids = modal_ids[order]
    row_count = left.shape[0]
    span_rows = group_span(row_count)
    block_count = row_count // span_rows

    def accumulate(acc, pieces):
        left_block, right_block, id_block = pieces
        for modal_id in range(mod_count):

            def accumulate_take_block():
                masked = jnp.where(
                    (id_block == modal_id)[:, None], left_block, jnp.zeros_like(left_block)
                )
                return contract(masked, right_block, 0, 0)

            def accumulate_skip_block():
                return jnp.zeros((left.shape[1], right.shape[1]), jnp.float32)

            present = (id_block[0] <= modal_id) & (modal_id <= id_block[-1])
            acc = acc.at[modal_id].add(
                lax.cond(present, accumulate_take_block, accumulate_skip_block)
            )
        return (acc, None)

    initial = jnp.zeros((mod_count, left.shape[1], right.shape[1]), jnp.float32)
    pieces = (
        sorted_left.reshape(block_count, span_rows, left.shape[1]),
        sorted_right.reshape(block_count, span_rows, right.shape[1]),
        sorted_ids.reshape(block_count, span_rows),
    )
    summed, _ = lax.scan(accumulate, initial, pieces)
    return summed


def to_stretches(tensor):
    return lax.all_to_all(tensor, "wide", split_axis=0, concat_axis=1, tiled=True)


def to_channels(tensor):
    return lax.all_to_all(tensor, "wide", split_axis=1, concat_axis=0, tiled=True)


def edge_state(exponent_rows, coef_rows, weight_rows, decay_rate):
    row_count, chan_count = exponent_rows.shape
    block_size = block_rows(row_count, chan_count)
    block_count = row_count // block_size

    def add_block(acc, pieces):
        exp_block, coef_block, weight_block = pieces
        term = (
            jnp.exp(exp_block[:, None, :] * decay_rate[None])
            * weight_block[:, None, :]
            * coef_block[:, :, None]
        )
        return (acc + jnp.sum(term, 0), None)

    pieces = tuple(
        (
            tensor.reshape(block_count, block_size, tensor.shape[1])
            for tensor in (exponent_rows, coef_rows, weight_rows)
        )
    )
    summed, _ = lax.scan(add_block, jnp.zeros(decay_rate.shape, jnp.float32), pieces)
    return summed


def forward_states(steps_dt, values, input_coef, output_coef, decay_rate, skip_gain, entry_state):
    row_count, chan_count = steps_dt.shape
    block_size = block_rows(row_count, chan_count)
    block_count = row_count // block_size

    def advance(carried, pieces):
        step_block, value_block, in_block, out_block = pieces
        factor = jnp.exp(step_block[:, None, :] * decay_rate[None])
        inject = (step_block * value_block)[:, None, :] * in_block[:, :, None]
        decay_run, local_part = lax.associative_scan(combine, (factor, inject), axis=0)
        states = local_part + decay_run * carried[None]
        result = jnp.sum(states * out_block[:, :, None], axis=1) + skip_gain[None] * value_block
        return (states[-1], (result, carried))

    pieces = tuple(
        (
            tensor.reshape(block_count, block_size, tensor.shape[1])
            for tensor in (steps_dt, values, input_coef, output_coef)
        )
    )
    final_state, stacked = lax.scan(advance, entry_state, pieces)
    results, starts = stacked
    return (final_state, results.reshape(row_count, chan_count), starts)


def backward_states(
    steps_dt, values, input_coef, output_coef, decay_rate, skip_gain, grad_out, starts, incoming
):
    row_count, chan_count = steps_dt.shape
    block_size = block_rows(row_count, chan_count)
    block_count = row_count // block_size

    def retreat(carried, pieces):
        step_block, value_block, in_block, out_block, grad_block, start_state = pieces
        factor = jnp.exp(step_block[:, None, :] * decay_rate[None])
        feed_back = grad_block[:, None, :] * out_block[:, :, None]
        later_decay = jnp.concatenate([factor[1:], jnp.ones_like(factor[:1])], 0)
        back_decay, back_local = lax.associative_scan(
            combine, (jnp.flip(later_decay, 0), jnp.flip(feed_back, 0)), axis=0
        )
        adjoint = jnp.flip(back_local, 0) + jnp.flip(back_decay, 0) * carried[None]
        into_start = factor[0] * adjoint[0]
        inject = (step_block * value_block)[:, None, :] * in_block[:, :, None]
        decay_run, local_part = lax.associative_scan(combine, (factor, inject), axis=0)
        states = local_part + decay_run * start_state[None]
        before = jnp.concatenate([start_state[None], states[:-1]], 0)
        growth = adjoint * before * factor
        through = jnp.sum(adjoint * in_block[:, :, None], axis=1)
        grad_step = jnp.sum(growth * decay_rate[None], axis=1) + through * value_block
        grad_value = through * step_block + skip_gain[None] * grad_block
        grad_in = jnp.sum(adjoint * (step_block * value_block)[:, None, :], axis=2)
        grad_outc = jnp.sum(states * grad_block[:, None, :], axis=2)
        grad_decay = jnp.sum(growth * step_block[:, None, :], axis=0)
        grad_skip = jnp.sum(grad_block * value_block, axis=0)
        return (into_start, (grad_step, grad_value, grad_in, grad_outc, grad_decay, grad_skip))

    pieces = tuple(
        (
            tensor.reshape(block_count, block_size, tensor.shape[1])
            for tensor in (steps_dt, values, input_coef, output_coef, grad_out)
        )
    ) + (starts,)
    into_start, stacked = lax.scan(retreat, incoming, pieces, reverse=True)
    grad_step, grad_value, grad_in, grad_outc, grad_decay, grad_skip = stacked
    return (
        grad_step.reshape(row_count, chan_count),
        grad_value.reshape(row_count, chan_count),
        grad_in.reshape(row_count, grad_in.shape[2]),
        grad_outc.reshape(row_count, grad_outc.shape[2]),
        jnp.sum(grad_decay, 0),
        jnp.sum(grad_skip, 0),
    )


def local(
    hidden,
    modality,
    norm_gain,
    in_proj,
    conv_weight,
    conv_bias,
    x_proj_dt,
    x_proj_bc,
    dt_proj,
    dt_bias,
    a_log,
    skip_weight,
    out_proj,
    cotangent,
):
    tok_rows, width = hidden.shape
    mod_count = in_proj.shape[0]
    chan = in_proj.shape[3]
    tap_count = conv_weight.shape[0]
    state_count = a_log.shape[0]
    residual = hidden.astype(jnp.float32)
    inv_rms = lax.rsqrt(jnp.mean(residual * residual, axis=-1, keepdims=True) + EPS)
    gain_vec = norm_gain.astype(jnp.float32)
    normed = (residual * inv_rms * gain_vec).astype(jnp.bfloat16)
    rows_all, ids_all = (
        lax.all_gather(normed, "wide", axis=0, tiled=True),
        lax.all_gather(modality, "wide", axis=0, tiled=True),
    )
    seq_rows = rows_all.shape[0]
    w_in = in_proj.reshape(mod_count, width, 2 * chan)
    seq_order, seq_inverse = modal_order(ids_all)
    mixed_proj = grouped_apply(rows_all, ids_all, w_in, 0, seq_order, seq_inverse)
    conv_in = mixed_proj[:, :chan]
    gate_in = mixed_proj[:, chan:]
    conv_taps = conv_weight.astype(jnp.float32)
    padded = jnp.concatenate([jnp.zeros((tap_count - 1, chan), jnp.float32), conv_in], 0)
    pre_act = jnp.broadcast_to(conv_bias.astype(jnp.float32)[None], (seq_rows, chan))
    for offset in range(tap_count):
        pre_act = pre_act + conv_taps[offset][None] * padded[offset : offset + seq_rows]
    sig_pre = jax.nn.sigmoid(pre_act)
    conv_out = (pre_act * sig_pre).astype(jnp.bfloat16)
    decay_all = -jnp.exp(a_log)
    used_u = to_stretches(conv_out)
    low_rank = jnp.dot(used_u, x_proj_dt, preferred_element_type=jnp.float32).astype(jnp.bfloat16)
    coefs = jnp.dot(used_u, x_proj_bc, preferred_element_type=jnp.float32)
    values = used_u.astype(jnp.float32)
    pre_step = jnp.dot(low_rank, dt_proj, preferred_element_type=jnp.float32) + dt_bias[None]
    steps_dt = jax.nn.softplus(pre_step)
    running_steps = jnp.cumsum(steps_dt, 0)
    step_total = running_steps[-1]
    local_end = edge_state(
        step_total[None] - running_steps, coefs[:, :state_count], steps_dt * values, decay_all
    )
    total_decay = jnp.exp(decay_all * step_total[None])
    _, entry_state = entering(
        (total_decay, local_end),
        "wide",
        combine,
        (jnp.ones_like(total_decay), jnp.zeros_like(local_end)),
        False,
    )
    _, scanned, starts = forward_states(
        steps_dt,
        values,
        coefs[:, :state_count],
        coefs[:, state_count:],
        decay_all,
        skip_weight,
        entry_state,
    )
    gate_y = to_channels(scanned.astype(jnp.bfloat16))
    y_value = gate_y.astype(jnp.float32)
    sig_gate = jax.nn.sigmoid(gate_in)
    silu_gate = gate_in * sig_gate
    gated = (y_value * silu_gate).astype(jnp.bfloat16)
    rows_part = gated
    ids_part = ids_all
    part_order, part_inverse = modal_order(ids_part)
    projected = lax.psum_scatter(
        grouped_apply(rows_part, ids_part, out_proj, 0, part_order, part_inverse).astype(
            jnp.bfloat16
        ),
        "wide",
        scatter_dimension=0,
        tiled=True,
    ).astype(jnp.float32)
    output = (residual + projected).astype(jnp.bfloat16)
    cot_all = lax.all_gather(cotangent, "wide", axis=0, tiled=True)
    d_gated = grouped_apply(cot_all, ids_all, out_proj, 1, seq_order, seq_inverse)
    grad_wout = grouped_grad(gated, cot_all, ids_all, seq_order, mod_count)
    d_gate_y = (d_gated * silu_gate).astype(jnp.bfloat16)
    d_gate_in = d_gated * y_value * sig_gate * (1.0 + gate_in * (1.0 - sig_gate))
    grad_seq = to_stretches(d_gate_y).astype(jnp.float32)
    into_local = edge_state(running_steps, coefs[:, state_count:], grad_seq, decay_all)
    _, incoming = entering(
        (total_decay, into_local),
        "wide",
        combine,
        (jnp.ones_like(total_decay), jnp.zeros_like(into_local)),
        True,
    )
    grad_step, grad_value, grad_in, grad_outc, grad_decay, grad_skip = backward_states(
        steps_dt,
        values,
        coefs[:, :state_count],
        coefs[:, state_count:],
        decay_all,
        skip_weight,
        grad_seq,
        starts,
        incoming,
    )
    d_pre_step = (grad_step * jax.nn.sigmoid(pre_step)).astype(jnp.bfloat16)
    grad_bias = jnp.sum(d_pre_step.astype(jnp.float32), 0)
    grad_wdtp = contract(low_rank, d_pre_step, 0, 0)
    d_low = contract(d_pre_step, dt_proj, 1, 1).astype(jnp.bfloat16)
    d_coefs = jnp.concatenate([grad_in, grad_outc], 1).astype(jnp.bfloat16)
    d_value = grad_value + contract(d_low, x_proj_dt, 1, 1) + contract(d_coefs, x_proj_bc, 1, 1)
    grad_wxdt = contract(used_u, d_low, 0, 0)
    grad_wxbc = contract(used_u, d_coefs, 0, 0)
    grad_alog = grad_decay * decay_all
    d_conv_out = to_channels(d_value.astype(jnp.bfloat16))
    d_pre_act = d_conv_out.astype(jnp.float32) * sig_pre * (1.0 + pre_act * (1.0 - sig_pre))
    grad_taps = jnp.stack(
        [jnp.sum(d_pre_act * padded[offset : offset + seq_rows], 0) for offset in range(tap_count)],
        0,
    )
    grad_cbias = jnp.sum(d_pre_act, 0)
    d_padded = jnp.concatenate([d_pre_act, jnp.zeros((tap_count - 1, chan), jnp.float32)], 0)
    d_conv_in = jnp.zeros((seq_rows, chan), jnp.float32)
    for offset in range(tap_count):
        lead = tap_count - 1 - offset
        d_conv_in = d_conv_in + conv_taps[offset][None] * d_padded[lead : lead + seq_rows]
    d_mixed = jnp.concatenate([d_conv_in, d_gate_in], 1).astype(jnp.bfloat16)
    grad_win = grouped_grad(rows_all, d_mixed, ids_all, seq_order, mod_count).reshape(
        mod_count, width, 2, chan
    )
    rows_part = d_mixed
    ids_part = ids_all
    part_order, part_inverse = modal_order(ids_part)
    d_normed = lax.psum_scatter(
        grouped_apply(rows_part, ids_part, w_in, 1, part_order, part_inverse).astype(jnp.bfloat16),
        "wide",
        scatter_dimension=0,
        tiled=True,
    ).astype(jnp.float32)
    weighted = gain_vec * d_normed
    grad_hidden = (
        cotangent.astype(jnp.float32)
        + inv_rms * weighted
        - residual
        * inv_rms
        * inv_rms
        * inv_rms
        * jnp.mean(weighted * residual, axis=-1, keepdims=True)
    )
    gain_part = jnp.sum(d_normed * residual * inv_rms, 0)
    gain_share, grad_wxdt, grad_wxbc, grad_wdtp, grad_bias, grad_alog, grad_skip = (
        lax.psum_scatter(
            gain_part.astype(jnp.bfloat16), "wide", scatter_dimension=0, tiled=True
        ).astype(jnp.float32),
        lax.psum_scatter(
            grad_wxdt.astype(jnp.bfloat16), "wide", scatter_dimension=0, tiled=True
        ).astype(jnp.float32),
        lax.psum_scatter(
            grad_wxbc.astype(jnp.bfloat16), "wide", scatter_dimension=0, tiled=True
        ).astype(jnp.float32),
        lax.psum_scatter(
            grad_wdtp.astype(jnp.bfloat16), "wide", scatter_dimension=1, tiled=True
        ).astype(jnp.float32),
        lax.psum_scatter(
            grad_bias.astype(jnp.bfloat16), "wide", scatter_dimension=0, tiled=True
        ).astype(jnp.float32),
        lax.psum_scatter(
            grad_alog.astype(jnp.bfloat16), "wide", scatter_dimension=1, tiled=True
        ).astype(jnp.float32),
        lax.psum_scatter(
            grad_skip.astype(jnp.bfloat16), "wide", scatter_dimension=0, tiled=True
        ).astype(jnp.float32),
    )
    summed = (
        lax.psum(gain_share.astype(jnp.bfloat16), "row").astype(jnp.float32),
        lax.psum(grad_win.astype(jnp.bfloat16), "row").astype(jnp.float32),
        lax.psum(grad_taps.astype(jnp.bfloat16), "row").astype(jnp.float32),
        lax.psum(grad_cbias.astype(jnp.bfloat16), "row").astype(jnp.float32),
        lax.psum(grad_wxdt.astype(jnp.bfloat16), "row").astype(jnp.float32),
        lax.psum(grad_wxbc.astype(jnp.bfloat16), "row").astype(jnp.float32),
        lax.psum(grad_wdtp.astype(jnp.bfloat16), "row").astype(jnp.float32),
        lax.psum(grad_bias.astype(jnp.bfloat16), "row").astype(jnp.float32),
        lax.psum(grad_alog.astype(jnp.bfloat16), "row").astype(jnp.float32),
        lax.psum(grad_skip.astype(jnp.bfloat16), "row").astype(jnp.float32),
        lax.psum(grad_wout.astype(jnp.bfloat16), "row").astype(jnp.float32),
    )
    return (
        output,
        grad_hidden,
        summed[0],
        summed[1],
        summed[2],
        summed[3],
        summed[4],
        summed[5],
        summed[6],
        summed[7],
        summed[8],
        summed[9],
        summed[10],
    )


def solution(mesh):
    return jax.shard_map(
        local,
        mesh=mesh,
        in_specs=(
            P(("row", "wide"), None),
            P(("row", "wide")),
            P(),
            P(None, None, None, "wide"),
            P(None, "wide"),
            P("wide"),
            P(),
            P(),
            P(),
            P(),
            P(),
            P(),
            P(None, "wide", None),
            P(("row", "wide"), None),
        ),
        out_specs=(
            P(("row", "wide"), None),
            P(("row", "wide"), None),
            P("wide"),
            P(None, None, None, "wide"),
            P(None, "wide"),
            P("wide"),
            P("wide", None),
            P("wide", None),
            P(None, "wide"),
            P("wide"),
            P(None, "wide"),
            P("wide"),
            P(None, "wide", None),
        ),
        check_vma=False,
    )
```

profile of v0, /device:TPU:0, one launch (start us, length us, event | category | flops | bytes accessed | tf_op | source)
XLA Modules:
  0.0 4393.9 jit_solution(13677134818179201257)
XLA Ops:
  36.2 21.1 reshape.627
  68.9 50.7 %while.160 = (s32[]{:T(128)}, f32[2,512,1024]{2,1,0:T(8,128)}, s32[2,512]{1,0:T(2,128)S(1)}, bf16[2,512,2048]{2,1,0:T(8,128)(2,1)}, bf16[3,2048,1024]{2,1,0:T(8,...) while((s32[]{:T(128)}, f32[2,512,1024]{2,1,0:T(8,128)}, ...), condition=%wide.region_9.10_spmd, body=%wide.region_2.9_spmd.sunk | while | flops 6445073920 | bytes 37762384 | solution.py:94
  138.3 15.1 all-to-all-done
  169.5 24.3 while.170
  220.2 898.0 %while.162 = (s32[]{:T(128)}, f32[16,4096]{1,0:T(8,128)}, bf16[4,32,4096]{2,1,0:T(8,128)(2,1)}, f32[4,16,4096]{2,1,0:T(8,128)}, f32[4,32,4096]{2,1,0:T(8,128)}, ...) while((s32[]{:T(128)}, f32[16,4096]{1,0:T(8,128)}, ...), condition=%wide.region_19.20_spmd, body=%wide.region_17.19_spmd.sunk | while | flops 39518208 | bytes 399020448 | solution.py:193
  427.5 14.6 multiply_reduce_fusion.17
  651.9 14.6 multiply_reduce_fusion.17
  876.3 14.6 multiply_reduce_fusion.17
  1100.6 14.6 multiply_reduce_fusion.17
  1121.3 15.1 all-to-all-start.1
  1136.4 40.2 while.164
  1191.6 15.4 all-to-all-done.2
  1211.5 24.3 while.171
  1237.4 22.7 all-gather.18.cloned.1.call-done
  1279.3 1988.9 %while.166 = (s32[]{:T(128)}, f32[16,4096]{1,0:T(8,128)}, f32[4,32,4096]{2,1,0:T(8,128)}, f32[4,32,4096]{2,1,0:T(8,128)}, bf16[4,32,16]{2,1,0:T(8,128)(2,1)}, /*...) while((s32[]{:T(128)}, f32[16,4096]{1,0:T(8,128)}, ...), condition=%wide.region_49.50_spmd, body=%wide.region_42.49_spmd.sunk | while | flops 97119232 | bytes 1076095872 | solution.py:235
  1512.6 18.9 multiply_reduce_fusion.18
  1768.5 15.4 multiply_reduce_fusion.19
  2003.6 18.9 multiply_reduce_fusion.18
  2259.5 15.4 multiply_reduce_fusion.19
  2494.7 18.9 multiply_reduce_fusion.18
  2750.6 15.4 multiply_reduce_fusion.19
  2985.7 18.9 multiply_reduce_fusion.18
  3241.6 15.4 multiply_reduce_fusion.19
  3313.0 58.3 %while.167 = (s32[]{:T(128)}, bf16[2,512,2048]{2,1,0:T(8,128)(2,1)}, s32[2,512]{1,0:T(2,128)S(1)}, bf16[2,512,1024]{2,1,0:T(8,128)(2,1)S(1)}, bf16[3,2048,1024]{...) while((s32[]{:T(128)}, bf16[2,512,2048]{2,1,0:T(8,128)(2,1)}, ...), condition=%wide.region_57.58_spmd, body=%wide.region_50.57_spmd.sunk | while | flops 6447695360 | bytes 47199568 | solution.py:94
  3389.6 77.2 %while.169 = (s32[]{:T(128)}, f32[3,512,2048]{2,1,0:T(8,128)}, s32[2,512]{1,0:T(2,128)S(1)}, bf16[2,512,512]{2,1,0:T(8,128)(2,1)S(1)}, bf16[2,512,2048]{2,1,0:T(...) while((s32[]{:T(128)}, f32[3,512,2048]{2,1,0:T(8,128)}, ...), condition=%wide.region_101.102_spmd, body=%wide.region_94.101_spmd.sunk | while | flops 3225159168 | bytes 67646840 | solution.py:137
  3473.7 48.8 %while.163 = (s32[]{:T(128)}, bf16[2,512,2048]{2,1,0:T(8,128)(2,1)}, s32[2,512]{1,0:T(2,128)S(1)}, bf16[2,512,512]{2,1,0:T(8,128)(2,1)S(1)}, bf16[3,512,2048]{2,...) while((s32[]{:T(128)}, bf16[2,512,2048]{2,1,0:T(8,128)(2,1)}, ...), condition=%wide.region_27.28_spmd, body=%wide.region_20.27_spmd.sunk | while | flops 3226469888 | bytes 38286672 | solution.py:94
  3556.0 131.4 %while.168 = (s32[]{:T(128)}, f32[3,2048,1024]{2,1,0:T(8,128)}, s32[2,512]{1,0:T(2,128)S(1)}, bf16[2,512,2048]{2,1,0:T(8,128)(2,1)}, bf16[2,512,1024]{2,1,0:T(8,...) while((s32[]{:T(128)}, f32[3,2048,1024]{2,1,0:T(8,128)}, ...), condition=%wide.region_70.71_spmd, body=%wide.region_63.70_spmd.sunk | while | flops 6451889664 | bytes 116405584 | solution.py:137
  3700.7 21.1 convert_element_type.394
  3726.0 23.6 all-reduce.67
  3749.8 28.7 all-reduce.68
  3785.6 578.7 %all-reduce.72.cloned.1.call-done = (bf16[3,2048,2,512]{3,2,1,0:T(2,128)(2,1)}, bf16[512,128]{1,0:T(8,128)(2,1)}, bf16[128,512]{1,0:T(8,128)(2,1)}, bf16[3,512,2048]{2,1,0:T(8,128)(2,1)}) async-done(((bf16[3,2048,2,512]{3,2,1,0:T(2,128)(2,1)}, bf16[512,128]{1,0:T(8,128)(2,1)}, bf16[128,512]{1,0:T(8,128)(2,1)}, bf16[3,512,2048]{2,1,0:T(8,128)(2,1)}), (bf16[3,2048,2,512]{3,2,1,0:T(2,128)(2,1)}, ...) | async-done | bytes 19136528 | tf_op jit(solution)/shard_map/psum | solution.py:430
  4364.3 14.8 convert_element_type.395
  (1552 shorter events, 3530.6 us)
Async XLA Ops:
  7.2 148.6 %copy-start = (bf16[128,4096]{1,0:T(8,128)(2,1)S(1)}, bf16[128,4096]{1,0:T(8,128)(2,1)}, u32[]{:S(2)}) copy-start(bf16[128,4096]{1,0:T(8,128)(2,1)} %param.94) | copy-start | bytes 3145732
  7.2 50.2 %all-gather.10.cloned.1.call-start = ((), (), s32[]{:S(2)}) async-start(), calls=%async_computation.10 | async-start | bytes 4718592 | tf_op jit(solution)/shard_map/all_gather | solution.py:273
  11.8 184.7 %all-gather.12.cloned.1.call-start = ((), (), s32[]{:S(2)}) async-start(), calls=%async_computation.12 | async-start | bytes 4718592 | tf_op jit(solution)/shard_map/all_gather | solution.py:335
  27.3 169.2 %copy-start.66 = (s32[1024]{0:T(1024)}, s32[1024]{0:T(1024)S(1)}, u32[]{:S(2)}) copy-start(s32[1024]{0:T(1024)S(1)} %fusion.142) | copy-start | bytes 12292
  57.3 62.3 %copy-start.74 = (s32[1024]{0:T(1024)}, s32[1024]{0:T(1024)S(1)}, u32[]{:S(2)}) copy-start(s32[1024]{0:T(1024)S(1)} %fusion.143) | copy-start | bytes 12292
  57.3 72.7 %copy-start.83 = (f32[1,512]{1,0:T(1,128)}, f32[1,512]{1,0:T(1,128)S(1)}, u32[]{:S(2)}) copy-start(f32[1,512]{1,0:T(1,128)S(1)} %get-tuple-element.1737) | copy-start | bytes 6148
  57.3 72.7 %copy-start.85 = (f32[1,512]{1,0:T(1,128)}, f32[1,512]{1,0:T(1,128)S(1)}, u32[]{:S(2)}) copy-start(f32[1,512]{1,0:T(1,128)S(1)} %get-tuple-element.1738) | copy-start | bytes 6148
  57.3 72.7 %copy-start.87 = (f32[1,512]{1,0:T(1,128)}, f32[1,512]{1,0:T(1,128)S(1)}, u32[]{:S(2)}) copy-start(f32[1,512]{1,0:T(1,128)S(1)} %get-tuple-element.1739) | copy-start | bytes 6148
  57.4 72.7 %copy-start.89 = (f32[1,512]{1,0:T(1,128)}, f32[1,512]{1,0:T(1,128)S(1)}, u32[]{:S(2)}) copy-start(f32[1,512]{1,0:T(1,128)S(1)} %get-tuple-element.1740) | copy-start | bytes 6148
  134.4 19.0 all-to-all-start
  138.1 73.9 %all-gather.14.cloned.1.call-start = ((), (), s32[]{:S(2)}) async-start(), calls=%async_computation.18 | async-start | bytes 1179648 | tf_op jit(solution)/shard_map/all_gather | solution.py:15
  169.4 49.0 %all-gather.16.cloned.1.call-start = ((), (), s32[]{:S(2)}) async-start(), calls=%async_computation.19 | async-start | bytes 1179648 | tf_op jit(solution)/shard_map/all_gather | solution.py:15
  1121.3 60.2 %all-to-all-start.1 = ((bf16[128,8,512]{2,0,1:T(8,128)(2,1)}), bf16[128,8,512]{2,0,1:T(8,128)(2,1)}, u32[]{:S(2)}, u32[]{:S(2)}) async-start(bf16[128,8,512]{2,0,1:T(8,128)(2,1)} %copy.103), calls=%async_computation.1 | async-start | bytes 2097152 | tf_op jit(solution)/shard_map/all_to_all | solution.py:146
  1136.4 40.2 copy-start.75
  1187.3 19.6 all-to-all-start.2
  1191.5 68.7 %all-gather.18.cloned.1.call-start = ((), (), s32[]{:S(2)}) async-start(), calls=%async_computation.20 | async-start | bytes 1179648 | tf_op jit(solution)/shard_map/all_gather | solution.py:15
  1237.4 2484.4 %reduce-scatter.11.cloned.1.call-start = ((), (), s32[]{:S(2)}) async-start(), calls=%async_computation.14 | async-start | bytes 1179648 | tf_op jit(solution)/shard_map/reduce_scatter | solution.py:409
  2248.1 26.8 slice-start.2
  3278.6 20.8 all-to-all-start.3
  3282.9 439.0 %reduce-scatter.15.cloned.1.call-start = ((), (), s32[]{:S(2)}) async-start(), calls=%async_computation.16 | async-start | bytes 1179648 | tf_op jit(solution)/shard_map/reduce_scatter | solution.py:415
  3290.9 433.7 %reduce-scatter.9.cloned.1.call-start = ((), (), s32[]{:S(2)}) async-start(), calls=%async_computation.13 | async-start | bytes 4718592 | tf_op jit(solution)/shard_map/reduce_scatter | solution.py:388
  3313.0 58.3 %copy-start.76 = (s32[1024]{0:T(1024)S(1)}, s32[1024]{0:T(1024)}, u32[]{:S(2)}) copy-start(s32[1024]{0:T(1024)} %copy-done.74) | copy-start | bytes 12292
  3383.2 366.7 %reduce-scatter.17.cloned.1.call-start = ((), (), s32[]{:S(2)}) async-start(), calls=%async_computation.17 | async-start | bytes 147456 | tf_op jit(solution)/shard_map/reduce_scatter | solution.py:421
  3389.6 78.5 %copy-start.60 = (f32[16,4096]{1,0:T(8,128)S(1)}, f32[16,4096]{1,0:T(8,128)}, u32[]{:S(2)}) copy-start(f32[16,4096]{1,0:T(8,128)} %param.96) | copy-start | bytes 786436
  3389.6 79.3 %copy-start.79 = (bf16[128,16]{0,1:T(8,128)(2,1)S(1)}, bf16[128,16]{0,1:T(8,128)(2,1)}, u32[]{:S(2)}) copy-start(bf16[128,16]{0,1:T(8,128)(2,1)} %copy-done.78) | copy-start | bytes 12292
  3389.6 79.3 %copy-start.81 = (bf16[128,16]{0,1:T(8,128)(2,1)S(1)}, bf16[128,16]{0,1:T(8,128)(2,1)}, u32[]{:S(2)}) copy-start(bf16[128,16]{0,1:T(8,128)(2,1)} %copy-done.80) | copy-start | bytes 12292
  3468.8 281.0 %reduce-scatter.13.cloned.1.call-start = ((), (), s32[]{:S(2)}) async-start(), calls=%async_computation.15 | async-start | bytes 294912 | tf_op jit(solution)/shard_map/reduce_scatter | solution.py:412
  3471.1 311.6 %reduce-scatter.7.cloned.1.call-start = ((), (), s32[]{:S(2)}) async-start(), calls=%async_computation.11 | async-start | bytes 4718592 | tf_op jit(solution)/shard_map/reduce_scatter | solution.py:326
  3473.7 48.8 %copy-start.77 = (s32[1024]{0:T(1024)S(1)}, s32[1024]{0:T(1024)}, u32[]{:S(2)}) copy-start(s32[1024]{0:T(1024)} %copy-done.74) | copy-start | bytes 12292
  3542.3 822.0 %all-reduce.72.cloned.1.call-start = ((), (), s32[]{:S(2)}) async-start(), calls=%async_computation.21 | async-start | bytes 38273024 | tf_op jit(solution)/shard_map/psum | solution.py:430
  3721.9 27.9 copy-start.95
  3721.9 60.8 %copy-start.55 = (bf16[128,2048]{1,0:T(8,128)(2,1)S(1)}, bf16[128,2048]{1,0:T(8,128)(2,1)}, u32[]{:S(2)}) copy-start(bf16[128,2048]{1,0:T(8,128)(2,1)} %param.99) | copy-start | bytes 1572868
  (240 other events, 1748.9 us)
Sparse Core Ops, SparseCore 0:
  11.9 39.8 all-gather.9
  53.7 36.7 all-gather.11
  169.5 22.8 all-gather.13
  195.5 22.8 all-gather.15
  1237.5 22.6 all-gather.17
  3275.1 35.8 reduce-scatter.10
  3314.2 35.9 reduce-scatter.14
  3383.3 50.6 reduce-scatter.8
  3469.0 32.6 reduce-scatter.16
  3505.1 33.5 reduce-scatter.12
  3542.5 51.3 reduce-scatter.6
  3722.1 642.1 all-reduce.71
where the time goes:
time: 4430 us; the launch traced here: 4390 us
  local copies, waits for them, and re-layouts  1790 us (40%)
  other arithmetic  1610 us (36%)
  waiting for transfers between devices  648 us (15%)
  matrix products  156 us (4%)
  loops' own time  75.7 us (2%)
  blocking collectives  62.6 us (1%)
    psum x1, waiting for transfers between devices, local(): lax.psum(grad_win.astype(jnp.bfloat16), 'row').astype(jnp.float32)  579 us
    pad x64, local copies, waits for them, and re-layouts, retreat(): lax.associative_scan(combine, (factor, inject), axis=0)  437 us
    add x103, other arithmetic, combine(): return (decay_one * decay_two, decay_two * state_one + state_two)  435 us
    pad x64, local copies, waits for them, and re-layouts, advance(): lax.associative_scan(combine, (factor, inject), axis=0)  435 us
    pad x64, local copies, waits for them, and re-layouts, retreat(): lax.associative_scan(combine, (jnp.flip(later_decay, 0), jnp.flip(feed_ba...  413 us
    add x40, other arithmetic, retreat(): lax.associative_scan(combine, (jnp.flip(later_decay, 0), jnp.flip(feed_ba...  185 us
    dot_general x30, matrix products, contract(): lax.dot_general(left, right, (((left_dim,), (right_dim,)), ((), ())), pre...  149 us
    scatter-add x12, other arithmetic, accumulate(): acc.at[modal_id]  113 us
  transfers between devices with their start and end apart: 16, of which 6 were waited for; matrix products, arithmetic and copies ran while one was open for 14% of the time, Pallas kernels for 0%

commit v1 on v0

v1 whole, which is shorter than its diff:
```python
import functools

import jax
import jax.numpy as jnp
from jax import lax
from jax.experimental import pallas as pl
from jax.experimental.pallas import tpu as pltpu
from jax.sharding import PartitionSpec as P
LOG2E = 1.4426950408889634
EPS = 1e-05
SPAN = 256
TILE = 16
FU, BU = 4, 2

def softplus(v):
    return jnp.maximum(v, 0.0) + jnp.log1p(jnp.exp(-jnp.abs(v)))

def spread(columns, n):
    wide = TILE * n
    pick = lax.broadcasted_iota(jnp.int32, (n, wide), 1) % n == lax.broadcasted_iota(jnp.int32, (n, wide), 0)
    tiled = jnp.dot(columns.astype(jnp.bfloat16), pick.astype(jnp.bfloat16), preferred_element_type=jnp.float32)
    return jnp.where(diagonal(columns.shape[0], n), tiled, 0.0).astype(jnp.bfloat16)

def diagonal(rows, n):
    wide = TILE * n
    return lax.broadcasted_iota(jnp.int32, (rows, wide), 1) // n == lax.broadcasted_iota(jnp.int32, (rows, wide), 0) % TILE

def mm(a, b):
    return jnp.dot(a, b, preferred_element_type=jnp.float32)

def mt(a, b):
    return lax.dot_general(a, b, (((1,), (1,)), ((), ())), preferred_element_type=jnp.float32)

WINDOW = 512
PEAK = 1.1e15


def taking(microseconds, moved=0):
    return pl.CostEstimate(flops=int(microseconds * 1e-6 * PEAK), bytes_accessed=int(moved), transcendentals=0)


def first_window(bounds, row, m, span, window):
    first, last = bounds[row, m], bounds[row, m + 1]
    base = lax.div(first, 128) * 128
    count = jnp.where(last > first, lax.div(last - base + window - 1, window), 0)
    return first, last, base, count


def inside(at, low, high, window):
    here = at + lax.broadcasted_iota(jnp.int32, (window, 128), 0)
    return jnp.where((here >= low) & (here < high), 1.0, 0.0).astype(jnp.bfloat16)


def grouped_sum(bounds, slots, m, span, window, left_at, right_at, acc, start):
    lefts, rights, more = [], [], []
    for s in range(slots):
        first, last, base, count = first_window(bounds, s, m, span, window)
        at = pl.multiple_of(jnp.minimum(base, span - window), 128)
        keep = inside(at, first, last, window)
        lefts.append(left_at(s, at, keep))
        rights.append(right_at(s, at, keep))
        more.append((last, base, count))
    total = mm(jnp.concatenate(lefts, 1), jnp.concatenate(rights, 0))
    acc[...] = total if start is None else total + start[0]
    for s, (last, base, count) in enumerate(more):

        def one(i, _):
            want = base + i * window
            at = pl.multiple_of(jnp.minimum(want, span - window), 128)
            keep = inside(at, want, last, window)
            acc[...] += mm(left_at(s, at, keep), right_at(s, at, keep))
            return 0

        lax.fori_loop(1, count, one, 0)


def grad_in_kernel(bounds, *refs, slots, begun, halves):
    rows, d, rest = refs[:slots], refs[slots : 2 * slots], refs[2 * slots : -2]
    out, acc = refs[-2:]
    wide, _, unit, bf = rows[0].shape
    span, chan = d[0].shape
    window = min(WINDOW, span)

    def left_at(s, at, keep):
        block = rows[s][pl.ds(lax.div(at, unit), window // unit), 0]
        return jnp.transpose(block.reshape(window, bf))

    def right_at(s, at, keep):
        return d[s][pl.ds(at, window), :] * jnp.concatenate([keep] * (chan // 128), 1)

    grouped_sum(bounds, slots, pl.program_id(1), span, window, left_at, right_at, acc, rest[0] if begun else None)
    if halves:
        other = rest[-1]
        lanes = chan // 128
        for j in range(lanes):
            out[0, pl.ds(j * 2, bf, stride=2 * lanes), :] = acc[:, j * 128 : (j + 1) * 128]
            out[0, pl.ds(j * 2 + 1, bf, stride=2 * lanes), :] = other[0, :, j * 128 : (j + 1) * 128]
    else:
        out[0] = acc[...]


def slot_spec(array, index, bf):
    return pl.BlockSpec((array.shape[0], 1, array.shape[2], bf), lambda f, m, b: (0, index, 0, f))


def side_spec(array, chan, side):
    return pl.BlockSpec((array.shape[0], chan), lambda f, m, b: (0, side))


def feature_block(rows):
    wide, _, unit, width = rows[0][0].shape
    return max(128, min(1024, (1 << 20) // (wide * unit)))


def grad_in(bounds, rows, d, mods, chan, side, start=None, other=None):
    width = rows[0][0].shape[3]
    bf = feature_block(rows)
    span, slots = d[0].shape[0], len(d)
    plain = pl.BlockSpec((1, bf, chan), lambda f, m, b: (m, f, 0))
    ins = [slot_spec(array, index, bf) for array, index in rows] + [side_spec(x, chan, side) for x in d]
    args = [array for array, _ in rows] + list(d)
    for extra in (start, other):
        if extra is not None:
            ins.append(plain)
            args.append(extra)
    if other is not None:
        out_shape = jax.ShapeDtypeStruct((mods, width * 2 * chan // 128, 128), jnp.float32)
        out_spec = pl.BlockSpec((1, bf * 2 * chan // 128, 128), lambda f, m, b: (m, f, 0))
    else:
        out_shape = jax.ShapeDtypeStruct((mods, width, chan), jnp.float32)
        out_spec = plain
    return pl.pallas_call(
        functools.partial(grad_in_kernel, slots=slots, begun=start is not None, halves=other is not None),
        grid_spec=pltpu.PrefetchScalarGridSpec(
            num_scalar_prefetch=1,
            grid=(width // bf, mods),
            in_specs=ins,
            out_specs=out_spec,
            scratch_shapes=[pltpu.VMEM((bf, chan), jnp.float32)],
        ),
        out_shape=out_shape,
        compiler_params=pltpu.CompilerParams(vmem_limit_bytes=56 << 20),
        cost_estimate=taking(6 * slots + 6),
    )(bounds, *args)


def grad_out_kernel(bounds, *refs, slots):
    cot, gated, out = refs[:slots], refs[slots : 2 * slots], refs[-1]
    wide, _, unit, bf = cot[0].shape
    span, chan = gated[0].shape
    window = min(WINDOW, span)

    def left_at(s, at, keep):
        return jnp.transpose(gated[s][pl.ds(at, window), :] * jnp.concatenate([keep] * (chan // 128), 1))

    def right_at(s, at, keep):
        return cot[s][pl.ds(lax.div(at, unit), window // unit), 0].reshape(window, bf)

    grouped_sum(bounds, slots, pl.program_id(1), span, window, left_at, right_at, out.at[0], None)


def grad_out(bounds, cot, gated, mods, chan, side):
    width = cot[0][0].shape[3]
    bf = feature_block(cot)
    slots = len(gated)
    return pl.pallas_call(
        functools.partial(grad_out_kernel, slots=slots),
        grid_spec=pltpu.PrefetchScalarGridSpec(
            num_scalar_prefetch=1,
            grid=(width // bf, mods),
            in_specs=[slot_spec(array, index, bf) for array, index in cot] + [side_spec(x, chan, side) for x in gated],
            out_specs=pl.BlockSpec((1, chan, bf), lambda f, m, b: (m, 0, f)),
        ),
        out_shape=jax.ShapeDtypeStruct((mods, chan, width), jnp.float32),
        compiler_params=pltpu.CompilerParams(vmem_limit_bytes=56 << 20),
        cost_estimate=taking(6 * slots + 4),
    )(bounds, *[array for array, _ in cot], *gated)


def fwd_kernel(lr, dtw, dtb, cf, ct, u, alog, skip, gate, dgated, gated, dy, dgate, starts, h_s, dt_s, du_s, y_s, bd_s, hb_s):
    span, chan = u.shape
    n = alog.shape[0]
    @pl.when(pl.program_id(0) == 0)
    def _():
        h_s[...] = jnp.zeros_like(h_s)
    rate = -jnp.exp(alog[...]) * LOG2E
    dt = softplus(mm(lr[...], dtw[...]) + dtb[...])
    uf = u[...].astype(jnp.float32)
    dt_s[...] = dt
    du_s[...] = dt * uf
    starts[0] = h_s[...]
    bd_s[...] = spread(cf[:, n:], n)
    block = FU * TILE
    def reduce(g):
        for k in range(FU):
            t0 = pl.multiple_of(g * block + k * TILE, TILE)
            y_s[pl.ds(t0, TILE), :] = mm(bd_s[pl.ds(t0, TILE), :], hb_s[pl.ds(pl.multiple_of(t0 * n, TILE * n), TILE * n), :])
    def group(g, h):
        c = pltpu.roll(ct[:n, :], span - g * block, 1)
        reduce(jnp.maximum(g - 1, 0))
        for j in range(block):
            t = g * block + j
            e = jnp.exp2(dt_s[pl.ds(t, 1), :] * rate)
            h = e * h + du_s[pl.ds(t, 1), :] * c[:, j:j+1]
            hb_s[pl.ds(pl.multiple_of(t * n, n), n), :] = h.astype(jnp.bfloat16)
        return h
    h_s[...] = lax.fori_loop(0, span // block, group, h_s[...])
    reduce(span // block - 1)
    y = (y_s[...] + skip[...] * uf).astype(jnp.bfloat16).astype(jnp.float32)
    g = gate[...]
    sig = jax.nn.sigmoid(g)
    silu = g * sig
    dg = dgated[...]
    gated[...] = (y * silu).astype(jnp.bfloat16)
    dy[...] = (dg * silu).astype(jnp.bfloat16)
    dgate[...] = (dg * y * sig * (1.0 + g * (1.0 - sig))).astype(jnp.bfloat16)

def scan_forward(lr, dtw, dtb, cf, ct, u, alog, skip, gate, dgated, span=SPAN):
    rows, chan = u.shape
    n = alog.shape[0]
    rank = lr.shape[1]
    steps = rows // span
    full = lambda a: pl.BlockSpec(a.shape, lambda i: (0,) * a.ndim)
    tok = lambda w: pl.BlockSpec((span, w), lambda i: (i, 0))
    return pl.pallas_call(
        fwd_kernel, grid=(steps,),
        in_specs=[tok(rank), full(dtw), full(dtb), tok(2*n), pl.BlockSpec((2*n, span), lambda i: (0, i)), tok(chan), full(alog), full(skip), tok(chan), tok(chan)],
        out_specs=[tok(chan)] * 3 + [pl.BlockSpec((1, n, chan), lambda i: (i, 0, 0))],
        out_shape=[jax.ShapeDtypeStruct((rows, chan), jnp.bfloat16)] * 3 + [jax.ShapeDtypeStruct((steps, n, chan), jnp.float32)],
        scratch_shapes=[pltpu.VMEM((n, chan), jnp.float32)] + [pltpu.VMEM((span, chan), jnp.float32)] * 3 + [pltpu.VMEM((span, TILE * n), jnp.bfloat16), pltpu.VMEM((span * n, chan), jnp.bfloat16)],
        compiler_params=pltpu.CompilerParams(vmem_limit_bytes=32 << 20),
        cost_estimate=taking(13 * rows / 1024),
    )(lr, dtw, dtb, cf, ct, u, alog, skip, gate, dgated)

def bwd_kernel(lr, dtw, dtb, cf, ct, u, alog, skip, dy, starts, dpre, dval, dlow, din, dout, galog, gskip, gbias, gdtw, lam_s, dt_s, du_s, dyf_s, hp_s, st_s, th_s, bd_s, hb_s, gb_s):
    span, chan = u.shape
    n = alog.shape[0]
    @pl.when(pl.program_id(0) == 0)
    def _():
        lam_s[...] = jnp.zeros_like(lam_s)
        galog[...] = jnp.zeros_like(galog)
        gskip[...] = jnp.zeros_like(gskip)
        gbias[...] = jnp.zeros_like(gbias)
        gdtw[...] = jnp.zeros_like(gdtw)
    decay = -jnp.exp(alog[...])
    rate = decay * LOG2E
    pre = mm(lr[...], dtw[...]) + dtb[...]
    dt = softplus(pre)
    uf = u[...].astype(jnp.float32)
    dyf = dy[...].astype(jnp.float32)
    dt_s[...] = dt
    du_s[...] = dt * uf
    dyf_s[...] = dyf
    bd_s[...] = spread(cf[:, :n], n)
    mask = diagonal(TILE, n)
    ones = mask.astype(jnp.bfloat16)
    block = FU * TILE
    def reduce_h(g):
        for k in range(FU):
            t0 = pl.multiple_of(g * block + k * TILE, TILE)
            cross = mt(dy[pl.ds(t0, TILE), :], hb_s[pl.ds(pl.multiple_of(t0 * n, TILE * n), TILE * n), :])
            dout[0, pl.ds(g * FU + k, 1), :] = jnp.sum(jnp.where(mask, cross, 0.0), axis=0, keepdims=True)
    def again(g, h):
        c = pltpu.roll(ct[:n, :], span - g * block, 1)
        reduce_h(jnp.maximum(g - 1, 0))
        for j in range(block):
            t = g * block + j
            hp_s[t] = h
            e = jnp.exp2(dt_s[pl.ds(t, 1), :] * rate)
            h = e * h + du_s[pl.ds(t, 1), :] * c[:, j:j+1]
            hb_s[pl.ds(pl.multiple_of(t * n, n), n), :] = h.astype(jnp.bfloat16)
        return h
    lax.fori_loop(0, span // block, again, starts[0])
    reduce_h(span // block - 1)
    back = BU * TILE
    per = span // back
    def reduce_lam(g):
        for k in range(BU - 1, -1, -1):
            t0 = pl.multiple_of(g * back + k * TILE, TILE)
            wide = pl.ds(pl.multiple_of(t0 * n, TILE * n), TILE * n)
            lam16 = hb_s[wide, :]
            st_s[pl.ds(t0, TILE), :] = mm(ones, gb_s[wide, :])
            th_s[pl.ds(t0, TILE), :] = mm(bd_s[pl.ds(t0, TILE), :], lam16)
            cross = mt(du_s[pl.ds(t0, TILE), :].astype(jnp.bfloat16), lam16)
            din[0, pl.ds(g * BU + k, 1), :] = jnp.sum(jnp.where(mask, cross, 0.0), axis=0, keepdims=True)
    def group(q, state):
        carry, gdec = state
        g = per - 1 - q
        c = pltpu.roll(ct[n:, :], span - g * back, 1)
        reduce_lam(jnp.minimum(g + 1, per - 1))
        for j in range(back - 1, -1, -1):
            t = g * back + j
            here = pl.ds(pl.multiple_of(t * n, n), n)
            d = dt_s[pl.ds(t, 1), :]
            lam = carry + dyf_s[pl.ds(t, 1), :] * c[:, j:j+1]
            carry = lam * jnp.exp2(d * rate)
            grow = carry * hp_s[t]
            gdec = gdec + grow * d
            hb_s[here, :] = lam.astype(jnp.bfloat16)
            gb_s[here, :] = (grow * decay).astype(jnp.bfloat16)
        return carry, gdec
    carry, gdec = lax.fori_loop(0, per, group, (lam_s[...], jnp.zeros_like(decay)))
    reduce_lam(0)
    lam_s[...] = carry
    galog[...] += gdec * decay
    gskip[...] += jnp.sum(dyf * uf, axis=0, keepdims=True)
    thru = th_s[...]
    dp = ((st_s[...] + thru * uf) * jax.nn.sigmoid(pre)).astype(jnp.bfloat16)
    dpre[...] = dp
    dval[...] = thru * dt + skip[...] * dyf
    gbias[...] += jnp.sum(dp.astype(jnp.float32), axis=0, keepdims=True)
    dlow[...] = mt(dp, dtw[...])
    gdtw[...] += lax.dot_general(lr[...], dp, (((0,), (0,)), ((), ())), preferred_element_type=jnp.float32)

def scan_backward(lr, dtw, dtb, cf, ct, u, alog, skip, dy, starts, span=SPAN):
    rows, chan = u.shape
    n = alog.shape[0]
    rank = lr.shape[1]
    steps = rows // span
    full = lambda a: pl.BlockSpec(a.shape, lambda i: (0,) * a.ndim)
    tok = lambda w: pl.BlockSpec((span, w), lambda i: (steps - 1 - i, 0))
    ctok = pl.BlockSpec((2*n, span), lambda i: (0, steps - 1 - i))
    ptok = pl.BlockSpec((1, span // TILE, TILE * n), lambda i: (steps - 1 - i, 0, 0))
    f = lambda *s: jax.ShapeDtypeStruct(s, jnp.float32)
    outs = [jax.ShapeDtypeStruct((rows, chan), jnp.bfloat16), f(rows, chan), f(rows, rank), f(steps, span // TILE, TILE * n), f(steps, span // TILE, TILE * n), f(n, chan), f(1, chan), f(1, chan), f(rank, chan)]
    return pl.pallas_call(
        bwd_kernel, grid=(steps,),
        in_specs=[tok(rank), full(dtw), full(dtb), tok(2*n), ctok, tok(chan), full(alog), full(skip), tok(chan), pl.BlockSpec((1, n, chan), lambda i: (steps - 1 - i, 0, 0))],
        out_specs=[tok(chan), tok(chan), tok(rank), ptok, ptok] + [full(o) for o in outs[5:]],
        out_shape=outs,
        scratch_shapes=[pltpu.VMEM((n, chan), jnp.float32)] + [pltpu.VMEM((span, chan), jnp.float32)] * 3 + [pltpu.VMEM((span, n, chan), jnp.float32)] + [pltpu.VMEM((span, chan), jnp.float32)] * 2 + [pltpu.VMEM((span, TILE * n), jnp.bfloat16)] + [pltpu.VMEM((span * n, chan), jnp.bfloat16)] * 2,
        compiler_params=pltpu.CompilerParams(vmem_limit_bytes=32 << 20),
        cost_estimate=taking(36 * rows / 1024),
    )(lr, dtw, dtb, cf, ct, u, alog, skip, dy, starts)


def shifted(block, before, back):
    if back == 0:
        return block
    rows = block.shape[0]
    return jnp.concatenate([before[8 - back :], block[: rows - back]], 0)


def masked_sum(x, masks, weights, product):
    total = None
    for m in range(weights[0].shape[0]):
        held = x * masks[:, m : m + 1]
        parts = [product(held, w[m]) for w in weights]
        total = parts if total is None else [t + p for t, p in zip(total, parts)]
    return total


def enter_kernel(rows, masks, w, cw, cb, xp, conv_in, gate_in, pre_act, conv_out, part, tail):
    @pl.when(pl.program_id(0) == 0)
    def _():
        tail[...] = jnp.zeros_like(tail)

    taps = cw.shape[0]
    ax, az = masked_sum(rows[...], masks[...], (w.at[0], w.at[1]), mm)
    before = tail[...]
    pre = cb[...]
    for k in range(taps):
        pre = pre + cw[k : k + 1] * shifted(ax, before, taps - 1 - k)
    tail[...] = ax[-8:]
    out = (pre * jax.nn.sigmoid(pre)).astype(jnp.bfloat16)
    conv_in[...] = ax
    gate_in[...] = az
    pre_act[...] = pre
    conv_out[...] = out
    part[...] = mm(out, xp[...])


def whole_spec(a):
    return pl.BlockSpec(a.shape, lambda i: (0,) * len(a.shape))


def enter(rows, masks, w, cw, cb, xp, block):
    span, width = rows.shape
    chan, small = xp.shape
    tok = lambda w: pl.BlockSpec((block, w), lambda i: (i, 0))
    f = lambda w, t=jnp.float32: jax.ShapeDtypeStruct((span, w), t)
    return pl.pallas_call(
        enter_kernel,
        grid=(span // block,),
        in_specs=[tok(width), tok(masks.shape[1])] + [whole_spec(a) for a in (w, cw, cb, xp)],
        out_specs=[tok(chan)] * 4 + [tok(small)],
        out_shape=[f(chan), f(chan), f(chan), f(chan, jnp.bfloat16), f(small)],
        scratch_shapes=[pltpu.VMEM((8, chan), jnp.float32)],
        compiler_params=pltpu.CompilerParams(vmem_limit_bytes=56 << 20),
        cost_estimate=taking(20),
    )(rows, masks, w, cw, cb, xp)


def apply_kernel(masks, *refs, turned):
    *inputs, w, out = refs
    total = None
    for k, x in enumerate(inputs):
        (part,) = masked_sum(x[...], masks[...], (w.at[k],), mt if turned else mm)
        total = part if total is None else total + part
    out[...] = total.astype(out.dtype)


def apply(masks, inputs, w, turned, dtype, block):
    span = masks.shape[0]
    width = w.shape[2 if turned else 3]
    tok = lambda c: pl.BlockSpec((block, c), lambda i: (i, 0))
    return pl.pallas_call(
        functools.partial(apply_kernel, turned=turned),
        grid=(span // block,),
        in_specs=[tok(masks.shape[1])] + [tok(x.shape[1]) for x in inputs] + [whole_spec(w)],
        out_specs=tok(width),
        out_shape=jax.ShapeDtypeStruct((span, width), dtype),
        compiler_params=pltpu.CompilerParams(vmem_limit_bytes=56 << 20),
        cost_estimate=taking(20 * w.size / 6e6),
    )(masks, *inputs, w)


def leave_kernel(dval, dsmall, xp, pre_act, conv_in, prev_in, conv_out, cw, d_conv_in, grad_taps, grad_bias, grad_x, head):
    i = pl.program_id(0)
    steps = pl.num_programs(0)

    @pl.when(i == 0)
    def _():
        head[...] = jnp.zeros_like(head)
        grad_taps[...] = jnp.zeros_like(grad_taps)
        grad_bias[...] = jnp.zeros_like(grad_bias)
        grad_x[...] = jnp.zeros_like(grad_x)

    taps = cw.shape[0]
    d_out = (dval[...] + mt(dsmall[...], xp[...])).astype(jnp.bfloat16).astype(jnp.float32)
    pre = pre_act[...]
    sig = jax.nn.sigmoid(pre)
    d_pre = d_out * sig * (1.0 + pre * (1.0 - sig))
    before = jnp.where(i == steps - 1, 0.0, prev_in[...])
    held = conv_in[...]
    rows = held.shape[0]
    after = head[...]
    total = None
    for k in range(taps):
        back = taps - 1 - k
        grad_taps[k : k + 1] += jnp.sum(d_pre * shifted(held, before, back), axis=0, keepdims=True)
        moved = d_pre if back == 0 else jnp.concatenate([d_pre[back:], after[:back]], 0)
        term = cw[k : k + 1] * moved
        total = term if total is None else total + term
    head[...] = d_pre[:8]
    d_conv_in[...] = total.astype(jnp.bfloat16)
    grad_bias[...] += jnp.sum(d_pre, axis=0, keepdims=True)
    grad_x[...] += lax.dot_general(conv_out[...], dsmall[...], (((0,), (0,)), ((), ())), preferred_element_type=jnp.float32)


def leave(dval, dsmall, xp, pre_act, conv_in, conv_out, cw, block):
    span, chan = pre_act.shape
    steps = span // block
    taps, small = cw.shape[0], xp.shape[1]
    tok = lambda w: pl.BlockSpec((block, w), lambda i: (steps - 1 - i, 0))
    prev = pl.BlockSpec((8, chan), lambda i: (jnp.maximum((steps - 1 - i) * (block // 8) - 1, 0), 0))
    f = lambda *s: jax.ShapeDtypeStruct(s, jnp.float32)
    outs = [jax.ShapeDtypeStruct((span, chan), jnp.bfloat16), f(taps, chan), f(1, chan), f(chan, small)]
    return pl.pallas_call(
        leave_kernel,
        grid=(steps,),
        in_specs=[tok(chan), tok(small), whole_spec(xp), tok(chan), tok(chan), prev, tok(chan), whole_spec(cw)],
        out_specs=[tok(chan)] + [whole_spec(o) for o in outs[1:]],
        out_shape=outs,
        scratch_shapes=[pltpu.VMEM((8, chan), jnp.float32)],
        compiler_params=pltpu.CompilerParams(vmem_limit_bytes=56 << 20),
        cost_estimate=taking(8),
    )(dval, dsmall, xp, pre_act, conv_in, conv_in, conv_out, cw)


def sort_kernel(start, rank, *refs):
    inputs, out = refs[:-1], refs[-1]
    rows, span = out.shape[0], inputs[0].shape[0]
    first = start[0] + pl.program_id(0) * rows
    here = lax.broadcasted_iota(jnp.int32, (rows, span), 0) + first
    choose = jnp.where(rank[...] == here, 1.0, 0.0).astype(jnp.bfloat16)
    at = 0
    for x in inputs:
        out[:, at : at + x.shape[1]] = mm(choose, x[...]).astype(out.dtype)
        at += x.shape[1]


def sort_rows(start, rank, inputs, rows, block):
    span = inputs[0].shape[0]
    width = sum(x.shape[1] for x in inputs)
    return pl.pallas_call(
        sort_kernel,
        grid_spec=pltpu.PrefetchScalarGridSpec(
            num_scalar_prefetch=1,
            grid=(rows // block,),
            in_specs=[pl.BlockSpec((1, span), lambda i, s: (0, 0))]
            + [pl.BlockSpec((span, x.shape[1]), lambda i, s: (0, 0)) for x in inputs],
            out_specs=pl.BlockSpec((block, width), lambda i, s: (i, 0)),
        ),
        out_shape=jax.ShapeDtypeStruct((rows, width), inputs[0].dtype),
        compiler_params=pltpu.CompilerParams(vmem_limit_bytes=56 << 20),
        cost_estimate=taking(2 + 2e-9 * rows * span * width),
    )(start, rank, *inputs)


def contract(left, right, left_dim, right_dim):
    return lax.dot_general(
        left, right, (((left_dim,), (right_dim,)), ((), ())), preferred_element_type=jnp.float32
    )


def own(array, dim, size):
    return lax.dynamic_slice_in_dim(array, lax.axis_index("wide") * size, size, dim)


def pick(array, index, dim=0):
    return lax.dynamic_index_in_dim(array, index, dim, False)


def cross(array, k):
    return lax.ppermute(array, "wide", [(i, i ^ k) for i in range(lax.axis_size("wide"))])


def gather_wide(shard, early, late):
    if lax.axis_size("wide") != 8:
        return lax.all_gather(shard, "wide", axis=0), early(), late()
    half = shard.shape[0] // 2
    by_x, by_y, pair = cross(shard, 2), cross(shard, 4), cross(shard, 1)
    early, by_x, by_y, pair = lax.optimization_barrier((early(), by_x, by_y, pair))
    far = (cross(by_y[:half], 2), cross(by_x[half:], 4))
    pair_x, pair_y = cross(by_x, 1), cross(by_y, 1)
    late, *far = lax.optimization_barrier((late(),) + far)
    far = jnp.concatenate(far, 0)
    blocks = [shard, pair, by_x, pair_x, by_y, pair_y, far, cross(far, 1)]
    here = lax.axis_index("wide")
    whole = jnp.zeros((8,) + shard.shape, shard.dtype)
    for k, block in enumerate(blocks):
        whole = lax.dynamic_update_index_in_dim(whole, block, here ^ k, 0)
    return whole, early, late


def sum_wide(part, work):
    if lax.axis_size("wide") != 8:
        return lax.psum(part, "wide"), work()
    half = part.shape[0] // 2
    core = lax.axis_index("wide") % 2
    mine = lax.dynamic_slice_in_dim(part, core * half, half, 0)
    other = lax.dynamic_slice_in_dim(part, (1 - core) * half, half, 0)
    mine = mine + cross(other, 1)
    sent = mine.astype(jnp.bfloat16)
    beside, *came = lax.optimization_barrier((work(),) + tuple(cross(sent, k) for k in (2, 4, 6)))
    total = mine
    for block in came:
        total = total + block.astype(jnp.float32)
    other = cross(total, 1)
    return jnp.where(core == 0, jnp.concatenate([total, other], 0), jnp.concatenate([other, total], 0)), beside


def scatter_wide(part, work):
    if lax.axis_size("wide") != 8:
        return lax.psum_scatter(part, "wide", scatter_dimension=0, tiled=True).astype(jnp.float32), work()
    here = lax.axis_index("wide")
    core, chip = here % 2, here // 2
    view = part.reshape(4, 2, part.shape[0] // 8, part.shape[1])
    mine = pick(view, core, 1).astype(jnp.float32) + cross(pick(view, 1 - core, 1), 1).astype(jnp.float32)
    came = tuple(cross(pick(mine, chip ^ (k // 2)).astype(jnp.bfloat16), k) for k in (2, 4, 6))
    beside, *came = lax.optimization_barrier((work(),) + came)
    total = pick(mine, chip)
    for block in came:
        total = total + block.astype(jnp.float32)
    return total, beside


def after(value, *first):
    return lax.optimization_barrier((value,) + first)[0]


def hop(rising, falling):
    return (
        lax.ppermute(rising, "row", [(0, 1), (1, 2), (2, 3)]),
        lax.ppermute(falling, "row", [(1, 0), (2, 1), (3, 2)]),
    )


def arrange_near(hops):
    return jnp.where(lax.axis_index("row") == 0, hops[0][1], hops[0][0])


def arrange_middle(hops):
    return hops[1][0] + hops[1][1]


def arrange_last(hops):
    here = lax.axis_index("row")
    return jnp.where(here == 3, hops[2][0], jnp.where(here == 0, hops[2][1], hops[0][1]))


def arrange(block, hops):
    return [block, arrange_near(hops), arrange_middle(hops), arrange_last(hops)]


def sum_row(part):
    if lax.axis_size("row") != 4:
        return lax.psum(part, "row")
    for k in (1, 2):
        part = part + lax.ppermute(part, "row", [(i, i ^ k) for i in range(4)])
    return part


def sum_row_low(part):
    if lax.axis_size("row") != 4:
        return lax.psum(part.astype(jnp.bfloat16), "row").astype(jnp.float32)
    for k in (1, 2):
        sent = lax.ppermute(part.astype(jnp.bfloat16), "row", [(i, i ^ k) for i in range(4)])
        part = part + sent.astype(jnp.float32)
    return part


def share_wide(part):
    count = lax.axis_size("wide")
    if count != 8:
        return lax.psum_scatter(part, "wide", scatter_dimension=0, tiled=True)
    for k in (1, 2, 4):
        part = part + cross(part, k)
    return own(part, 0, part.shape[0] // count)


def row_order():
    count = lax.axis_size("row")
    here = lax.axis_index("row")
    if count != 4:
        return [lax.rem(here + s, count) for s in range(count)]
    near = jnp.where(here == 0, 1, here - 1)
    last = jnp.where(here == 3, 0, jnp.where(here == 0, 3, here + 1))
    return [here, near, lax.rem(here + 2, 4), last]


def others(array, order):
    return jnp.stack([pick(array, q) for q in order[1:]], 0)


def gather_ordered(block, order):
    whole = lax.all_gather(block, "row", axis=0)
    return [block] + [pick(whole, q) for q in order[1:]]


def sorted_places(ids, mods):
    one = (ids[:, None] == jnp.arange(mods, dtype=ids.dtype)[None]).astype(jnp.int32)
    before = jnp.cumsum(one, 0)
    total = before[-1]
    first = jnp.cumsum(total) - total
    return jnp.sum(one * (before - 1 + first[None]), 1)[None]


def group_bounds(ids, mods):
    count = jnp.sum((ids[:, None] == jnp.arange(mods, dtype=ids.dtype)).astype(jnp.int32), 0)
    return jnp.concatenate([jnp.zeros((1,), jnp.int32), jnp.cumsum(count)], 0)


def local(
    hidden,
    modality,
    norm_gain,
    in_proj,
    conv_weight,
    conv_bias,
    x_proj_dt,
    x_proj_bc,
    dt_proj,
    dt_bias,
    a_log,
    skip_weight,
    out_proj,
    cotangent,
):
    shard_rows, width = hidden.shape
    mods = in_proj.shape[0]
    chan = in_proj.shape[3]
    taps = conv_weight.shape[0]
    n = a_log.shape[0]
    rank = dt_proj.shape[0]
    row_count = lax.axis_size("row")
    residual = hidden.astype(jnp.float32)
    inv_rms = lax.rsqrt(jnp.mean(residual * residual, axis=-1, keepdims=True) + EPS)
    gain_vec = norm_gain.astype(jnp.float32)
    normed = (residual * inv_rms * gain_vec).astype(jnp.bfloat16)
    lanes = jnp.pad(modality.astype(jnp.bfloat16)[None], ((0, 15), (0, width - shard_rows)))
    conv_taps = conv_weight.astype(jnp.float32)
    w_out = out_proj[None]

    def small_slices():
        x_proj = jnp.concatenate([own(x_proj_dt, 0, chan), own(x_proj_bc, 0, chan)], 1)
        return x_proj, own(dt_proj, 1, chan), own(dt_bias, 0, chan)[None], own(a_log, 1, chan), own(skip_weight, 0, chan)[None]

    gathered, w_in, (x_proj, dtw, dtb, alog, skip) = gather_wide(
        jnp.concatenate([normed, lanes], 0), lambda: jnp.transpose(in_proj, (2, 0, 1, 3)), small_slices
    )
    rows = gathered[:, :shard_rows].reshape(-1, width)
    ids = gathered[:, shard_rows, :shard_rows].astype(jnp.int32).reshape(-1)
    masks = (ids[:, None] == jnp.arange(128, dtype=ids.dtype)[None]).astype(jnp.bfloat16)
    span_rows = rows.shape[0]
    block = min(256, span_rows)
    order = row_order()
    slot = jnp.arange(row_count, dtype=jnp.int32)[:, None] == lax.axis_index("row")
    whole = jnp.zeros((1,), jnp.int32)
    chunk = lax.axis_index("wide").astype(jnp.int32)[None] * shard_rows
    conv_in, gate_in, pre_act, conv_out, part = enter(
        rows, masks, w_in, conv_taps, conv_bias.astype(jnp.float32)[None], x_proj, block
    )
    places = sorted_places(ids, mods)

    def sort_chunk():
        return sort_rows(chunk, places, (rows,), shard_rows, shard_rows)

    cot_gathered, part, rows_chunk = gather_wide(after(cotangent, rows), lambda: part, sort_chunk)
    cot_rows = cot_gathered.reshape(-1, width)
    rows_near = lax.all_gather(rows_chunk, "row", axis=0)

    def first_work():
        cot_chunk = sort_rows(chunk, places, (cot_rows,), shard_rows, shard_rows)
        return cot_chunk, apply(masks, (cot_rows,), w_out, True, jnp.float32, block)

    small, (cot_chunk, d_gated) = sum_wide(part, first_work)
    small, rows_near = lax.optimization_barrier((small, rows_near))
    cot_near = lax.all_gather(cot_chunk, "row", axis=0)
    rows_far = lax.all_gather(others(rows_near, order), "wide", axis=0)
    low_rank = small[:, :rank].astype(jnp.bfloat16)
    coefs = small[:, rank:]
    gated, d_y, d_gate_in, starts = scan_forward(
        low_rank, dtw, dtb, coefs, coefs.T, conv_out, alog, skip, gate_in, d_gated
    )
    line = row_count == 4
    gates = sort_rows(whole, places, (gated, d_gate_in), span_rows, block)
    d_y, gates = lax.optimization_barrier((d_y, gates))
    gate_hops = [hop(gates, gates)] if line else []
    d_pre_step, d_value, d_low_part, d_in, d_out, grad_alog, grad_skip, grad_bias, grad_wdtp = scan_backward(
        low_rank, dtw, dtb, coefs, coefs.T, conv_out, alog, skip, d_y, starts
    )
    d_part = jnp.concatenate([d_low_part, d_in.reshape(span_rows, n), d_out.reshape(span_rows, n)], 1)
    if line:
        d_part, cot_near, gate_hops[0] = lax.optimization_barrier((d_part, cot_near, gate_hops[0]))
        gate_hops.append(hop(*gate_hops[0]))
    cot_far = lax.all_gather(others(cot_near, order), "wide", axis=0)
    d_small, projected = sum_wide(
        d_part, lambda: apply(masks, (after(gated, d_part),), w_out, False, jnp.bfloat16, block)
    )
    d_small = d_small.astype(jnp.bfloat16)
    if line:
        d_small, projected, gate_hops[1] = lax.optimization_barrier((d_small, projected, gate_hops[1]))
        gate_hops.append(hop(*gate_hops[1]))
    d_conv_in, grad_taps, grad_cbias, grad_x = leave(
        d_value, d_small, x_proj, pre_act, conv_in, conv_out, conv_taps, block
    )
    conv_sorted = sort_rows(whole, places, (d_conv_in,), span_rows, block)
    d_conv_in, conv_sorted = lax.optimization_barrier((d_conv_in, conv_sorted))
    conv_hops = [hop(conv_sorted, conv_sorted)] if line else []

    def second_work():
        part = apply(masks, (d_conv_in, d_gate_in), w_in, True, jnp.bfloat16, block)
        rows_sorted = sort_rows(whole, places, (after(rows, d_conv_in),), span_rows, block)
        cot_sorted = sort_rows(whole, places, (after(cot_rows, d_conv_in),), span_rows, block)
        return part, rows_sorted, cot_sorted

    projected, (normed_part, rows_sorted, cot_sorted) = scatter_wide(projected, second_work)
    output = (residual + projected).astype(jnp.bfloat16)
    bounds = sum_row(jnp.where(slot, group_bounds(after(ids, d_small), mods)[None], 0))
    bounds = jnp.stack([pick(bounds, q) for q in order], 0)
    if line:
        normed_part, gate_hops[2], conv_hops[0] = lax.optimization_barrier((normed_part, gate_hops[2], conv_hops[0]))
        conv_hops.append(hop(*conv_hops[0]))
        gates = arrange(gates, gate_hops)
    else:
        gates = gather_ordered(gates, order)
        conv_all = gather_ordered(conv_sorted, order)
    apart = lambda a: a.reshape(span_rows // shard_rows, 1, shard_rows, width)
    far = range(row_count - 1)
    rows_slots = [(apart(rows_sorted), 0)] + [(rows_far, s) for s in far]
    cot_slots = [(apart(cot_sorted), 0)] + [(cot_far, s) for s in far]
    d_normed, grad_z = scatter_wide(normed_part, lambda: grad_in(bounds, rows_slots, gates, mods, chan, 1))
    weighted = gain_vec * d_normed
    grad_hidden = (
        cotangent.astype(jnp.float32)
        + inv_rms * weighted
        - residual * inv_rms * inv_rms * inv_rms * jnp.mean(weighted * residual, axis=-1, keepdims=True)
    )
    g_gain = sum_row(share_wide(jnp.sum(d_normed * residual * inv_rms, 0)))

    if line:
        grad_z, conv_hops[1] = lax.optimization_barrier((grad_z, conv_hops[1]))
        conv_hops.append(hop(*conv_hops[1]))
        early = [conv_sorted, arrange_near(conv_hops), arrange_middle(conv_hops)]
    else:
        early = conv_all[:-1]
    grad_x_most = grad_in(bounds[:-1], rows_slots[:-1], early, mods, chan, 0)
    grad_wout = grad_out(bounds, cot_slots, gates, mods, chan, 0)
    if line:
        grad_x_most, grad_wout, conv_hops[2] = lax.optimization_barrier((grad_x_most, grad_wout, conv_hops[2]))
        last = arrange_last(conv_hops)
    else:
        last = conv_all[-1]
    grad_win = grad_in(bounds[-1:], rows_slots[-1:], [last], mods, chan, 0, grad_x_most, grad_z)
    grad_win = grad_win.reshape(mods, width, chan // 128, 2, 128).transpose(0, 1, 3, 2, 4).reshape(mods, width, 2, chan)
    small_grads = (grad_taps, grad_cbias[0], grad_x, grad_wdtp, grad_bias[0], grad_alog, grad_skip[0])
    flat = after(jnp.concatenate([g.reshape(-1) for g in small_grads]).reshape(-1, 128), grad_z)
    flat = sum_row_low(flat).reshape(-1)
    summed, at = [], 0
    for g in small_grads:
        summed.append(flat[at : at + g.size].reshape(g.shape))
        at += g.size
    g_taps, g_cbias, g_x, g_wdtp, g_bias, g_alog, g_skip = summed
    return (
        output,
        grad_hidden,
        g_gain,
        grad_win,
        g_taps,
        g_cbias,
        g_x[:, :rank],
        g_x[:, rank:],
        g_wdtp,
        g_bias,
        g_alog,
        g_skip,
        grad_wout,
    )


def solution(mesh):
    return jax.shard_map(
        local,
        mesh=mesh,
        in_specs=(
            P(("row", "wide"), None),
            P(("row", "wide")),
            P(),
            P(None, None, None, "wide"),
            P(None, "wide"),
            P("wide"),
            P(),
            P(),
            P(),
            P(),
            P(),
            P(),
            P(None, "wide", None),
            P(("row", "wide"), None),
        ),
        out_specs=(
            P(("row", "wide"), None),
            P(("row", "wide"), None),
            P("wide"),
            P(None, None, None, "wide"),
            P(None, "wide"),
            P("wide"),
            P("wide", None),
            P("wide", None),
            P(None, "wide"),
            P("wide"),
            P(None, "wide"),
            P("wide"),
            P(None, "wide", None),
        ),
        check_vma=False,
    )
```

time: 4430 us -> 573 us (0.13)
  local copies, waits for them, and re-layouts: 1790 us -> 64.4 us
  other arithmetic: 1610 us -> 47.1 us
  waiting for transfers between devices: 648 us -> 117 us
  Pallas kernels: 0 us -> 246 us
  matrix products: 156 us -> 0 us
  loops' own time: 75.7 us -> 0 us
  blocking collectives: 62.6 us -> 0 us
  starting transfers between devices: 27.9 us -> 73.8 us
    pad x192 -> x0, local copies, waits for them, and re-layouts: 1280 us -> none  [the longest x64 437 us: retreat(): lax.associative_scan(combine, (factor, inject), axis=0)]
    add x215 -> x15, other arithmetic: 846 us -> 14.3 us  [the longest x2 7.3 us: arrange_middle(): return hops[1][0] + hops[1][1]]
    psum x1 -> x0, waiting for transfers between devices: 579 us -> none  [local(): lax.psum(grad_win.astype(jnp.bfloat16), 'row').astype(jnp.float32)]
    pallas_call x0 -> x17, Pallas kernels: none -> 246 us  [the longest x3 68.6 us: grad_in(): pl.pallas_call(functools.partial(grad_in_kernel, slots=slots, begun=start...]
    reduce_sum x29 -> x3, other arithmetic: 234 us -> 3.39 us  [the longest x1 2.3 us: local(): g_gain = sum_row(share_wide(jnp.sum(d_normed * residual * inv_rms, 0)))]
    concatenate x93 -> x4, other arithmetic: 168 us -> 1.91 us  [the longest x1 0.88 us: local(): jnp.concatenate([normed, lanes], 0)]
    dot_general x33 -> x0, matrix products: 156 us -> none  [the longest x30 149 us: contract(): lax.dot_general(left, right, (((left_dim,), (right_dim,)), ((), ())), pre...]
    slice x124 -> x15, local copies, waits for them, and re-layouts: 157 us -> 4.98 us  [the longest x1 2.32 us: local(): rows = gathered[:, :shard_rows].reshape(-1, width)]
  transfers between devices with their start and end apart: 16 -> 59, of which waited for: 6 -> 20; matrix products, arithmetic and copies ran while one was open for 14% -> 16% of each run, Pallas kernels for 0% -> 39%
where the time goes in v1:
time: 573 us; the launch traced here: 563 us
  Pallas kernels  246 us (43%)
  waiting for transfers between devices  117 us (20%)
  starting transfers between devices  73.8 us (13%)
  local copies, waits for them, and re-layouts  64.4 us (11%)
  other arithmetic  47.1 us (8%)
  between operations  15.2 us (3%)
    pallas_call x3, Pallas kernels, grad_in(): pl.pallas_call(functools.partial(grad_in_kernel, slots=slots, begun=start...  68.6 us
    ppermute x37, waiting for transfers between devices, cross(): lax.ppermute(array, 'wide', [(i, i ^ k) for i in range(lax.axis_size('wid...  47.4 us
    pallas_call x3, Pallas kernels, apply(): pl.pallas_call(functools.partial(apply_kernel, turned=turned), grid=(span...  42.5 us
    pallas_call x1, Pallas kernels, scan_backward(): pl.pallas_call(bwd_kernel, grid=(steps,), in_specs=[tok(rank), full(dtw),...  36.3 us
    pallas_call x6, Pallas kernels, sort_rows(): pl.pallas_call(sort_kernel, grid_spec=pltpu.PrefetchScalarGridSpec(num_sc...  33.9 us
    ppermute x6, starting transfers between devices, hop(): lax.ppermute(rising, 'row', [(0, 1), (1, 2), (2, 3)])  29 us
    ppermute x37, starting transfers between devices, cross(): lax.ppermute(array, 'wide', [(i, i ^ k) for i in range(lax.axis_size('wid...  27.2 us
    unnamed x82, local copies, waits for them, and re-layouts  26.1 us
  transfers between devices with their start and end apart: 59, of which 20 were waited for; matrix products, arithmetic and copies ran while one was open for 16% of the time, Pallas kernels for 39%

profile of v1, /device:TPU:0, one launch (start us, length us, event | category | flops | bytes accessed | tf_op | source)
XLA Modules:
  0.0 563.4 jit_solution(8960686159803561969)
XLA Ops:
  22.2 12.1 %copy.71 = bf16[3,2048,2,512]{3,1,0,2:T(8,128)(2,1)} copy(bf16[3,2048,2,512]{3,2,1,0:T(2,128)(2,1)} %param.17) | data formatting | bytes 25165824 | tf_op args[3]
  38.1 8.6 %collective-permute-done.5 = bf16[72,2048]{1,0:T(8,128)(2,1)S(1)} collective-permute-done((bf16[72,2048]{1,0:T(8,128)(2,1)S(1)}, bf16[72,2048]{1,0:T(8,128)(2,1)S(1)}, u32[]{:S(2)}, u32[]{:S(2)}) %collective-permute-start.5) | collective-permute-done | bytes 294944 | tf_op jit(solution)/shard_map/ppermute | solution.py:516
  57.4 20.6 %shard_map.237 = (f32[1024,512]{1,0:T(8,128)}, f32[1024,512]{1,0:T(8,128)}, f32[1024,512]{1,0:T(8,128)}, bf16[1024,512]{1,0:T(8,128)(2,1)}, f32[1024,160]{1,0:T(8,128)}) custom-call(bf16[1024,2048]{1,0:T(8,128)(2,1)} %bitcast.148, bf16[1024,128]{1,0:T(8,128)(2,1)} %fusion.24.masks, bf16[2,3,2048,512]{3,2,1,0:T(8,128)(2,1)} %bitcast.143, ...), custom_call_target="tpu_custom_call" | custom-call | flops 21999998976 | tf_op jit(solution)/shard_map/pallas_call | solution.py:382
  107.3 11.4 %shard_map.240.dgated = f32[1024,512]{1,0:T(8,128)} custom-call(bf16[1024,128]{1,0:T(8,128)(2,1)} %fusion.24.masks, bf16[1024,2048]{1,0:T(8,128)(2,1)} %bitcast.30.refs_0_, bf16[1,3,512,2048]{3,2,1,0:T(8,128)(2,1)} %bitcast.180), custom_call_target="tpu_custom_call" | custom-call | flops 11534336000 | tf_op jit(solution)/shard_map/pallas_call | solution.py:407
  127.4 15.1 %all-gather.9.cloned.1.call-done = bf16[512,2048]{1,0:T(8,128)(2,1)} async-done(((bf16[128,2048]{1,0:T(8,128)(2,1)}), bf16[512,2048]{1,0:T(8,128)(2,1)}) %all-gather.9.cloned.1.call-update) | async-done | bytes 2097168 | tf_op jit(solution)/shard_map/all_gather | solution.py:712
  150.1 12.8 %shard_map.241 = (bf16[1024,512]{1,0:T(8,128)(2,1)S(1)}, bf16[1024,512]{1,0:T(8,128)(2,1)S(1)}, bf16[1024,512]{1,0:T(8,128)(2,1)S(1)}, f32[4,16,512]{2,1,0:T(8,128)S(1)}) custom-call(bf16[1024,128]{1,0:T(8,128)(2,1)S(1)} %slice.121.lr, bf16[128,512]{1,0:T(8,128)(2,1)S(1)} %constant_dynamic-slice_fusion.13.dtw, f32[1,512]{1,0:T(1,128)S(1)} %bitcast.130, ...), custom_call_target="tpu_custom_call" | custom-call | flops 14300000256 | tf_op jit(solution)/shard_map/pallas_call | solution.py:225
  164.9 5.3 shard_map.242.refs_4_
  171.5 5.8 %collective-permute-start.21 = (bf16[1024,1024]{1,0:T(8,128)(2,1)}, bf16[1024,1024]{1,0:T(8,128)(2,1)}, u32[]{:S(2)}, u32[]{:S(2)}) collective-permute-start(bf16[1024,1024]{1,0:T(8,128)(2,1)} %shard_map.242.refs_4_), channel_id=1, source_target_pairs={{0,8},{8,16},{16,24},{1,9},{9,17},{17,25},{2,10},{10,18},{18,26},{... | collective-permute-start | bytes 6291464 | tf_op jit(solution)/shard_map/ppermute | solution.py:575
  177.3 36.3 %shard_map.243 = (bf16[1024,512]{1,0:T(8,128)(2,1)}, f32[1024,512]{1,0:T(8,128)S(1)}, f32[1024,128]{1,0:T(8,128)S(1)}, f32[4,16,256]{2,1,0:T(8,128)S(1)}, f32[4,...) custom-call(bf16[1024,128]{1,0:T(8,128)(2,1)S(1)} %slice.121.lr, ...), custom_call_target="tpu_custom_call" | custom-call | flops 39600001024 | tf_op jit(solution)/shard_map/pallas_call | solution.py:326
  215.6 16.4 %collective-permute-done.22 = bf16[1024,1024]{1,0:T(8,128)(2,1)} collective-permute-done((bf16[1024,1024]{1,0:T(8,128)(2,1)}, bf16[1024,1024]{1,0:T(8,128)(2,1)}, u32[]{:S(2)}, u32[]{:S(2)}) %collective-permute-start.22) | collective-permute-done | bytes 2097184 | tf_op jit(solution)/shard_map/ppermute | solution.py:576
  235.0 5.1 collective-permute-start.28
  245.0 11.4 %shard_map.244 = bf16[1024,2048]{1,0:T(8,128)(2,1)} custom-call(bf16[1024,128]{1,0:T(8,128)(2,1)} %fusion.24.masks, bf16[1024,512]{1,0:T(8,128)(2,1)} %copy-done.3, bf16[1,3,512,2048]{3,2,1,0:T(8,128)(2,1)} %bitcast.181), custom_call_target="tpu_custom_call" | custom-call | flops 11534336000 | tf_op jit(solution)/shard_map/pallas_call | solution.py:407
  257.2 5.9 %collective-permute-done.25 = bf16[512,160]{1,0:T(8,128)(2,1)S(1)} collective-permute-done((bf16[512,160]{1,0:T(8,128)(2,1)S(1)}, bf16[512,160]{1,0:T(8,128)(2,1)S(1)}, u32[]{:S(2)}, u32[]{:S(2)}) %collective-permute-start.25) | collective-permute-done | bytes 163872 | tf_op jit(solution)/shard_map/ppermute | solution.py:516
  263.1 5.1 collective-permute-done.24
  271.0 13.6 %collective-permute-done.28 = bf16[1024,1024]{1,0:T(8,128)(2,1)} collective-permute-done((bf16[1024,1024]{1,0:T(8,128)(2,1)}, bf16[1024,1024]{1,0:T(8,128)(2,1)}, u32[]{:S(2)}, u32[]{:S(2)}) %collective-permute-start.28) | collective-permute-done | bytes 2097184 | tf_op jit(solution)/shard_map/ppermute | solution.py:575
  284.6 5.4 collective-permute-done.29
  292.0 7.6 %shard_map.245 = (bf16[1024,512]{1,0:T(8,128)(2,1)}, f32[4,512]{1,0:T(4,128)}, f32[1,512]{1,0:T(1,128)}, f32[512,160]{1,0:T(8,128)}) custom-call(f32[1024,512]{1,0:T(8,128)} %copy-done.4, bf16[1024,160]{1,0:T(8,128)(2,1)} %fusion.12.dsmall, bf16[512,160]{1,0:T(8,128)(2,1)} %pad_maximum_fusion.3.xp, f32[1024,512]{1,0:T(8,128)} %get-tuple-element.151.pre_act, ...), custom_call_target="tpu_custom_call" | custom-call | flops 8800000000 | tf_op jit(solution)/shard_map/pallas_call | solution.py:459
  299.6 4.1 shard_map.246.refs_3_
  316.4 19.8 %shard_map.247 = bf16[1024,2048]{1,0:T(8,128)(2,1)} custom-call(bf16[1024,128]{1,0:T(8,128)(2,1)} %fusion.24.masks, bf16[1024,512]{1,0:T(8,128)(2,1)} %get-tuple-element.154.refs_0_, bf16[1024,512]{1,0:T(8,128)(2,1)} %copy-done.2, bf16[2,3,2048,512]{3,2,1,0:T(8,128)(2,1)} %bitcast.144), custom_call_target="tpu_custom_call" | custom-call | flops 23068672000 | tf_op jit(solution)/shard_map/pallas_call | solution.py:407
  337.5 5.2 collective-permute-start.36
  343.7 8.4 %shard_map.249 = bf16[1024,2048]{1,0:T(8,128)(2,1)} custom-call(s32[1]{0:T(128)} %constant.178.clone.1.start, s32[1,1024]{1,0:T(1,128)} %bitcast.172, bf16[1024,2048]{1,0:T(8,128)(2,1)} %bitcast.30.refs_0_), custom_call_target="tpu_custom_call" | custom-call | flops 6924464128 | tf_op jit(solution)/shard_map/pallas_call | solution.py:486
  352.1 16.7 %collective-permute-done.32 = bf16[128,2048]{1,0:T(8,128)(2,1)S(1)} collective-permute-done((bf16[128,2048]{1,0:T(8,128)(2,1)}, bf16[128,2048]{1,0:T(8,128)(2,1)S(1)}, u32[]{:S(2)}, u32[]{:S(2)}) %collective-permute-start.32) | collective-permute-done | bytes 524320 | tf_op jit(solution)/shard_map/ppermute | solution.py:516
  370.1 8.5 %shard_map.248 = bf16[1024,2048]{1,0:T(8,128)(2,1)} custom-call(s32[1]{0:T(128)} %constant.178.clone.1.start, s32[1,1024]{1,0:T(1,128)} %bitcast.173, bf16[1024,2048]{1,0:T(8,128)(2,1)} %bitcast.150), custom_call_target="tpu_custom_call" | custom-call | flops 6924464128 | tf_op jit(solution)/shard_map/pallas_call | solution.py:486
  388.8 4.5 add.271.refs_6_
  399.5 4.7 select_select_fusion
  413.3 24.6 %shard_map.250.refs_3_ = f32[3,2048,512]{2,1,0:T(8,128)} custom-call(s32[4,4]{1,0:T(4,128)} %pad_add_fusion.bounds, bf16[8,1,128,2048]{3,2,1,0:T(8,128)(2,1)} %bitcast.183, bf16[8,3,128,2048]{3,2,1,0:T(8,128)(2,1)} %bitcast.137, bf16[8,3,128,2048]{3,2,1,0:T(8,128)(2,1)} %bitcast.138, bf16[8,3,128,2048]{3,2,1,0:T(8,128)(2,1)} %bitcast.139, ...), custom_call_target="tpu_custom_call" | custom-call | flops 32999999488 | tf_op jit(solution)/shard_map/pallas_call | solution.py:132
  443.2 5.6 collective-permute-start.51
  457.4 20.2 %shard_map.251.refs_2_ = f32[3,2048,512]{2,1,0:T(8,128)} custom-call(s32[3,4]{1,0:T(4,128)} %pad_add_fusion.1.bounds, bf16[8,1,128,2048]{3,2,1,0:T(8,128)(2,1)} %bitcast.184, bf16[8,3,128,2048]{3,2,1,0:T(8,128)(2,1)} %bitcast.140, bf16[8,3,128,2048]{3,2,1,0:T(8,128)(2,1)} %bitcast.141, bf16[1024,512]{1,0:T(8,128)(2,1)} %shard_map.246.refs_3_, ...), custom_call_target="tpu_custom_call" | custom-call | flops 26400000000 | tf_op jit(solution)/shard_map/pallas_call | solution.py:132
  477.7 7.5 %collective-permute-done.47 = f32[256]{0:T(256)S(1)} collective-permute-done((f32[256]{0:T(256)S(1)}, f32[256]{0:T(256)S(1)}, u32[]{:S(2)}, u32[]{:S(2)}) %collective-permute-start.47) | collective-permute-done | bytes 1056 | tf_op jit(solution)/shard_map/ppermute | solution.py:601
  492.1 9.7 %collective-permute-done.54 = bf16[1244,128]{1,0:T(8,128)(2,1)S(1)} collective-permute-done((bf16[1244,128]{1,0:T(8,128)(2,1)S(1)}, bf16[1244,128]{1,0:T(8,128)(2,1)S(1)}, u32[]{:S(2)}, u32[]{:S(2)}) %collective-permute-start.54) | collective-permute-done | bytes 318496 | tf_op jit(solution)/shard_map/ppermute | solution.py:609
  506.3 24.0 %shard_map.252 = f32[3,512,2048]{2,1,0:T(8,128)} custom-call(s32[4,4]{1,0:T(4,128)} %pad_add_fusion.bounds, bf16[8,1,128,2048]{3,2,1,0:T(8,128)(2,1)} %bitcast.182, bf16[8,3,128,2048]{3,2,1,0:T(8,128)(2,1)} %bitcast.177, bf16[8,3,128,2048]{3,2,1,0:T(8,128)(2,1)} %bitcast.178, bf16[8,3,128,2048]{3,2,1,0:T(8,128)(2,1)} %bitcast.179, ...), custom_call_target="tpu_custom_call" | custom-call | flops 30799998976 | tf_op jit(solution)/shard_map/pallas_call | solution.py:166
  532.7 23.8 %shard_map.253 = f32[3,16384,128]{2,1,0:T(8,128)} custom-call(s32[1,4]{1,0:T(1,128)} %copy-done.30, bf16[8,3,128,2048]{3,2,1,0:T(8,128)(2,1)} %bitcast.142, bf16[1024,512]{1,0:T(8,128)(2,1)} %select_select_fusion.1.refs_1_, f32[3,2048,512]{2,1,0:T(8,128)} %shard_map.251.refs_2_, f32[3,2048,512]{2,1,0:T(8,128)} %shard_map.250.refs_3_), custom_call_target="tpu_custom_call" | custom-call | flops 13200000000 | tf_op jit(solution)/shard_map/pallas_call | solution.py:132
  (304 shorter events, 162.3 us)
Async XLA Ops:
  7.2 135.3 %all-gather.9.cloned.1.call-start = ((), (), s32[]{:S(2)}) async-start(), calls=%async_computation | async-start | bytes 2621440 | tf_op jit(solution)/shard_map/all_gather | solution.py:712
  12.0 24.6 %collective-permute-start.1 = (bf16[144,2048]{1,0:T(8,128)(2,1)}, bf16[144,2048]{1,0:T(8,128)(2,1)S(1)}, u32[]{:S(2)}, u32[]{:S(2)}) collective-permute-start(bf16[144,2048]{1,0:T(8,128)(2,1)} %fusion.17), channel_id=1, source_target_pairs={{0,4},{1,5},{2,6},{3,7},{4,0},{5,1},{6,2},{7,3},{8,12},{9,13},{10,... | collective-permute-start | bytes 1769480 | tf_op jit(solution)/shard_map/ppermute | solution.py:516
  15.0 21.6 %collective-permute-start = (bf16[144,2048]{1,0:T(8,128)(2,1)}, bf16[144,2048]{1,0:T(8,128)(2,1)S(1)}, u32[]{:S(2)}, u32[]{:S(2)}) collective-permute-start(bf16[144,2048]{1,0:T(8,128)(2,1)} %fusion.17), channel_id=1, source_target_pairs={{0,2},{1,3},{2,0},{3,1},{4,6},{5,7},{6,4},{7,5},{8,10},{9,11},{10,... | collective-permute-start | bytes 1769480 | tf_op jit(solution)/shard_map/ppermute | solution.py:516
  51.6 33.4 %collective-permute-start.10 = (bf16[128,2048]{1,0:T(8,128)(2,1)S(1)}, bf16[128,2048]{1,0:T(8,128)(2,1)}, u32[]{:S(2)}, u32[]{:S(2)}) collective-permute-start(bf16[128,2048]{1,0:T(8,128)(2,1)S(1)} %copy-done.17), channel_id=1, source_target_pairs={{0,1},{1,0},{2,3},{3,2},{4,5},{5,4},{6,7},{7,6},{8,9},{9,8},{10,11... | collective-permute-start | bytes 1572872 | tf_op jit(solution)/shard_map/ppermute | solution.py:516
  51.7 33.2 %collective-permute-start.9 = (bf16[128,2048]{1,0:T(8,128)(2,1)S(1)}, bf16[128,2048]{1,0:T(8,128)(2,1)S(1)}, u32[]{:S(2)}, u32[]{:S(2)}) collective-permute-start(bf16[128,2048]{1,0:T(8,128)(2,1)S(1)} %copy-done.17), channel_id=1, source_target_pairs={{0,4},{1,5},{2,6},{3,7},{4,0},{5,1},{6,2},{7,3},{8,12},{9,13},{10,... | collective-permute-start | bytes 1572872 | tf_op jit(solution)/shard_map/ppermute | solution.py:516
  52.0 32.9 %collective-permute-start.8 = (bf16[128,2048]{1,0:T(8,128)(2,1)S(1)}, bf16[128,2048]{1,0:T(8,128)(2,1)}, u32[]{:S(2)}, u32[]{:S(2)}) collective-permute-start(bf16[128,2048]{1,0:T(8,128)(2,1)S(1)} %copy-done.17), channel_id=1, source_target_pairs={{0,2},{1,3},{2,0},{3,1},{4,6},{5,7},{6,4},{7,5},{8,10},{9,11},{10,... | collective-permute-start | bytes 1572872 | tf_op jit(solution)/shard_map/ppermute | solution.py:516
  95.6 119.9 %all-gather.11.cloned.1.call-start = ((), (), s32[]{:S(2)}) async-start(), calls=%async_computation.1 | async-start | bytes 2621440 | tf_op jit(solution)/shard_map/all_gather | solution.py:720
  97.5 24.9 %collective-permute-start.19 = (bf16[512,160]{1,0:T(8,128)(2,1)}, bf16[512,160]{1,0:T(8,128)(2,1)S(1)}, u32[]{:S(2)}, u32[]{:S(2)}) collective-permute-start(bf16[512,160]{1,0:T(8,128)(2,1)} %fusion.26), channel_id=1, source_target_pairs={{0,6},{1,7},{2,4},{3,5},{4,2},{5,3},{6,0},{7,1},{8,14},{9,15},{10,... | collective-permute-start | bytes 491528 | tf_op jit(solution)/shard_map/ppermute | solution.py:516
  100.1 22.3 %collective-permute-start.18 = (bf16[512,160]{1,0:T(8,128)(2,1)}, bf16[512,160]{1,0:T(8,128)(2,1)S(1)}, u32[]{:S(2)}, u32[]{:S(2)}) collective-permute-start(bf16[512,160]{1,0:T(8,128)(2,1)} %fusion.26), channel_id=1, source_target_pairs={{0,4},{1,5},{2,6},{3,7},{4,0},{5,1},{6,2},{7,3},{8,12},{9,13},{10,... | collective-permute-start | bytes 491528 | tf_op jit(solution)/shard_map/ppermute | solution.py:516
  100.6 21.8 %collective-permute-start.17 = (bf16[512,160]{1,0:T(8,128)(2,1)}, bf16[512,160]{1,0:T(8,128)(2,1)}, u32[]{:S(2)}, u32[]{:S(2)}) collective-permute-start(bf16[512,160]{1,0:T(8,128)(2,1)} %fusion.26), channel_id=1, source_target_pairs={{0,2},{1,3},{2,0},{3,1},{4,6},{5,7},{6,4},{7,5},{8,10},{9,11},{10,... | collective-permute-start | bytes 491528 | tf_op jit(solution)/shard_map/ppermute | solution.py:516
  122.4 290.9 %all-gather.13.cloned.1.call-start = ((), (), s32[]{:S(2)}) async-start(), calls=%async_computation.2 | async-start | bytes 14155776 | tf_op jit(solution)/shard_map/all_gather | solution.py:721
  145.4 361.0 %all-gather.15.cloned.1.call-start = ((), (), s32[]{:S(2)}) async-start(), calls=%async_computation.3 | async-start | bytes 14155776 | tf_op jit(solution)/shard_map/all_gather | solution.py:738
  170.2 61.8 %collective-permute-start.22 = (bf16[1024,1024]{1,0:T(8,128)(2,1)}, bf16[1024,1024]{1,0:T(8,128)(2,1)}, u32[]{:S(2)}, u32[]{:S(2)}) collective-permute-start(bf16[1024,1024]{1,0:T(8,128)(2,1)} %shard_map.242.refs_4_), channel_id=1, source_target_pairs={{8,0},{16,8},{24,16},{9,1},{17,9},{25,17},{10,2},{18,10},{26,18},{... | collective-permute-start | bytes 6291464 | tf_op jit(solution)/shard_map/ppermute | solution.py:576
  171.5 60.5 %collective-permute-start.21 = (bf16[1024,1024]{1,0:T(8,128)(2,1)}, bf16[1024,1024]{1,0:T(8,128)(2,1)}, u32[]{:S(2)}, u32[]{:S(2)}) collective-permute-start(bf16[1024,1024]{1,0:T(8,128)(2,1)} %shard_map.242.refs_4_), channel_id=1, source_target_pairs={{0,8},{8,16},{16,24},{1,9},{9,17},{17,25},{2,10},{10,18},{18,26},{... | collective-permute-start | bytes 6291464 | tf_op jit(solution)/shard_map/ppermute | solution.py:575
  235.0 49.7 %collective-permute-start.28 = (bf16[1024,1024]{1,0:T(8,128)(2,1)}, bf16[1024,1024]{1,0:T(8,128)(2,1)}, u32[]{:S(2)}, u32[]{:S(2)}) collective-permute-start(bf16[1024,1024]{1,0:T(8,128)(2,1)} %collective-permute-done.21), channel_id=1, source_target_pairs={{0,8},{8,16},{16,24},{1,9},{9,17},{17,25},{2,10},{10,18},{18,26},{... | collective-permute-start | bytes 6291464 | tf_op jit(solution)/shard_map/ppermute | solution.py:575
  240.1 49.9 %collective-permute-start.29 = (bf16[1024,1024]{1,0:T(8,128)(2,1)}, bf16[1024,1024]{1,0:T(8,128)(2,1)}, u32[]{:S(2)}, u32[]{:S(2)}) collective-permute-start(bf16[1024,1024]{1,0:T(8,128)(2,1)} %collective-permute-done.22), channel_id=1, source_target_pairs={{8,0},{16,8},{24,16},{9,1},{17,9},{25,17},{10,2},{18,10},{26,18},{... | collective-permute-start | bytes 6291464 | tf_op jit(solution)/shard_map/ppermute | solution.py:576
  244.5 23.7 %collective-permute-start.24 = (bf16[512,160]{1,0:T(8,128)(2,1)S(1)}, bf16[512,160]{1,0:T(8,128)(2,1)S(1)}, u32[]{:S(2)}, u32[]{:S(2)}) collective-permute-start(bf16[512,160]{1,0:T(8,128)(2,1)S(1)} %fusion.27), channel_id=1, source_target_pairs={{0,2},{1,3},{2,0},{3,1},{4,6},{5,7},{6,4},{7,5},{8,10},{9,11},{10,... | collective-permute-start | bytes 491528 | tf_op jit(solution)/shard_map/ppermute | solution.py:516
  303.7 78.3 %collective-permute-start.34 = (bf16[1024,1024]{1,0:T(8,128)(2,1)}, bf16[1024,1024]{1,0:T(8,128)(2,1)}, u32[]{:S(2)}, u32[]{:S(2)}) collective-permute-start(bf16[1024,1024]{1,0:T(8,128)(2,1)} %collective-permute-done.28), channel_id=1, source_target_pairs={{0,8},{8,16},{16,24},{1,9},{9,17},{17,25},{2,10},{10,18},{18,26},{... | collective-permute-start | bytes 6291464 | tf_op jit(solution)/shard_map/ppermute | solution.py:575
  306.9 75.1 %collective-permute-start.35 = (bf16[1024,1024]{1,0:T(8,128)(2,1)}, bf16[1024,1024]{1,0:T(8,128)(2,1)}, u32[]{:S(2)}, u32[]{:S(2)}) collective-permute-start(bf16[1024,1024]{1,0:T(8,128)(2,1)} %collective-permute-done.29), channel_id=1, source_target_pairs={{8,0},{16,8},{24,16},{9,1},{17,9},{25,17},{10,2},{18,10},{26,18},{... | collective-permute-start | bytes 6291464 | tf_op jit(solution)/shard_map/ppermute | solution.py:576
  314.0 29.1 %collective-permute-start.33 = (bf16[128,2048]{1,0:T(8,128)(2,1)}, bf16[128,2048]{1,0:T(8,128)(2,1)}, u32[]{:S(2)}, u32[]{:S(2)}) collective-permute-start(bf16[128,2048]{1,0:T(8,128)(2,1)} %get-tuple-element.251), channel_id=1, source_target_pairs={{0,6},{1,7},{2,4},{3,5},{4,2},{5,3},{6,0},{7,1},{8,14},{9,15},{10,... | collective-permute-start | bytes 1572872 | tf_op jit(solution)/shard_map/ppermute | solution.py:516
  336.2 45.8 %collective-permute-start.37 = (bf16[1024,512]{1,0:T(8,128)(2,1)}, bf16[1024,512]{1,0:T(8,128)(2,1)S(1)}, u32[]{:S(2)}, u32[]{:S(2)}) collective-permute-start(bf16[1024,512]{1,0:T(8,128)(2,1)} %shard_map.246.refs_3_), channel_id=1, source_target_pairs={{8,0},{16,8},{24,16},{9,1},{17,9},{25,17},{10,2},{18,10},{26,18},{... | collective-permute-start | bytes 3145736 | tf_op jit(solution)/shard_map/ppermute | solution.py:576
  337.5 44.5 %collective-permute-start.36 = (bf16[1024,512]{1,0:T(8,128)(2,1)}, bf16[1024,512]{1,0:T(8,128)(2,1)S(1)}, u32[]{:S(2)}, u32[]{:S(2)}) collective-permute-start(bf16[1024,512]{1,0:T(8,128)(2,1)} %shard_map.246.refs_3_), channel_id=1, source_target_pairs={{0,8},{8,16},{16,24},{1,9},{9,17},{17,25},{2,10},{10,18},{18,26},{... | collective-permute-start | bytes 3145736 | tf_op jit(solution)/shard_map/ppermute | solution.py:575
  343.1 25.7 %collective-permute-start.32 = (bf16[128,2048]{1,0:T(8,128)(2,1)}, bf16[128,2048]{1,0:T(8,128)(2,1)S(1)}, u32[]{:S(2)}, u32[]{:S(2)}) collective-permute-start(bf16[128,2048]{1,0:T(8,128)(2,1)} %get-tuple-element.252), channel_id=1, source_target_pairs={{0,4},{1,5},{2,6},{3,7},{4,0},{5,1},{6,2},{7,3},{8,12},{9,13},{10,... | collective-permute-start | bytes 1572872 | tf_op jit(solution)/shard_map/ppermute | solution.py:516
  394.0 49.2 %collective-permute-start.49 = (bf16[1024,512]{1,0:T(8,128)(2,1)S(1)}, bf16[1024,512]{1,0:T(8,128)(2,1)}, u32[]{:S(2)}, u32[]{:S(2)}) collective-permute-start(bf16[1024,512]{1,0:T(8,128)(2,1)S(1)} %collective-permute-done.36), channel_id=1, source_target_pairs={{0,8},{8,16},{16,24},{1,9},{9,17},{17,25},{2,10},{10,18},{18,26},{... | collective-permute-start | bytes 3145736 | tf_op jit(solution)/shard_map/ppermute | solution.py:575
  398.0 45.2 %collective-permute-start.50 = (bf16[1024,512]{1,0:T(8,128)(2,1)S(1)}, bf16[1024,512]{1,0:T(8,128)(2,1)}, u32[]{:S(2)}, u32[]{:S(2)}) collective-permute-start(bf16[1024,512]{1,0:T(8,128)(2,1)S(1)} %collective-permute-done.37), channel_id=1, source_target_pairs={{8,0},{16,8},{24,16},{9,1},{17,9},{25,17},{10,2},{18,10},{26,18},{... | collective-permute-start | bytes 3145736 | tf_op jit(solution)/shard_map/ppermute | solution.py:576
  409.8 28.1 %collective-permute-start.43 = (bf16[128,2048]{1,0:T(8,128)(2,1)}, bf16[128,2048]{1,0:T(8,128)(2,1)}, u32[]{:S(2)}, u32[]{:S(2)}) collective-permute-start(bf16[128,2048]{1,0:T(8,128)(2,1)} %get-tuple-element.248), channel_id=1, source_target_pairs={{0,6},{1,7},{2,4},{3,5},{4,2},{5,3},{6,0},{7,1},{8,14},{9,15},{10,... | collective-permute-start | bytes 1572872 | tf_op jit(solution)/shard_map/ppermute | solution.py:516
  411.3 26.7 %collective-permute-start.42 = (bf16[128,2048]{1,0:T(8,128)(2,1)}, bf16[128,2048]{1,0:T(8,128)(2,1)}, u32[]{:S(2)}, u32[]{:S(2)}) collective-permute-start(bf16[128,2048]{1,0:T(8,128)(2,1)} %get-tuple-element.249), channel_id=1, source_target_pairs={{0,4},{1,5},{2,6},{3,7},{4,0},{5,1},{6,2},{7,3},{8,12},{9,13},{10,... | collective-permute-start | bytes 1572872 | tf_op jit(solution)/shard_map/ppermute | solution.py:516
  411.8 26.1 %collective-permute-start.41 = (bf16[128,2048]{1,0:T(8,128)(2,1)}, bf16[128,2048]{1,0:T(8,128)(2,1)}, u32[]{:S(2)}, u32[]{:S(2)}) collective-permute-start(bf16[128,2048]{1,0:T(8,128)(2,1)} %get-tuple-element.250), channel_id=1, source_target_pairs={{0,2},{1,3},{2,0},{3,1},{4,6},{5,7},{6,4},{7,5},{8,10},{9,11},{10,... | collective-permute-start | bytes 1572872 | tf_op jit(solution)/shard_map/ppermute | solution.py:516
  443.2 87.1 %collective-permute-start.51 = (bf16[1024,512]{1,0:T(8,128)(2,1)}, bf16[1024,512]{1,0:T(8,128)(2,1)}, u32[]{:S(2)}, u32[]{:S(2)}) collective-permute-start(bf16[1024,512]{1,0:T(8,128)(2,1)} %collective-permute-done.49), channel_id=1, source_target_pairs={{0,8},{8,16},{16,24},{1,9},{9,17},{17,25},{2,10},{10,18},{18,26},{... | collective-permute-start | bytes 3145736 | tf_op jit(solution)/shard_map/ppermute | solution.py:575
  451.5 78.8 %collective-permute-start.52 = (bf16[1024,512]{1,0:T(8,128)(2,1)}, bf16[1024,512]{1,0:T(8,128)(2,1)}, u32[]{:S(2)}, u32[]{:S(2)}) collective-permute-start(bf16[1024,512]{1,0:T(8,128)(2,1)} %collective-permute-done.50), channel_id=1, source_target_pairs={{8,0},{16,8},{24,16},{9,1},{17,9},{25,17},{10,2},{18,10},{26,18},{... | collective-permute-start | bytes 3145736 | tf_op jit(solution)/shard_map/ppermute | solution.py:576
  453.1 34.0 %collective-permute-start.53 = (bf16[1244,128]{1,0:T(8,128)(2,1)S(1)}, bf16[1244,128]{1,0:T(8,128)(2,1)S(1)}, u32[]{:S(2)}, u32[]{:S(2)}) collective-permute-start(bf16[1244,128]{1,0:T(8,128)(2,1)S(1)} %convert_element_type.211), channel_id=1, source_target_pairs={{0,8},{8,0},{16,24},{24,16},{1,9},{9,1},{17,25},{25,17},{2,10},{10... | collective-permute-start | bytes 955400 | tf_op jit(solution)/shard_map/ppermute | solution.py:609
  455.9 21.7 %collective-permute-start.46 = (f32[2048]{0:T(1024)S(1)}, f32[2048]{0:T(1024)S(1)}, u32[]{:S(2)}, u32[]{:S(2)}) collective-permute-start(f32[2048]{0:T(1024)S(1)} %add.277), channel_id=1, source_target_pairs={{0,4},{1,5},{2,6},{3,7},{4,0},{5,1},{6,2},{7,3},{8,12},{9,13},{10,... | collective-permute-start | bytes 24584 | tf_op jit(solution)/shard_map/ppermute | solution.py:516
  (61 other events, 649.6 us)
Sparse Core Ops, SparseCore 0:
  95.1 47.3 all-gather.8
  144.1 50.3 all-gather.10
  196.4 89.8 all-gather.12
  288.0 94.5 all-gather.14

commit v2 on v1

--- a/solution.py
+++ b/solution.py
@@ -31,17 +31,12 @@
 def mt(a, b):
     return lax.dot_general(a, b, (((1,), (1,)), ((), ())), preferred_element_type=jnp.float32)
 
-WINDOW = 512
-PEAK = 1.1e15
-
-
-def taking(microseconds, moved=0):
-    return pl.CostEstimate(flops=int(microseconds * 1e-6 * PEAK), bytes_accessed=int(moved), transcendentals=0)
-
+WINDOW = 384
+ALIGN = 16
 
 def first_window(bounds, row, m, span, window):
     first, last = bounds[row, m], bounds[row, m + 1]
-    base = lax.div(first, 128) * 128
+    base = lax.div(first, ALIGN) * ALIGN
     count = jnp.where(last > first, lax.div(last - base + window - 1, window), 0)
     return first, last, base, count
 
@@ -51,22 +46,24 @@
     return jnp.where((here >= low) & (here < high), 1.0, 0.0).astype(jnp.bfloat16)
 
 
-def grouped_sum(bounds, slots, m, span, window, left_at, right_at, acc, start):
+def grouped_sum(bounds, slots, m, span, window, left_at, right_at, acc, starts):
     lefts, rights, more = [], [], []
     for s in range(slots):
         first, last, base, count = first_window(bounds, s, m, span, window)
-        at = pl.multiple_of(jnp.minimum(base, span - window), 128)
+        at = pl.multiple_of(jnp.minimum(base, span - window), ALIGN)
         keep = inside(at, first, last, window)
         lefts.append(left_at(s, at, keep))
         rights.append(right_at(s, at, keep))
         more.append((last, base, count))
     total = mm(jnp.concatenate(lefts, 1), jnp.concatenate(rights, 0))
-    acc[...] = total if start is None else total + start[0]
+    if starts:
+        total = total + jnp.concatenate([start[0] for start in starts], 1)
+    acc[...] = total
     for s, (last, base, count) in enumerate(more):
 
         def one(i, _):
             want = base + i * window
-            at = pl.multiple_of(jnp.minimum(want, span - window), 128)
+            at = pl.multiple_of(jnp.minimum(want, span - window), ALIGN)
             keep = inside(at, want, last, window)
             acc[...] += mm(left_at(s, at, keep), right_at(s, at, keep))
             return 0
@@ -74,37 +71,54 @@
         lax.fori_loop(1, count, one, 0)
 
 
-def grad_in_kernel(bounds, *refs, slots, begun, halves):
-    rows, d, rest = refs[:slots], refs[slots : 2 * slots], refs[2 * slots : -2]
-    out, acc = refs[-2:]
+def choose(picks, choices, refs, held):
+    @pl.when((pl.program_id(0) == 0) & (pl.program_id(1) == 0))
+    def _():
+        at = 0
+        for i, count in enumerate(choices):
+            for j in range(count):
+
+                @pl.when(picks[i] == j)
+                def _(ref=refs[at + j], i=i):
+                    held[i] = ref[...]
+
+            at += count
+
+
+def grad_in_kernel(bounds, picks, *refs, slots, choices, begun, halves):
+    total = sum(choices)
+    rows, d, starts = refs[:slots], refs[slots : slots + total], refs[slots + total : -3]
+    out, acc, held = refs[-3:]
+    parts = len(choices) // slots
     wide, _, unit, bf = rows[0].shape
     span, chan = d[0].shape
     window = min(WINDOW, span)
+    choose(picks, choices, d, held)
 
     def left_at(s, at, keep):
-        block = rows[s][pl.ds(lax.div(at, unit), window // unit), 0]
-        return jnp.transpose(block.reshape(window, bf))
+        return jnp.transpose(rows[s].reshape(span, bf)[pl.ds(at, window), :])
 
     def right_at(s, at, keep):
-        return d[s][pl.ds(at, window), :] * jnp.concatenate([keep] * (chan // 128), 1)
-
-    grouped_sum(bounds, slots, pl.program_id(1), span, window, left_at, right_at, acc, rest[0] if begun else None)
+        tiled = jnp.concatenate([keep] * (chan // 128), 1)
+        return jnp.concatenate([held[s * parts + p, pl.ds(at, window), :] * tiled for p in range(parts)], 1)
+
+    grouped_sum(bounds, slots, pl.program_id(1), span, window, left_at, right_at, acc, starts)
     if halves:
-        other = rest[-1]
-        lanes = chan // 128
-        for j in range(lanes):
-            out[0, pl.ds(j * 2, bf, stride=2 * lanes), :] = acc[:, j * 128 : (j + 1) * 128]
-            out[0, pl.ds(j * 2 + 1, bf, stride=2 * lanes), :] = other[0, :, j * 128 : (j + 1) * 128]
+        tiles = chan // 128
+        for h in range(2):
+            for j in range(tiles):
+                at = h * chan + j * 128
+                out[0, pl.ds(j * 2 + h, bf, stride=2 * tiles), :] = acc[:, at : at + 128]
     else:
         out[0] = acc[...]
 
 
 def slot_spec(array, index, bf):
-    return pl.BlockSpec((array.shape[0], 1, array.shape[2], bf), lambda f, m, b: (0, index, 0, f))
+    return pl.BlockSpec((array.shape[0], 1, array.shape[2], bf), lambda f, m, b, p: (0, index, 0, f))
 
 
 def side_spec(array, chan, side):
-    return pl.BlockSpec((array.shape[0], chan), lambda f, m, b: (0, side))
+    return pl.BlockSpec((array.shape[0], chan), lambda f, m, b, p: (0, side))
 
 
 def feature_block(rows):
@@ -112,69 +126,80 @@
     return max(128, min(1024, (1 << 20) // (wide * unit)))
 
 
-def grad_in(bounds, rows, d, mods, chan, side, start=None, other=None):
+def grad_in(bounds, rows, d, mods, chan, starts=()):
     width = rows[0][0].shape[3]
     bf = feature_block(rows)
-    span, slots = d[0].shape[0], len(d)
-    plain = pl.BlockSpec((1, bf, chan), lambda f, m, b: (m, f, 0))
-    ins = [slot_spec(array, index, bf) for array, index in rows] + [side_spec(x, chan, side) for x in d]
-    args = [array for array, _ in rows] + list(d)
-    for extra in (start, other):
-        if extra is not None:
-            ins.append(plain)
-            args.append(extra)
-    if other is not None:
+    slots, parts = len(d), len(d[0])
+    flat = [part for entry in d for part in entry]
+    choices = tuple(len(arrays) for arrays, _, _ in flat)
+    picks = jnp.stack([jnp.asarray(pick, jnp.int32) for _, pick, _ in flat])
+    span = flat[0][0][0].shape[0]
+    plain = pl.BlockSpec((1, bf, chan), lambda f, m, b, p: (m, f, 0))
+    ins = [slot_spec(array, index, bf) for array, index in rows]
+    args = [array for array, _ in rows]
+    for arrays, _, side in flat:
+        for x in arrays:
+            ins.append(side_spec(x, chan, side))
+            args.append(x)
+    for start in starts:
+        ins.append(plain)
+        args.append(start)
+    if parts == 2:
         out_shape = jax.ShapeDtypeStruct((mods, width * 2 * chan // 128, 128), jnp.float32)
-        out_spec = pl.BlockSpec((1, bf * 2 * chan // 128, 128), lambda f, m, b: (m, f, 0))
+        out_spec = pl.BlockSpec((1, bf * 2 * chan // 128, 128), lambda f, m, b, p: (m, f, 0))
     else:
         out_shape = jax.ShapeDtypeStruct((mods, width, chan), jnp.float32)
         out_spec = plain
     return pl.pallas_call(
-        functools.partial(grad_in_kernel, slots=slots, begun=start is not None, halves=other is not None),
+        functools.partial(grad_in_kernel, slots=slots, choices=choices, begun=bool(starts), halves=parts == 2),
         grid_spec=pltpu.PrefetchScalarGridSpec(
-            num_scalar_prefetch=1,
+            num_scalar_prefetch=2,
             grid=(width // bf, mods),
             in_specs=ins,
             out_specs=out_spec,
-            scratch_shapes=[pltpu.VMEM((bf, chan), jnp.float32)],
+            scratch_shapes=[pltpu.VMEM((bf, parts * chan), jnp.float32), pltpu.VMEM((len(flat), span, chan), jnp.bfloat16)],
         ),
         out_shape=out_shape,
-        compiler_params=pltpu.CompilerParams(vmem_limit_bytes=56 << 20),
-        cost_estimate=taking(6 * slots + 6),
-    )(bounds, *args)
-
-
-def grad_out_kernel(bounds, *refs, slots):
-    cot, gated, out = refs[:slots], refs[slots : 2 * slots], refs[-1]
+        compiler_params=pltpu.CompilerParams(vmem_limit_bytes=58 << 20),
+    )(bounds, picks, *args)
+
+
+def grad_out_kernel(bounds, picks, *refs, slots, choices):
+    cot, gated, out, held = refs[:slots], refs[slots:-2], refs[-2], refs[-1]
     wide, _, unit, bf = cot[0].shape
     span, chan = gated[0].shape
     window = min(WINDOW, span)
+    choose(picks, choices, gated, held)
 
     def left_at(s, at, keep):
-        return jnp.transpose(gated[s][pl.ds(at, window), :] * jnp.concatenate([keep] * (chan // 128), 1))
+        return jnp.transpose(held[s, pl.ds(at, window), :] * jnp.concatenate([keep] * (chan // 128), 1))
 
     def right_at(s, at, keep):
-        return cot[s][pl.ds(lax.div(at, unit), window // unit), 0].reshape(window, bf)
-
-    grouped_sum(bounds, slots, pl.program_id(1), span, window, left_at, right_at, out.at[0], None)
-
-
-def grad_out(bounds, cot, gated, mods, chan, side):
+        return cot[s].reshape(span, bf)[pl.ds(at, window), :]
+
+    grouped_sum(bounds, slots, pl.program_id(1), span, window, left_at, right_at, out.at[0], ())
+
+
+def grad_out(bounds, cot, gated, mods, chan):
     width = cot[0][0].shape[3]
     bf = feature_block(cot)
     slots = len(gated)
+    choices = tuple(len(arrays) for arrays, _, _ in gated)
+    picks = jnp.stack([jnp.asarray(pick, jnp.int32) for _, pick, _ in gated])
+    span = gated[0][0][0].shape[0]
     return pl.pallas_call(
-        functools.partial(grad_out_kernel, slots=slots),
+        functools.partial(grad_out_kernel, slots=slots, choices=choices),
         grid_spec=pltpu.PrefetchScalarGridSpec(
-            num_scalar_prefetch=1,
+            num_scalar_prefetch=2,
             grid=(width // bf, mods),
-            in_specs=[slot_spec(array, index, bf) for array, index in cot] + [side_spec(x, chan, side) for x in gated],
-            out_specs=pl.BlockSpec((1, chan, bf), lambda f, m, b: (m, 0, f)),
+            in_specs=[slot_spec(array, index, bf) for array, index in cot]
+            + [side_spec(x, chan, side) for arrays, _, side in gated for x in arrays],
+            out_specs=pl.BlockSpec((1, chan, bf), lambda f, m, b, p: (m, 0, f)),
+            scratch_shapes=[pltpu.VMEM((slots, span, chan), jnp.bfloat16)],
         ),
         out_shape=jax.ShapeDtypeStruct((mods, chan, width), jnp.float32),
-        compiler_params=pltpu.CompilerParams(vmem_limit_bytes=56 << 20),
-        cost_estimate=taking(6 * slots + 4),
-    )(bounds, *[array for array, _ in cot], *gated)
+        compiler_params=pltpu.CompilerParams(vmem_limit_bytes=58 << 20),
+    )(bounds, picks, *[array for array, _ in cot], *[x for arrays, _, _ in gated for x in arrays])
 
 
 def fwd_kernel(lr, dtw, dtb, cf, ct, u, alog, skip, gate, dgated, gated, dy, dgate, starts, h_s, dt_s, du_s, y_s, bd_s, hb_s):
@@ -229,7 +254,6 @@
         out_shape=[jax.ShapeDtypeStruct((rows, chan), jnp.bfloat16)] * 3 + [jax.ShapeDtypeStruct((steps, n, chan), jnp.float32)],
         scratch_shapes=[pltpu.VMEM((n, chan), jnp.float32)] + [pltpu.VMEM((span, chan), jnp.float32)] * 3 + [pltpu.VMEM((span, TILE * n), jnp.bfloat16), pltpu.VMEM((span * n, chan), jnp.bfloat16)],
         compiler_params=pltpu.CompilerParams(vmem_limit_bytes=32 << 20),
-        cost_estimate=taking(13 * rows / 1024),
     )(lr, dtw, dtb, cf, ct, u, alog, skip, gate, dgated)
 
 def bwd_kernel(lr, dtw, dtb, cf, ct, u, alog, skip, dy, starts, dpre, dval, dlow, din, dout, galog, gskip, gbias, gdtw, lam_s, dt_s, du_s, dyf_s, hp_s, st_s, th_s, bd_s, hb_s, gb_s):
@@ -330,7 +354,6 @@
         out_shape=outs,
         scratch_shapes=[pltpu.VMEM((n, chan), jnp.float32)] + [pltpu.VMEM((span, chan), jnp.float32)] * 3 + [pltpu.VMEM((span, n, chan), jnp.float32)] + [pltpu.VMEM((span, chan), jnp.float32)] * 2 + [pltpu.VMEM((span, TILE * n), jnp.bfloat16)] + [pltpu.VMEM((span * n, chan), jnp.bfloat16)] * 2,
         compiler_params=pltpu.CompilerParams(vmem_limit_bytes=32 << 20),
-        cost_estimate=taking(36 * rows / 1024),
     )(lr, dtw, dtb, cf, ct, u, alog, skip, dy, starts)
 
 
@@ -356,7 +379,9 @@
         tail[...] = jnp.zeros_like(tail)
 
     taps = cw.shape[0]
-    ax, az = masked_sum(rows[...], masks[...], (w.at[0], w.at[1]), mm)
+    unit = masks.shape[0] // rows.shape[0]
+    x = jnp.concatenate([rows[k, :unit] for k in range(rows.shape[0])], 0)
+    ax, az = masked_sum(x, masks[...], (w.at[0], w.at[1]), mm)
     before = tail[...]
     pre = cb[...]
     for k in range(taps):
@@ -375,19 +400,20 @@
 
 
 def enter(rows, masks, w, cw, cb, xp, block):
-    span, width = rows.shape
+    wide, padded, width = rows.shape
+    span = masks.shape[0]
     chan, small = xp.shape
     tok = lambda w: pl.BlockSpec((block, w), lambda i: (i, 0))
     f = lambda w, t=jnp.float32: jax.ShapeDtypeStruct((span, w), t)
     return pl.pallas_call(
         enter_kernel,
         grid=(span // block,),
-        in_specs=[tok(width), tok(masks.shape[1])] + [whole_spec(a) for a in (w, cw, cb, xp)],
+        in_specs=[pl.BlockSpec((block * wide // span, padded, width), lambda i: (i, 0, 0)), tok(masks.shape[1])]
+        + [whole_spec(a) for a in (w, cw, cb, xp)],
         out_specs=[tok(chan)] * 4 + [tok(small)],
         out_shape=[f(chan), f(chan), f(chan), f(chan, jnp.bfloat16), f(small)],
         scratch_shapes=[pltpu.VMEM((8, chan), jnp.float32)],
         compiler_params=pltpu.CompilerParams(vmem_limit_bytes=56 << 20),
-        cost_estimate=taking(20),
     )(rows, masks, w, cw, cb, xp)
 
 
@@ -411,7 +437,6 @@
         out_specs=tok(width),
         out_shape=jax.ShapeDtypeStruct((span, width), dtype),
         compiler_params=pltpu.CompilerParams(vmem_limit_bytes=56 << 20),
-        cost_estimate=taking(20 * w.size / 6e6),
     )(masks, *inputs, w)
 
 
@@ -464,38 +489,69 @@
         out_shape=outs,
         scratch_shapes=[pltpu.VMEM((8, chan), jnp.float32)],
         compiler_params=pltpu.CompilerParams(vmem_limit_bytes=56 << 20),
-        cost_estimate=taking(8),
     )(dval, dsmall, xp, pre_act, conv_in, conv_in, conv_out, cw)
 
 
-def sort_kernel(start, rank, *refs):
+def sort_kernel(start, rank, *refs, pieces):
     inputs, out = refs[:-1], refs[-1]
-    rows, span = out.shape[0], inputs[0].shape[0]
+    rows = out.shape[0]
+    span = rank.shape[1]
     first = start[0] + pl.program_id(0) * rows
     here = lax.broadcasted_iota(jnp.int32, (rows, span), 0) + first
     choose = jnp.where(rank[...] == here, 1.0, 0.0).astype(jnp.bfloat16)
     at = 0
-    for x in inputs:
-        out[:, at : at + x.shape[1]] = mm(choose, x[...]).astype(out.dtype)
+    for k in range(0, len(inputs), pieces):
+        group = inputs[k : k + pieces]
+        x = group[0][...] if pieces == 1 else jnp.concatenate([g[: span // pieces] for g in group], 0)
+        out[:, at : at + x.shape[1]] = mm(choose, x).astype(out.dtype)
         at += x.shape[1]
 
 
-def sort_rows(start, rank, inputs, rows, block):
-    span = inputs[0].shape[0]
-    width = sum(x.shape[1] for x in inputs)
+def sort_rows(start, rank, inputs, rows, block, pieces=1):
+    span = rank.shape[1]
+    width = sum(x.shape[1] for x in inputs) // pieces
     return pl.pallas_call(
-        sort_kernel,
+        functools.partial(sort_kernel, pieces=pieces),
         grid_spec=pltpu.PrefetchScalarGridSpec(
             num_scalar_prefetch=1,
             grid=(rows // block,),
             in_specs=[pl.BlockSpec((1, span), lambda i, s: (0, 0))]
-            + [pl.BlockSpec((span, x.shape[1]), lambda i, s: (0, 0)) for x in inputs],
+            + [pl.BlockSpec(x.shape, lambda i, s: (0, 0)) for x in inputs],
             out_specs=pl.BlockSpec((block, width), lambda i, s: (i, 0)),
         ),
         out_shape=jax.ShapeDtypeStruct((rows, width), inputs[0].dtype),
-        compiler_params=pltpu.CompilerParams(vmem_limit_bytes=56 << 20),
-        cost_estimate=taking(2 + 2e-9 * rows * span * width),
+        compiler_params=pltpu.CompilerParams(vmem_limit_bytes=40 << 20),
     )(start, rank, *inputs)
+
+
+def blocks_kernel(place, masks, *refs, pairs):
+    blocks, w, out = refs[:-2], refs[-2], refs[-1]
+    unit = blocks[0].shape[0]
+    core, chip = place[0] % 2, place[0] // 2
+    for k in range(pairs):
+        here = pl.multiple_of((chip ^ k) * 2 * unit, 2 * unit)
+        low = pl.ds(pl.multiple_of(here + core * unit, unit), unit)
+        high = pl.ds(pl.multiple_of(here + (1 - core) * unit, unit), unit)
+        x = jnp.concatenate([blocks[2 * k][...], blocks[2 * k + 1][...]], 0)
+        marks = jnp.concatenate([masks[low, :], masks[high, :]], 0)
+        (total,) = masked_sum(x, marks, (w,), mt)
+        out[low, :] = total[:unit]
+        out[high, :] = total[unit:]
+
+
+def apply_blocks(place, masks, blocks, w):
+    span, chan = masks.shape[0], w.shape[1]
+    return pl.pallas_call(
+        functools.partial(blocks_kernel, pairs=len(blocks) // 2),
+        grid_spec=pltpu.PrefetchScalarGridSpec(
+            num_scalar_prefetch=1,
+            grid=(1,),
+            in_specs=[pl.BlockSpec(a.shape, lambda i, s, n=a.ndim: (0,) * n) for a in (masks, *blocks, w)],
+            out_specs=pl.BlockSpec((span, chan), lambda i, s: (0, 0)),
+        ),
+        out_shape=jax.ShapeDtypeStruct((span, chan), jnp.float32),
+        compiler_params=pltpu.CompilerParams(vmem_limit_bytes=40 << 20),
+    )(place, masks, *blocks, w)
 
 
 def contract(left, right, left_dim, right_dim):
@@ -516,34 +572,47 @@
     return lax.ppermute(array, "wide", [(i, i ^ k) for i in range(lax.axis_size("wide"))])
 
 
-def gather_wide(shard, early, late):
+def begin_gather(shard):
     if lax.axis_size("wide") != 8:
-        return lax.all_gather(shard, "wide", axis=0), early(), late()
+        return (shard,)
+    return shard, cross(shard, 2), cross(shard, 4), cross(shard, 1)
+
+
+def end_gather(begun, work):
+    if lax.axis_size("wide") != 8:
+        whole = lax.all_gather(begun[0], "wide", axis=0)
+        return [whole[k] for k in range(whole.shape[0])], work()
+    shard, by_x, by_y, pair = begun
     half = shard.shape[0] // 2
-    by_x, by_y, pair = cross(shard, 2), cross(shard, 4), cross(shard, 1)
-    early, by_x, by_y, pair = lax.optimization_barrier((early(), by_x, by_y, pair))
     far = (cross(by_y[:half], 2), cross(by_x[half:], 4))
     pair_x, pair_y = cross(by_x, 1), cross(by_y, 1)
-    late, *far = lax.optimization_barrier((late(),) + far)
+    beside, *far = lax.optimization_barrier((work(),) + far)
     far = jnp.concatenate(far, 0)
-    blocks = [shard, pair, by_x, pair_x, by_y, pair_y, far, cross(far, 1)]
+    return [shard, pair, by_x, pair_x, by_y, pair_y, far, cross(far, 1)], beside
+
+
+def assemble(blocks):
+    if lax.axis_size("wide") != 8:
+        return jnp.stack(blocks)
     here = lax.axis_index("wide")
-    whole = jnp.zeros((8,) + shard.shape, shard.dtype)
+    whole = jnp.zeros((8,) + blocks[0].shape, blocks[0].dtype)
     for k, block in enumerate(blocks):
         whole = lax.dynamic_update_index_in_dim(whole, block, here ^ k, 0)
-    return whole, early, late
-
-
-def sum_wide(part, work):
+    return whole
+
+
+def sum_wide(part, held, work, ordered=True):
     if lax.axis_size("wide") != 8:
-        return lax.psum(part, "wide"), work()
+        return lax.psum(part, "wide"), work(held)
     half = part.shape[0] // 2
     core = lax.axis_index("wide") % 2
     mine = lax.dynamic_slice_in_dim(part, core * half, half, 0)
     other = lax.dynamic_slice_in_dim(part, (1 - core) * half, half, 0)
     mine = mine + cross(other, 1)
+    if ordered:
+        mine, held = lax.optimization_barrier((mine, held))
     sent = mine.astype(jnp.bfloat16)
-    beside, *came = lax.optimization_barrier((work(),) + tuple(cross(sent, k) for k in (2, 4, 6)))
+    beside, *came = lax.optimization_barrier((work(held),) + tuple(cross(sent, k) for k in (2, 4, 6)))
     total = mine
     for block in came:
         total = total + block.astype(jnp.float32)
@@ -551,19 +620,8 @@
     return jnp.where(core == 0, jnp.concatenate([total, other], 0), jnp.concatenate([other, total], 0)), beside
 
 
-def scatter_wide(part, work):
-    if lax.axis_size("wide") != 8:
-        return lax.psum_scatter(part, "wide", scatter_dimension=0, tiled=True).astype(jnp.float32), work()
-    here = lax.axis_index("wide")
-    core, chip = here % 2, here // 2
-    view = part.reshape(4, 2, part.shape[0] // 8, part.shape[1])
-    mine = pick(view, core, 1).astype(jnp.float32) + cross(pick(view, 1 - core, 1), 1).astype(jnp.float32)
-    came = tuple(cross(pick(mine, chip ^ (k // 2)).astype(jnp.bfloat16), k) for k in (2, 4, 6))
-    beside, *came = lax.optimization_barrier((work(),) + came)
-    total = pick(mine, chip)
-    for block in came:
-        total = total + block.astype(jnp.float32)
-    return total, beside
+def scatter_wide(part):
+    return lax.psum_scatter(part, "wide", scatter_dimension=0, tiled=True).astype(jnp.float32)
 
 
 def after(value, *first):
@@ -577,21 +635,22 @@
     )
 
 
-def arrange_near(hops):
-    return jnp.where(lax.axis_index("row") == 0, hops[0][1], hops[0][0])
-
-
-def arrange_middle(hops):
-    return hops[1][0] + hops[1][1]
-
-
-def arrange_last(hops):
+def near_slot(hops, side):
     here = lax.axis_index("row")
-    return jnp.where(here == 3, hops[2][0], jnp.where(here == 0, hops[2][1], hops[0][1]))
-
-
-def arrange(block, hops):
-    return [block, arrange_near(hops), arrange_middle(hops), arrange_last(hops)]
+    return (hops[0][0], hops[0][1]), jnp.where(here == 0, 1, 0), side
+
+
+def middle_slot(hops, side):
+    return (hops[1][0], hops[1][1]), jnp.where(lax.axis_index("row") < 2, 1, 0), side
+
+
+def last_slot(hops, side):
+    here = lax.axis_index("row")
+    return (hops[0][1], hops[2][0], hops[2][1]), jnp.where(here == 3, 1, jnp.where(here == 0, 2, 0)), side
+
+
+def only(array, side):
+    return (array,), 0, side
 
 
 def sum_row(part):
@@ -602,13 +661,15 @@
     return part
 
 
-def sum_row_low(part):
+def sum_row_low(part, beside):
     if lax.axis_size("row") != 4:
-        return lax.psum(part.astype(jnp.bfloat16), "row").astype(jnp.float32)
+        return lax.psum(part.astype(jnp.bfloat16), "row").astype(jnp.float32), beside
     for k in (1, 2):
         sent = lax.ppermute(part.astype(jnp.bfloat16), "row", [(i, i ^ k) for i in range(4)])
+        if k == 1:
+            sent, beside = lax.optimization_barrier((sent, beside))
         part = part + sent.astype(jnp.float32)
-    return part
+    return part, beside
 
 
 def share_wide(part):
@@ -687,38 +748,47 @@
         x_proj = jnp.concatenate([own(x_proj_dt, 0, chan), own(x_proj_bc, 0, chan)], 1)
         return x_proj, own(dt_proj, 1, chan), own(dt_bias, 0, chan)[None], own(a_log, 1, chan), own(skip_weight, 0, chan)[None]
 
-    gathered, w_in, (x_proj, dtw, dtb, alog, skip) = gather_wide(
-        jnp.concatenate([normed, lanes], 0), lambda: jnp.transpose(in_proj, (2, 0, 1, 3)), small_slices
-    )
-    rows = gathered[:, :shard_rows].reshape(-1, width)
-    ids = gathered[:, shard_rows, :shard_rows].astype(jnp.int32).reshape(-1)
+    begun = begin_gather(jnp.concatenate([normed, lanes], 0))
+    begun, w_in = lax.optimization_barrier((begun, jnp.transpose(in_proj, (2, 0, 1, 3))))
+    row_blocks, (x_proj, dtw, dtb, alog, skip) = end_gather(begun, small_slices)
+    rows = assemble(row_blocks)
+    ids = rows[:, shard_rows, :shard_rows].astype(jnp.int32).reshape(-1)
     masks = (ids[:, None] == jnp.arange(128, dtype=ids.dtype)[None]).astype(jnp.bfloat16)
-    span_rows = rows.shape[0]
+    span_rows = ids.shape[0]
     block = min(256, span_rows)
     order = row_order()
     slot = jnp.arange(row_count, dtype=jnp.int32)[:, None] == lax.axis_index("row")
     whole = jnp.zeros((1,), jnp.int32)
     chunk = lax.axis_index("wide").astype(jnp.int32)[None] * shard_rows
+    places = sorted_places(ids, mods)
+    pieces = len(row_blocks)
+    here = lax.axis_index("wide").astype(jnp.int32)
+    if pieces == 8:
+        swapped = places.reshape(pieces, shard_rows)
+        block_places = jnp.concatenate([pick(swapped, here ^ k)[None] for k in range(pieces)], 1)
+    else:
+        block_places = places
+    rows_chunk = sort_rows(chunk, block_places, row_blocks, shard_rows, shard_rows, pieces)
+    rows, rows_chunk = lax.optimization_barrier((rows, rows_chunk))
+    rows_near = lax.all_gather(rows_chunk, "row", axis=0)
+    cot_begun = begin_gather(after(cotangent, rows_chunk))
     conv_in, gate_in, pre_act, conv_out, part = enter(
         rows, masks, w_in, conv_taps, conv_bias.astype(jnp.float32)[None], x_proj, block
     )
-    places = sorted_places(ids, mods)
-
-    def sort_chunk():
-        return sort_rows(chunk, places, (rows,), shard_rows, shard_rows)
-
-    cot_gathered, part, rows_chunk = gather_wide(after(cotangent, rows), lambda: part, sort_chunk)
-    cot_rows = cot_gathered.reshape(-1, width)
-    rows_near = lax.all_gather(rows_chunk, "row", axis=0)
-
-    def first_work():
-        cot_chunk = sort_rows(chunk, places, (cot_rows,), shard_rows, shard_rows)
-        return cot_chunk, apply(masks, (cot_rows,), w_out, True, jnp.float32, block)
-
-    small, (cot_chunk, d_gated) = sum_wide(part, first_work)
-    small, rows_near = lax.optimization_barrier((small, rows_near))
+    part, cot_begun = lax.optimization_barrier((part, cot_begun))
+
+    cot_blocks, _ = end_gather(cot_begun, lambda: ())
+
+    def first_work(cot_blocks):
+        cot_chunk = sort_rows(chunk, block_places, cot_blocks, shard_rows, shard_rows, pieces)
+        if pieces == 8:
+            d_gated = apply_blocks(here[None], masks, cot_blocks, out_proj)
+        else:
+            d_gated = apply(masks, (jnp.concatenate(cot_blocks, 0),), w_out, True, jnp.float32, block)
+        return cot_chunk, d_gated
+
+    small, (cot_chunk, d_gated) = sum_wide(part, cot_blocks, first_work, False)
     cot_near = lax.all_gather(cot_chunk, "row", axis=0)
-    rows_far = lax.all_gather(others(rows_near, order), "wide", axis=0)
     low_rank = small[:, :rank].astype(jnp.bfloat16)
     coefs = small[:, rank:]
     gated, d_y, d_gate_in, starts = scan_forward(
@@ -726,52 +796,54 @@
     )
     line = row_count == 4
     gates = sort_rows(whole, places, (gated, d_gate_in), span_rows, block)
-    d_y, gates = lax.optimization_barrier((d_y, gates))
+    bounds = sum_row(jnp.where(slot, group_bounds(after(ids, part), mods)[None], 0))
+    bounds = jnp.stack([pick(bounds, q) for q in order], 0)
+    d_y, gates, bounds, rows_near = lax.optimization_barrier((d_y, gates, bounds, rows_near))
+    rows_far = lax.all_gather(others(rows_near, order), "wide", axis=0)
     gate_hops = [hop(gates, gates)] if line else []
     d_pre_step, d_value, d_low_part, d_in, d_out, grad_alog, grad_skip, grad_bias, grad_wdtp = scan_backward(
         low_rank, dtw, dtb, coefs, coefs.T, conv_out, alog, skip, d_y, starts
     )
     d_part = jnp.concatenate([d_low_part, d_in.reshape(span_rows, n), d_out.reshape(span_rows, n)], 1)
+    d_part, cot_near, gate_hops = lax.optimization_barrier((d_part, cot_near, gate_hops))
+    cot_far = lax.all_gather(others(cot_near, order), "wide", axis=0)
+
+    def third_work(gated):
+        part = apply(masks, (gated,), w_out, False, jnp.bfloat16, block)
+        return part
+
+    d_small, projected = sum_wide(d_part, gated, third_work)
     if line:
-        d_part, cot_near, gate_hops[0] = lax.optimization_barrier((d_part, cot_near, gate_hops[0]))
         gate_hops.append(hop(*gate_hops[0]))
-    cot_far = lax.all_gather(others(cot_near, order), "wide", axis=0)
-    d_small, projected = sum_wide(
-        d_part, lambda: apply(masks, (after(gated, d_part),), w_out, False, jnp.bfloat16, block)
-    )
     d_small = d_small.astype(jnp.bfloat16)
-    if line:
-        d_small, projected, gate_hops[1] = lax.optimization_barrier((d_small, projected, gate_hops[1]))
-        gate_hops.append(hop(*gate_hops[1]))
     d_conv_in, grad_taps, grad_cbias, grad_x = leave(
         d_value, d_small, x_proj, pre_act, conv_in, conv_out, conv_taps, block
     )
     conv_sorted = sort_rows(whole, places, (d_conv_in,), span_rows, block)
     d_conv_in, conv_sorted = lax.optimization_barrier((d_conv_in, conv_sorted))
     conv_hops = [hop(conv_sorted, conv_sorted)] if line else []
-
-    def second_work():
-        part = apply(masks, (d_conv_in, d_gate_in), w_in, True, jnp.bfloat16, block)
-        rows_sorted = sort_rows(whole, places, (after(rows, d_conv_in),), span_rows, block)
-        cot_sorted = sort_rows(whole, places, (after(cot_rows, d_conv_in),), span_rows, block)
-        return part, rows_sorted, cot_sorted
-
-    projected, (normed_part, rows_sorted, cot_sorted) = scatter_wide(projected, second_work)
-    output = (residual + projected).astype(jnp.bfloat16)
-    bounds = sum_row(jnp.where(slot, group_bounds(after(ids, d_small), mods)[None], 0))
-    bounds = jnp.stack([pick(bounds, q) for q in order], 0)
+    normed_part = apply(masks, (d_conv_in, d_gate_in), w_in, True, jnp.bfloat16, block)
+    normed_part, rows_far = lax.optimization_barrier((normed_part, rows_far))
     if line:
-        normed_part, gate_hops[2], conv_hops[0] = lax.optimization_barrier((normed_part, gate_hops[2], conv_hops[0]))
+        normed_part, gate_hops[1] = lax.optimization_barrier((normed_part, gate_hops[1]))
+        gate_hops.append(hop(*gate_hops[1]))
+    rows_sorted = sort_rows(whole, block_places, [after(x, normed_part) for x in row_blocks], span_rows, block, pieces)
+    cot_sorted = sort_rows(whole, block_places, [after(x, normed_part) for x in cot_blocks], span_rows, block, pieces)
+    if line:
+        rows_sorted, cot_sorted, conv_hops[0] = lax.optimization_barrier((rows_sorted, cot_sorted, conv_hops[0]))
         conv_hops.append(hop(*conv_hops[0]))
-        gates = arrange(gates, gate_hops)
+        gates_all = lambda side: [only(gates, side), near_slot(gate_hops, side), middle_slot(gate_hops, side)]
     else:
-        gates = gather_ordered(gates, order)
-        conv_all = gather_ordered(conv_sorted, order)
+        gates_rows = gather_ordered(gates, order)
+        gates_all = lambda side: [only(g, side) for g in gates_rows]
+        conv_all = [only(d, 0) for d in gather_ordered(conv_sorted, order)]
     apart = lambda a: a.reshape(span_rows // shard_rows, 1, shard_rows, width)
     far = range(row_count - 1)
     rows_slots = [(apart(rows_sorted), 0)] + [(rows_far, s) for s in far]
     cot_slots = [(apart(cot_sorted), 0)] + [(cot_far, s) for s in far]
-    d_normed, grad_z = scatter_wide(normed_part, lambda: grad_in(bounds, rows_slots, gates, mods, chan, 1))
+    most = len(far)
+    z_most = grad_in(bounds[:-1], rows_slots[:-1], [(g,) for g in gates_all(1)[:most]], mods, chan)
+    d_normed = scatter_wide(normed_part)
     weighted = gain_vec * d_normed
     grad_hidden = (
         cotangent.astype(jnp.float32)
@@ -780,24 +852,27 @@
     )
     g_gain = sum_row(share_wide(jnp.sum(d_normed * residual * inv_rms, 0)))
 
+    small_grads = (grad_taps, grad_cbias[0], grad_x, grad_wdtp, grad_bias[0], grad_alog, grad_skip[0])
+    flat = after(jnp.concatenate([g.reshape(-1) for g in small_grads]).reshape(-1, 128), z_most)
+    z_most, cot_far = lax.optimization_barrier((z_most, cot_far))
+    cot_slots = [(apart(cot_sorted), 0)] + [(cot_far, s) for s in far]
     if line:
-        grad_z, conv_hops[1] = lax.optimization_barrier((grad_z, conv_hops[1]))
+        z_most, gate_hops[2], conv_hops[1] = lax.optimization_barrier((z_most, gate_hops[2], conv_hops[1]))
         conv_hops.append(hop(*conv_hops[1]))
-        early = [conv_sorted, arrange_near(conv_hops), arrange_middle(conv_hops)]
+        conv_all = [only(conv_sorted, 0), near_slot(conv_hops, 0), middle_slot(conv_hops, 0)]
+        gates_all = [[*gates_all(side), last_slot(gate_hops, side)] for side in (0, 1)]
     else:
-        early = conv_all[:-1]
-    grad_x_most = grad_in(bounds[:-1], rows_slots[:-1], early, mods, chan, 0)
-    grad_wout = grad_out(bounds, cot_slots, gates, mods, chan, 0)
+        gates_all = [gates_all(0), gates_all(1)]
+    x_most = grad_in(bounds[:-1], rows_slots[:-1], [(d,) for d in conv_all[:most]], mods, chan)
+    output = (residual + scatter_wide(after(projected, normed_part))).astype(jnp.bfloat16)
+    flat, x_most = sum_row_low(flat, x_most)
+    grad_wout = grad_out(bounds, cot_slots, gates_all[0], mods, chan)
     if line:
-        grad_x_most, grad_wout, conv_hops[2] = lax.optimization_barrier((grad_x_most, grad_wout, conv_hops[2]))
-        last = arrange_last(conv_hops)
-    else:
-        last = conv_all[-1]
-    grad_win = grad_in(bounds[-1:], rows_slots[-1:], [last], mods, chan, 0, grad_x_most, grad_z)
+        x_most, grad_wout, conv_hops[2] = lax.optimization_barrier((x_most, grad_wout, conv_hops[2]))
+        conv_all.append(last_slot(conv_hops, 0))
+    grad_win = grad_in(bounds[-1:], rows_slots[-1:], [(conv_all[-1], gates_all[1][-1])], mods, chan, (x_most, z_most))
     grad_win = grad_win.reshape(mods, width, chan // 128, 2, 128).transpose(0, 1, 3, 2, 4).reshape(mods, width, 2, chan)
-    small_grads = (grad_taps, grad_cbias[0], grad_x, grad_wdtp, grad_bias[0], grad_alog, grad_skip[0])
-    flat = after(jnp.concatenate([g.reshape(-1) for g in small_grads]).reshape(-1, 128), grad_z)
-    flat = sum_row_low(flat).reshape(-1)
+    flat = flat.reshape(-1)
     summed, at = [], 0
     for g in small_grads:
         summed.append(flat[at : at + g.size].reshape(g.shape))

time: 573 us -> 503 us (0.88)
  waiting for transfers between devices: 117 us -> 63.7 us
  local copies, waits for them, and re-layouts: 64.4 us -> 84.6 us
  other arithmetic: 47.1 us -> 28.3 us
  Pallas kernels: 246 us -> 228 us
    unnamed x82 -> x181, local copies, waits for them, and re-layouts: 26.1 us -> 57.3 us
    ppermute x37 -> x29, waiting for transfers between devices: 47.4 us -> 24.3 us  [cross(): lax.ppermute(array, 'wide', [(i, i ^ k) for i in range(lax.axis_size('wid...]
    ppermute x6, waiting for transfers between devices: 21.8 us -> 0.02 us  [hop(): lax.ppermute(falling, 'row', [(1, 0), (2, 1), (3, 2)])]
    ppermute x6, waiting for transfers between devices: 13.6 us -> 33.8 us  [hop(): lax.ppermute(rising, 'row', [(0, 1), (1, 2), (2, 3)])]
    all_gather x1, waiting for transfers between devices: 15.1 us -> 0.01 us  [local(): rows_near = lax.all_gather(rows_chunk, 'row', axis=0)]
    add x4 -> x1, other arithmetic: 12.1 us -> 0.07 us  [sum_wide(): mine = mine + cross(other, 1)]
    pallas_call x3 -> x2, Pallas kernels: 42.5 us -> 31.3 us  [apply(): pl.pallas_call(functools.partial(apply_kernel, turned=turned), grid=(span...]
    dynamic_update_slice x15 -> x8, local copies, waits for them, and re-layouts: 11.3 us -> 1.52 us  [assemble(): whole = lax.dynamic_update_index_in_dim(whole, block, here ^ k, 0)]
  transfers between devices with their start and end apart: 59 -> 53, of which waited for: 20 -> 15; matrix products, arithmetic and copies ran while one was open for 16% -> 12% of each run, Pallas kernels for 39% -> 46%
where the time goes in v2:
time: 503 us; the launch traced here: 493 us
  Pallas kernels  228 us (45%)
  local copies, waits for them, and re-layouts  84.6 us (17%)
  starting transfers between devices  72.4 us (14%)
  waiting for transfers between devices  63.7 us (13%)
  other arithmetic  28.3 us (6%)
  between operations  15.6 us (3%)
    pallas_call x3, Pallas kernels, grad_in(): pl.pallas_call(functools.partial(grad_in_kernel, slots=slots, choices=cho...  67.1 us
    unnamed x181, local copies, waits for them, and re-layouts  57.3 us
    pallas_call x1, Pallas kernels, scan_backward(): pl.pallas_call(bwd_kernel, grid=(steps,), in_specs=[tok(rank), full(dtw),...  36.3 us
    ppermute x6, waiting for transfers between devices, hop(): lax.ppermute(rising, 'row', [(0, 1), (1, 2), (2, 3)])  33.8 us
    pallas_call x2, Pallas kernels, apply(): pl.pallas_call(functools.partial(apply_kernel, turned=turned), grid=(span...  31.3 us
    ppermute x6, starting transfers between devices, hop(): lax.ppermute(rising, 'row', [(0, 1), (1, 2), (2, 3)])  28.7 us
    ppermute x29, waiting for transfers between devices, cross(): lax.ppermute(array, 'wide', [(i, i ^ k) for i in range(lax.axis_size('wid...  24.3 us
    pallas_call x1, Pallas kernels, grad_out(): pl.pallas_call(functools.partial(grad_out_kernel, slots=slots, choices=ch...  23.1 us
  transfers between devices with their start and end apart: 53, of which 15 were waited for; matrix products, arithmetic and copies ran while one was open for 12% of the time, Pallas kernels for 46%

profile of v2, /device:TPU:0, one launch (start us, length us, event | category | flops | bytes accessed | tf_op | source)
XLA Modules:
  0.0 493.0 jit_solution(13761193273476948835)
XLA Ops:
  11.7 2.6 collective-permute-start.1
  18.2 12.1 %copy.61 = bf16[3,2048,2,512]{3,1,0,2:T(8,128)(2,1)} copy(bf16[3,2048,2,512]{3,2,1,0:T(2,128)(2,1)} %param.17) | data formatting | bytes 25165824 | tf_op args[3]
  36.6 6.5 %collective-permute-done.5 = bf16[72,2048]{1,0:T(8,128)(2,1)S(1)} collective-permute-done((bf16[72,2048]{1,0:T(8,128)(2,1)S(1)}, bf16[72,2048]{1,0:T(8,128)(2,1)S(1)}, u32[]{:S(2)}, u32[]{:S(2)}) %collective-permute-start.5) | collective-permute-done | bytes 294944 | tf_op jit(solution)/shard_map/ppermute | solution.py:572
  64.9 21.2 %shard_map.238 = (f32[1024,512]{1,0:T(8,128)}, f32[1024,512]{1,0:T(8,128)}, f32[1024,512]{1,0:T(8,128)}, bf16[1024,512]{1,0:T(8,128)(2,1)}, f32[1024,160]{1,0:T(8,128)}) custom-call(bf16[8,144,2048]{2,1,0:T(8,128)(2,1)} %copy-done.64, bf16[1024,128]{1,0:T(8,128)(2,1)} %fusion.16.masks, bf16[2,3,2048,512]{3,2,1,0:T(8,128)(2,1)} %bitcast.102, ...), custom_call_target="tpu_custom_call" | custom-call | tf_op jit(solution)/shard_map/pallas_call | solution.py:408
  91.2 3.9 collective-permute-done.14
  106.3 2.8 copy-done.3
  109.1 8.0 %shard_map.240.dgated = f32[1024,512]{1,0:T(8,128)S(1)} custom-call(s32[1]{0:T(128)} %bitcast.13.place, bf16[1024,128]{1,0:T(8,128)(2,1)S(1)} %copy-done.19, bf16[128,2048]{1,0:T(8,128)(2,1)S(1)} %copy-done.10, bf16[128,2048]{1,0:T(8,128)(2,1)S(1)} %collective-permute-done.10.refs_1_, bf16[128,2048]{1,0:T(8,128)(2,1)S(1)} %collective-permute-done.8.refs_2_, ...), custom_call_target="tpu_custom_call" | custom-call | tf_op jit(solution)/shard_map/pallas_call | solution.py:544
  122.9 2.6 collective-permute-start.22
  134.8 12.8 %shard_map.241 = (bf16[1024,512]{1,0:T(8,128)(2,1)S(1)}, bf16[1024,512]{1,0:T(8,128)(2,1)S(1)}, bf16[1024,512]{1,0:T(8,128)(2,1)S(1)}, f32[4,16,512]{2,1,0:T(8,128)S(1)}) custom-call(bf16[1024,128]{1,0:T(8,128)(2,1)S(1)} %slice.124.lr, bf16[128,512]{1,0:T(8,128)(2,1)S(1)} %copy-done.49, f32[1,512]{1,0:T(1,128)S(1)} %bitcast.88, ...), custom_call_target="tpu_custom_call" | custom-call | tf_op jit(solution)/shard_map/pallas_call | solution.py:250
  149.3 2.9 shard_map.242.refs_3_.refs_4_
  159.1 5.9 %collective-permute-start.23 = (bf16[1024,1024]{1,0:T(8,128)(2,1)S(1)}, bf16[1024,1024]{1,0:T(8,128)(2,1)}, u32[]{:S(2)}, u32[]{:S(2)}) collective-permute-start(bf16[1024,1024]{1,0:T(8,128)(2,1)S(1)} %shard_map.242.refs_3_.refs_4_), channel_id=1, source_target_pairs={{0,8},{8,16},{16,24},{1,9},{9,17},{17,25},{2,10},{10,18},{18,26},{... | collective-permute-start | bytes 6291464 | tf_op jit(solution)/shard_map/ppermute | solution.py:633
  171.2 36.3 %shard_map.243 = (bf16[1024,512]{1,0:T(8,128)(2,1)}, f32[1024,512]{1,0:T(8,128)S(1)}, f32[1024,128]{1,0:T(8,128)S(1)}, f32[4,16,256]{2,1,0:T(8,128)S(1)}, f32[4,...) custom-call(bf16[1024,128]{1,0:T(8,128)(2,1)S(1)} %slice.124.lr, ...), custom_call_target="tpu_custom_call" | custom-call | tf_op jit(solution)/shard_map/pallas_call | solution.py:350
  216.4 2.6 pad_maximum_fusion.2
  222.0 3.6 collective-permute-start.30
  233.0 11.3 %shard_map.244 = bf16[1024,2048]{1,0:T(8,128)(2,1)} custom-call(bf16[1024,128]{1,0:T(8,128)(2,1)} %fusion.16.masks, bf16[1024,512]{1,0:T(8,128)(2,1)} %copy-done.40, bf16[1,3,512,2048]{3,2,1,0:T(8,128)(2,1)} %bitcast.74), custom_call_target="tpu_custom_call" | custom-call | tf_op jit(solution)/shard_map/pallas_call | solution.py:433
  245.2 5.0 %collective-permute-done.27 = bf16[512,160]{1,0:T(8,128)(2,1)S(1)} collective-permute-done((bf16[512,160]{1,0:T(8,128)(2,1)S(1)}, bf16[512,160]{1,0:T(8,128)(2,1)S(1)}, u32[]{:S(2)}, u32[]{:S(2)}) %collective-permute-start.27) | collective-permute-done | bytes 163872 | tf_op jit(solution)/shard_map/ppermute | solution.py:572
  252.9 7.2 %shard_map.245 = (bf16[1024,512]{1,0:T(8,128)(2,1)}, f32[4,512]{1,0:T(4,128)}, f32[1,512]{1,0:T(1,128)}, f32[512,160]{1,0:T(8,128)}) custom-call(f32[1024,512]{1,0:T(8,128)} %copy-done.45, bf16[1024,160]{1,0:T(8,128)(2,1)} %fusion.14.dsmall, bf16[512,160]{1,0:T(8,128)(2,1)} %pad_maximum_fusion.3.xp, f32[1024,512]{1,0:T(8,128)} %get-tuple-element.166.pre_act, ...), custom_call_target="tpu_custom_call" | custom-call | tf_op jit(solution)/shard_map/pallas_call | solution.py:484
  264.2 20.0 %shard_map.247 = bf16[1024,2048]{1,0:T(8,128)(2,1)} custom-call(bf16[1024,128]{1,0:T(8,128)(2,1)} %fusion.16.masks, bf16[1024,512]{1,0:T(8,128)(2,1)} %get-tuple-element.169.refs_0_, bf16[1024,512]{1,0:T(8,128)(2,1)} %copy-done.39, bf16[2,3,2048,512]{3,2,1,0:T(8,128)(2,1)} %bitcast.103), custom_call_target="tpu_custom_call" | custom-call | tf_op jit(solution)/shard_map/pallas_call | solution.py:433
  286.1 5.5 %collective-permute-start.37 = (bf16[1024,512]{1,0:T(8,128)(2,1)}, bf16[1024,512]{1,0:T(8,128)(2,1)}, u32[]{:S(2)}, u32[]{:S(2)}) collective-permute-start(bf16[1024,512]{1,0:T(8,128)(2,1)} %copy-done.41), channel_id=1, source_target_pairs={{0,8},{8,16},{16,24},{1,9},{9,17},{17,25},{2,10},{10,18},{18,26},{... | collective-permute-start | bytes 3145736 | tf_op jit(solution)/shard_map/ppermute | solution.py:633
  291.7 3.9 collective-permute-start.40
  301.4 6.3 %shard_map.248 = bf16[1024,2048]{1,0:T(8,128)(2,1)S(1)} custom-call(s32[1]{0:T(128)} %constant.131.clone.1.start, s32[1,1024]{1,0:T(1,128)S(1)} %constant_dynamic-update-slice_fusion.2.rank, bf16[144,2048]{1,0:T(8,128)(2,1)S(1)} %fusion.15.refs_0_, bf16[144,2048]{1,0:T(8,128)(2,1)} %collective-permute-done.2.refs_1_, bf16[144,2048]{1,0:T(8,128)(2,1)S(1)} %copy-done.15, ...), custom_call_target="tpu_custom_call" | custom-call | tf_op jit(solution)/shard_map/pallas_call | solution.py:513
  309.9 6.5 %shard_map.249 = bf16[1024,2048]{1,0:T(8,128)(2,1)S(1)} custom-call(s32[1]{0:T(128)} %constant.131.clone.1.start, s32[1,1024]{1,0:T(1,128)S(1)} %constant_dynamic-update-slice_fusion.2.rank, bf16[128,2048]{1,0:T(8,128)(2,1)S(1)} %copy-done.10, bf16[128,2048]{1,0:T(8,128)(2,1)S(1)} %copy-done.38, bf16[128,2048]{1,0:T(8,128)(2,1)S(1)} %copy-done.23, ...), custom_call_target="tpu_custom_call" | custom-call | tf_op jit(solution)/shard_map/pallas_call | solution.py:513
  318.4 4.6 collective-permute-start.42
  325.1 20.4 %shard_map.250.refs_8_ = f32[3,2048,512]{2,1,0:T(8,128)} custom-call(s32[3,4]{1,0:T(4,128)} %bitcast.118, s32[3]{0:T(128)} %pad_add_fusion.4.picks, bf16[8,1,128,2048]{3,2,1,0:T(8,128)(2,1)} %bitcast.72, bf16[8,3,128,2048]{3,2,1,0:T(8,128)(2,1)} %bitcast.94, bf16[8,3,128,2048]{3,2,1,0:T(8,128)(2,1)} %bitcast.95, bf16[1024,1024]{1,0:T(8,128)(2,1)} %copy-done.4, ...), custom_call_target="tpu_custom_call" | custom-call | tf_op jit(solution)/shard_map/pallas_call | solution.py:153
  348.1 33.8 %collective-permute-done.42.refs_6_ = bf16[1024,512]{1,0:T(8,128)(2,1)S(1)} collective-permute-done((bf16[1024,512]{1,0:T(8,128)(2,1)}, bf16[1024,512]{1,0:T(8,128)(2,1)S(1)}, u32[]{:S(2)}, u32[]{:S(2)}) %collective-permute-start.42) | collective-permute-done | bytes 1048608 | tf_op jit(solution)/shard_map/ppermute | solution.py:633
  383.0 20.4 %shard_map.251.refs_7_ = f32[3,2048,512]{2,1,0:T(8,128)} custom-call(s32[3,4]{1,0:T(4,128)} %bitcast.119, s32[3]{0:T(128)} %pad_add_fusion.4.picks, bf16[8,1,128,2048]{3,2,1,0:T(8,128)(2,1)} %bitcast.73, bf16[8,3,128,2048]{3,2,1,0:T(8,128)(2,1)} %bitcast.96, bf16[8,3,128,2048]{3,2,1,0:T(8,128)(2,1)} %bitcast.97, bf16[1024,512]{1,0:T(8,128)(2,1)} %copy-done.41, ...), custom_call_target="tpu_custom_call" | custom-call | tf_op jit(solution)/shard_map/pallas_call | solution.py:153
  403.5 3.6 collective-permute-start.46
  407.7 5.2 %collective-permute-start.44 = (bf16[1024,512]{1,0:T(8,128)(2,1)}, bf16[1024,512]{1,0:T(8,128)(2,1)}, u32[]{:S(2)}, u32[]{:S(2)}) collective-permute-start(bf16[1024,512]{1,0:T(8,128)(2,1)} %copy-done.68), channel_id=1, source_target_pairs={{0,8},{8,16},{16,24},{1,9},{9,17},{17,25},{2,10},{10,18},{18,26},{... | collective-permute-start | bytes 3145736 | tf_op jit(solution)/shard_map/ppermute | solution.py:633
  417.7 23.1 %shard_map.252 = f32[3,512,2048]{2,1,0:T(8,128)} custom-call(s32[4,4]{1,0:T(4,128)} %pad_add_fusion.bounds, s32[4]{0:T(128)} %fusion.21.picks, bf16[8,1,128,2048]{3,2,1,0:T(8,128)(2,1)} %bitcast.75, bf16[8,3,128,2048]{3,2,1,0:T(8,128)(2,1)} %bitcast.99, bf16[8,3,128,2048]{3,2,1,0:T(8,128)(2,1)} %bitcast.100, bf16[8,3,128,2048]{3,2,1,0:T(8,128)(2,1)} %bitcast.101, ...), custom_call_target="tpu_custom_call" | custom-call | tf_op jit(solution)/shard_map/pallas_call | solution.py:190
  450.4 26.3 %shard_map.253 = f32[3,16384,128]{2,1,0:T(8,128)} custom-call(s32[1,4]{1,0:T(1,128)} %slice.88.bounds, s32[2]{0:T(128)} %pad_add_fusion.3.picks, bf16[8,3,128,2048]{3,2,1,0:T(8,128)(2,1)} %bitcast.98, bf16[1024,512]{1,0:T(8,128)(2,1)} %collective-permute-done.38.refs_5_.refs_1_, bf16[1024,512]{1,0:T(8,128)(2,1)} %collective-permute-done.44.refs_2_, ...), custom_call_target="tpu_custom_call" | custom-call | tf_op jit(solution)/shard_map/pallas_call | solution.py:153
  476.7 2.6 collective-permute-start.35
  481.5 2.7 fusion.7
  (377 shorter events, 145.3 us)
Async XLA Ops:
  7.2 147.0 %all-gather.9.cloned.1.call-start = ((), (), s32[]{:S(2)}) async-start(), calls=%async_computation.4 | async-start | bytes 2621440 | tf_op jit(solution)/shard_map/all_gather | solution.py:773
  11.2 22.2 %collective-permute-start.2 = (bf16[144,2048]{1,0:T(8,128)(2,1)S(1)}, bf16[144,2048]{1,0:T(8,128)(2,1)}, u32[]{:S(2)}, u32[]{:S(2)}) collective-permute-start(bf16[144,2048]{1,0:T(8,128)(2,1)S(1)} %fusion.15.refs_0_), channel_id=1, source_target_pairs={{0,1},{1,0},{2,3},{3,2},{4,5},{5,4},{6,7},{7,6},{8,9},{9,8},{10,11... | collective-permute-start | bytes 1769480 | tf_op jit(solution)/shard_map/ppermute | solution.py:572
  11.7 21.7 %collective-permute-start.1 = (bf16[144,2048]{1,0:T(8,128)(2,1)S(1)}, bf16[144,2048]{1,0:T(8,128)(2,1)S(1)}, u32[]{:S(2)}, u32[]{:S(2)}) collective-permute-start(bf16[144,2048]{1,0:T(8,128)(2,1)S(1)} %fusion.15.refs_0_), channel_id=1, source_target_pairs={{0,4},{1,5},{2,6},{3,7},{4,0},{5,1},{6,2},{7,3},{8,12},{9,13},{10,... | collective-permute-start | bytes 1769480 | tf_op jit(solution)/shard_map/ppermute | solution.py:572
  14.3 19.1 %collective-permute-start = (bf16[144,2048]{1,0:T(8,128)(2,1)S(1)}, bf16[144,2048]{1,0:T(8,128)(2,1)S(1)}, u32[]{:S(2)}, u32[]{:S(2)}) collective-permute-start(bf16[144,2048]{1,0:T(8,128)(2,1)S(1)} %fusion.15.refs_0_), channel_id=1, source_target_pairs={{0,2},{1,3},{2,0},{3,1},{4,6},{5,7},{6,4},{7,5},{8,10},{9,11},{10,... | collective-permute-start | bytes 1769480 | tf_op jit(solution)/shard_map/ppermute | solution.py:572
  60.3 158.7 %all-gather.11.cloned.1.call-start = ((), (), s32[]{:S(2)}) async-start(), calls=%async_computation.5 | async-start | bytes 2621440 | tf_op jit(solution)/shard_map/all_gather | solution.py:791
  60.5 25.5 %collective-permute-start.10 = (bf16[128,2048]{1,0:T(8,128)(2,1)S(1)}, bf16[128,2048]{1,0:T(8,128)(2,1)S(1)}, u32[]{:S(2)}, u32[]{:S(2)}) collective-permute-start(bf16[128,2048]{1,0:T(8,128)(2,1)S(1)} %copy-done.10), channel_id=1, source_target_pairs={{0,1},{1,0},{2,3},{3,2},{4,5},{5,4},{6,7},{7,6},{8,9},{9,8},{10,11... | collective-permute-start | bytes 1572872 | tf_op jit(solution)/shard_map/ppermute | solution.py:572
  60.8 25.3 %collective-permute-start.9 = (bf16[128,2048]{1,0:T(8,128)(2,1)S(1)}, bf16[128,2048]{1,0:T(8,128)(2,1)S(1)}, u32[]{:S(2)}, u32[]{:S(2)}) collective-permute-start(bf16[128,2048]{1,0:T(8,128)(2,1)S(1)} %copy-done.10), channel_id=1, source_target_pairs={{0,4},{1,5},{2,6},{3,7},{4,0},{5,1},{6,2},{7,3},{8,12},{9,13},{10,... | collective-permute-start | bytes 1572872 | tf_op jit(solution)/shard_map/ppermute | solution.py:572
  61.1 25.0 %collective-permute-start.8 = (bf16[128,2048]{1,0:T(8,128)(2,1)S(1)}, bf16[128,2048]{1,0:T(8,128)(2,1)S(1)}, u32[]{:S(2)}, u32[]{:S(2)}) collective-permute-start(bf16[128,2048]{1,0:T(8,128)(2,1)S(1)} %copy-done.10), channel_id=1, source_target_pairs={{0,2},{1,3},{2,0},{3,1},{4,6},{5,7},{6,4},{7,5},{8,10},{9,11},{10,... | collective-permute-start | bytes 1572872 | tf_op jit(solution)/shard_map/ppermute | solution.py:572
  99.8 18.6 %collective-permute-start.19 = (bf16[512,160]{1,0:T(8,128)(2,1)}, bf16[512,160]{1,0:T(8,128)(2,1)}, u32[]{:S(2)}, u32[]{:S(2)}) collective-permute-start(bf16[512,160]{1,0:T(8,128)(2,1)} %fusion.18), channel_id=1, source_target_pairs={{0,6},{1,7},{2,4},{3,5},{4,2},{5,3},{6,0},{7,1},{8,14},{9,15},{10,... | collective-permute-start | bytes 491528 | tf_op jit(solution)/shard_map/ppermute | solution.py:572
  101.7 16.7 %collective-permute-start.18 = (bf16[512,160]{1,0:T(8,128)(2,1)}, bf16[512,160]{1,0:T(8,128)(2,1)}, u32[]{:S(2)}, u32[]{:S(2)}) collective-permute-start(bf16[512,160]{1,0:T(8,128)(2,1)} %fusion.18), channel_id=1, source_target_pairs={{0,4},{1,5},{2,6},{3,7},{4,0},{5,1},{6,2},{7,3},{8,12},{9,13},{10,... | collective-permute-start | bytes 491528 | tf_op jit(solution)/shard_map/ppermute | solution.py:572
  118.5 165.7 %all-gather.13.cloned.1.call-start = ((), (), s32[]{:S(2)}) async-start(), calls=%async_computation.6 | async-start | bytes 14155776 | tf_op jit(solution)/shard_map/all_gather | solution.py:802
  157.8 190.3 %all-gather.15.cloned.1.call-start = ((), (), s32[]{:S(2)}) async-start(), calls=%async_computation.7 | async-start | bytes 14155776 | tf_op jit(solution)/shard_map/all_gather | solution.py:809
  157.8 61.2 %collective-permute-start.24 = (bf16[1024,1024]{1,0:T(8,128)(2,1)S(1)}, bf16[1024,1024]{1,0:T(8,128)(2,1)}, u32[]{:S(2)}, u32[]{:S(2)}) collective-permute-start(bf16[1024,1024]{1,0:T(8,128)(2,1)S(1)} %shard_map.242.refs_3_.refs_4_), channel_id=1, source_target_pairs={{8,0},{16,8},{24,16},{9,1},{17,9},{25,17},{10,2},{18,10},{26,18},{... | collective-permute-start | bytes 6291464 | tf_op jit(solution)/shard_map/ppermute | solution.py:634
  159.1 59.9 %collective-permute-start.23 = (bf16[1024,1024]{1,0:T(8,128)(2,1)S(1)}, bf16[1024,1024]{1,0:T(8,128)(2,1)}, u32[]{:S(2)}, u32[]{:S(2)}) collective-permute-start(bf16[1024,1024]{1,0:T(8,128)(2,1)S(1)} %shard_map.242.refs_3_.refs_4_), channel_id=1, source_target_pairs={{0,8},{8,16},{16,24},{1,9},{9,17},{17,25},{2,10},{10,18},{18,26},{... | collective-permute-start | bytes 6291464 | tf_op jit(solution)/shard_map/ppermute | solution.py:633
  221.9 192.5 %reduce-scatter.5.cloned.1.call-start = ((), (), s32[]{:S(2)}) async-start(), calls=%async_computation.3 | async-start | bytes 4718592 | tf_op jit(solution)/shard_map/reduce_scatter | solution.py:624
  222.0 62.2 %collective-permute-start.30 = (bf16[1024,1024]{1,0:T(8,128)(2,1)}, bf16[1024,1024]{1,0:T(8,128)(2,1)}, u32[]{:S(2)}, u32[]{:S(2)}) collective-permute-start(bf16[1024,1024]{1,0:T(8,128)(2,1)} %collective-permute-done.23.refs_4_.refs_5_), channel_id=1, source_target_pairs={{0,8},{8,16},{16,24},{1,9},{9,17},{17,25},{2,10},{10,18},{18,26},{... | collective-permute-start | bytes 6291464 | tf_op jit(solution)/shard_map/ppermute | solution.py:633
  225.5 58.7 %collective-permute-start.31 = (bf16[1024,1024]{1,0:T(8,128)(2,1)}, bf16[1024,1024]{1,0:T(8,128)(2,1)}, u32[]{:S(2)}, u32[]{:S(2)}) collective-permute-start(bf16[1024,1024]{1,0:T(8,128)(2,1)} %collective-permute-done.24.refs_5_.refs_6_.refs_9_.refs_4_), channel_id=1, source_target_pairs={{8,0},{16,8},{24,16},{9,1},{17,9},{25,17},{10,2},{18,10},{26,18},{... | collective-permute-start | bytes 6291464 | tf_op jit(solution)/shard_map/ppermute | solution.py:634
  231.5 18.7 %collective-permute-start.27 = (bf16[512,160]{1,0:T(8,128)(2,1)S(1)}, bf16[512,160]{1,0:T(8,128)(2,1)S(1)}, u32[]{:S(2)}, u32[]{:S(2)}) collective-permute-start(bf16[512,160]{1,0:T(8,128)(2,1)S(1)} %convert_element_type.114), channel_id=1, source_target_pairs={{0,4},{1,5},{2,6},{3,7},{4,0},{5,1},{6,2},{7,3},{8,12},{9,13},{10,... | collective-permute-start | bytes 491528 | tf_op jit(solution)/shard_map/ppermute | solution.py:572
  231.9 18.2 %collective-permute-start.26 = (bf16[512,160]{1,0:T(8,128)(2,1)S(1)}, bf16[512,160]{1,0:T(8,128)(2,1)S(1)}, u32[]{:S(2)}, u32[]{:S(2)}) collective-permute-start(bf16[512,160]{1,0:T(8,128)(2,1)S(1)} %convert_element_type.114), channel_id=1, source_target_pairs={{0,2},{1,3},{2,0},{3,1},{4,6},{5,7},{6,4},{7,5},{8,10},{9,11},{10,... | collective-permute-start | bytes 491528 | tf_op jit(solution)/shard_map/ppermute | solution.py:572
  284.3 197.2 %reduce-scatter.3.cloned.1.call-start = ((), (), s32[]{:S(2)}) async-start(), calls=%async_computation.2 | async-start | bytes 4718592 | tf_op jit(solution)/shard_map/reduce_scatter | solution.py:624
  284.8 33.5 %collective-permute-start.38 = (bf16[1024,512]{1,0:T(8,128)(2,1)}, bf16[1024,512]{1,0:T(8,128)(2,1)}, u32[]{:S(2)}, u32[]{:S(2)}) collective-permute-start(bf16[1024,512]{1,0:T(8,128)(2,1)} %copy-done.41), channel_id=1, source_target_pairs={{8,0},{16,8},{24,16},{9,1},{17,9},{25,17},{10,2},{18,10},{26,18},{... | collective-permute-start | bytes 3145736 | tf_op jit(solution)/shard_map/ppermute | solution.py:634
  286.1 32.2 %collective-permute-start.37 = (bf16[1024,512]{1,0:T(8,128)(2,1)}, bf16[1024,512]{1,0:T(8,128)(2,1)}, u32[]{:S(2)}, u32[]{:S(2)}) collective-permute-start(bf16[1024,512]{1,0:T(8,128)(2,1)} %copy-done.41), channel_id=1, source_target_pairs={{0,8},{8,16},{16,24},{1,9},{9,17},{17,25},{2,10},{10,18},{18,26},{... | collective-permute-start | bytes 3145736 | tf_op jit(solution)/shard_map/ppermute | solution.py:633
  291.7 90.3 %collective-permute-start.40 = (bf16[1024,1024]{1,0:T(8,128)(2,1)}, bf16[1024,1024]{1,0:T(8,128)(2,1)}, u32[]{:S(2)}, u32[]{:S(2)}) collective-permute-start(bf16[1024,1024]{1,0:T(8,128)(2,1)} %collective-permute-done.30.refs_6_.refs_7_), channel_id=1, source_target_pairs={{0,8},{8,16},{16,24},{1,9},{9,17},{17,25},{2,10},{10,18},{18,26},{... | collective-permute-start | bytes 6291464 | tf_op jit(solution)/shard_map/ppermute | solution.py:633
  295.6 86.4 %collective-permute-start.41 = (bf16[1024,1024]{1,0:T(8,128)(2,1)}, bf16[1024,1024]{1,0:T(8,128)(2,1)}, u32[]{:S(2)}, u32[]{:S(2)}) collective-permute-start(bf16[1024,1024]{1,0:T(8,128)(2,1)} %collective-permute-done.31.refs_7_.refs_8_), channel_id=1, source_target_pairs={{8,0},{16,8},{24,16},{9,1},{17,9},{25,17},{10,2},{18,10},{26,18},{... | collective-permute-start | bytes 6291464 | tf_op jit(solution)/shard_map/ppermute | solution.py:634
  318.4 63.6 %collective-permute-start.42 = (bf16[1024,512]{1,0:T(8,128)(2,1)}, bf16[1024,512]{1,0:T(8,128)(2,1)S(1)}, u32[]{:S(2)}, u32[]{:S(2)}) collective-permute-start(bf16[1024,512]{1,0:T(8,128)(2,1)} %collective-permute-done.37.refs_4_), channel_id=1, source_target_pairs={{0,8},{8,16},{16,24},{1,9},{9,17},{17,25},{2,10},{10,18},{18,26},{... | collective-permute-start | bytes 3145736 | tf_op jit(solution)/shard_map/ppermute | solution.py:633
  323.0 59.0 %collective-permute-start.43 = (bf16[1024,512]{1,0:T(8,128)(2,1)}, bf16[1024,512]{1,0:T(8,128)(2,1)}, u32[]{:S(2)}, u32[]{:S(2)}) collective-permute-start(bf16[1024,512]{1,0:T(8,128)(2,1)} %collective-permute-done.38.refs_5_.refs_1_), channel_id=1, source_target_pairs={{8,0},{16,8},{24,16},{9,1},{17,9},{25,17},{10,2},{18,10},{26,18},{... | collective-permute-start | bytes 3145736 | tf_op jit(solution)/shard_map/ppermute | solution.py:634
  345.6 57.8 %collective-permute-start.39 = (bf16[1244,128]{1,0:T(8,128)(2,1)S(1)}, bf16[1244,128]{1,0:T(8,128)(2,1)S(1)}, u32[]{:S(2)}, u32[]{:S(2)}) collective-permute-start(bf16[1244,128]{1,0:T(8,128)(2,1)S(1)} %convert_element_type.123), channel_id=1, source_target_pairs={{0,8},{8,0},{16,24},{24,16},{1,9},{9,1},{17,25},{25,17},{2,10},{10... | collective-permute-start | bytes 955400 | tf_op jit(solution)/shard_map/ppermute | solution.py:668
  403.5 38.9 %collective-permute-start.46 = (bf16[1244,128]{1,0:T(8,128)(2,1)S(1)}, bf16[1244,128]{1,0:T(8,128)(2,1)S(1)}, u32[]{:S(2)}, u32[]{:S(2)}) collective-permute-start(bf16[1244,128]{1,0:T(8,128)(2,1)S(1)} %fusion.17), channel_id=1, source_target_pairs={{0,16},{8,24},{16,0},{24,8},{1,17},{9,25},{17,1},{25,9},{2,18},{10... | collective-permute-start | bytes 955400 | tf_op jit(solution)/shard_map/ppermute | solution.py:668
  407.7 42.7 %collective-permute-start.44 = (bf16[1024,512]{1,0:T(8,128)(2,1)}, bf16[1024,512]{1,0:T(8,128)(2,1)}, u32[]{:S(2)}, u32[]{:S(2)}) collective-permute-start(bf16[1024,512]{1,0:T(8,128)(2,1)} %copy-done.68), channel_id=1, source_target_pairs={{0,8},{8,16},{16,24},{1,9},{9,17},{17,25},{2,10},{10,18},{18,26},{... | collective-permute-start | bytes 3145736 | tf_op jit(solution)/shard_map/ppermute | solution.py:633
  412.9 37.5 %collective-permute-start.45 = (bf16[1024,512]{1,0:T(8,128)(2,1)}, bf16[1024,512]{1,0:T(8,128)(2,1)}, u32[]{:S(2)}, u32[]{:S(2)}) collective-permute-start(bf16[1024,512]{1,0:T(8,128)(2,1)} %collective-permute-done.43.refs_7_), channel_id=1, source_target_pairs={{8,0},{16,8},{24,16},{9,1},{17,9},{25,17},{10,2},{18,10},{26,18},{... | collective-permute-start | bytes 3145736 | tf_op jit(solution)/shard_map/ppermute | solution.py:634
  415.9 24.9 %collective-permute-start.32 = (f32[2048]{0:T(1024)S(1)}, f32[2048]{0:T(1024)S(1)}, u32[]{:S(2)}, u32[]{:S(2)}) collective-permute-start(f32[2048]{0:T(1024)S(1)} %get-tuple-element.275), channel_id=1, source_target_pairs={{0,1},{1,0},{2,3},{3,2},{4,5},{5,4},{6,7},{7,6},{8,9},{9,8},{10,11... | collective-permute-start | bytes 24584 | tf_op jit(solution)/shard_map/ppermute | solution.py:572
  444.5 32.1 %collective-permute-start.34 = (f32[2048]{0:T(1024)S(1)}, f32[2048]{0:T(1024)S(1)}, u32[]{:S(2)}, u32[]{:S(2)}) collective-permute-start(f32[2048]{0:T(1024)S(1)} %add.206), channel_id=1, source_target_pairs={{0,4},{1,5},{2,6},{3,7},{4,0},{5,1},{6,2},{7,3},{8,12},{9,13},{10,... | collective-permute-start | bytes 24584 | tf_op jit(solution)/shard_map/ppermute | solution.py:572
  (101 other events, 988.9 us)
Sparse Core Ops, SparseCore 0:
  60.4 46.2 all-gather.8
  118.6 47.3 all-gather.10
  167.9 84.6 all-gather.12
  254.3 72.1 all-gather.14
  330.3 51.3 reduce-scatter.4
  385.2 51.3 reduce-scatter.2

commit v3 on v2

--- a/solution.py
+++ b/solution.py
@@ -253,7 +253,7 @@
         out_specs=[tok(chan)] * 3 + [pl.BlockSpec((1, n, chan), lambda i: (i, 0, 0))],
         out_shape=[jax.ShapeDtypeStruct((rows, chan), jnp.bfloat16)] * 3 + [jax.ShapeDtypeStruct((steps, n, chan), jnp.float32)],
         scratch_shapes=[pltpu.VMEM((n, chan), jnp.float32)] + [pltpu.VMEM((span, chan), jnp.float32)] * 3 + [pltpu.VMEM((span, TILE * n), jnp.bfloat16), pltpu.VMEM((span * n, chan), jnp.bfloat16)],
-        compiler_params=pltpu.CompilerParams(vmem_limit_bytes=32 << 20),
+        compiler_params=pltpu.CompilerParams(vmem_limit_bytes=56 << 20),
     )(lr, dtw, dtb, cf, ct, u, alog, skip, gate, dgated)
 
 def bwd_kernel(lr, dtw, dtb, cf, ct, u, alog, skip, dy, starts, dpre, dval, dlow, din, dout, galog, gskip, gbias, gdtw, lam_s, dt_s, du_s, dyf_s, hp_s, st_s, th_s, bd_s, hb_s, gb_s):
@@ -353,7 +353,7 @@
         out_specs=[tok(chan), tok(chan), tok(rank), ptok, ptok] + [full(o) for o in outs[5:]],
         out_shape=outs,
         scratch_shapes=[pltpu.VMEM((n, chan), jnp.float32)] + [pltpu.VMEM((span, chan), jnp.float32)] * 3 + [pltpu.VMEM((span, n, chan), jnp.float32)] + [pltpu.VMEM((span, chan), jnp.float32)] * 2 + [pltpu.VMEM((span, TILE * n), jnp.bfloat16)] + [pltpu.VMEM((span * n, chan), jnp.bfloat16)] * 2,
-        compiler_params=pltpu.CompilerParams(vmem_limit_bytes=32 << 20),
+        compiler_params=pltpu.CompilerParams(vmem_limit_bytes=56 << 20),
     )(lr, dtw, dtb, cf, ct, u, alog, skip, dy, starts)
 
 
@@ -520,7 +520,7 @@
             out_specs=pl.BlockSpec((block, width), lambda i, s: (i, 0)),
         ),
         out_shape=jax.ShapeDtypeStruct((rows, width), inputs[0].dtype),
-        compiler_params=pltpu.CompilerParams(vmem_limit_bytes=40 << 20),
+        compiler_params=pltpu.CompilerParams(vmem_limit_bytes=56 << 20),
     )(start, rank, *inputs)
 
 
@@ -550,7 +550,7 @@
             out_specs=pl.BlockSpec((span, chan), lambda i, s: (0, 0)),
         ),
         out_shape=jax.ShapeDtypeStruct((span, chan), jnp.float32),
-        compiler_params=pltpu.CompilerParams(vmem_limit_bytes=40 << 20),
+        compiler_params=pltpu.CompilerParams(vmem_limit_bytes=56 << 20),
     )(place, masks, *blocks, w)
 
 
@@ -825,13 +825,13 @@
     normed_part = apply(masks, (d_conv_in, d_gate_in), w_in, True, jnp.bfloat16, block)
     normed_part, rows_far = lax.optimization_barrier((normed_part, rows_far))
     if line:
-        normed_part, gate_hops[1] = lax.optimization_barrier((normed_part, gate_hops[1]))
+        normed_part, gate_hops[1], conv_hops[0] = lax.optimization_barrier((normed_part, gate_hops[1], conv_hops[0]))
         gate_hops.append(hop(*gate_hops[1]))
+        conv_hops.append(hop(*conv_hops[0]))
     rows_sorted = sort_rows(whole, block_places, [after(x, normed_part) for x in row_blocks], span_rows, block, pieces)
     cot_sorted = sort_rows(whole, block_places, [after(x, normed_part) for x in cot_blocks], span_rows, block, pieces)
     if line:
-        rows_sorted, cot_sorted, conv_hops[0] = lax.optimization_barrier((rows_sorted, cot_sorted, conv_hops[0]))
-        conv_hops.append(hop(*conv_hops[0]))
+        rows_sorted, cot_sorted = lax.optimization_barrier((rows_sorted, cot_sorted))
         gates_all = lambda side: [only(gates, side), near_slot(gate_hops, side), middle_slot(gate_hops, side)]
     else:
         gates_rows = gather_ordered(gates, order)

time: 503 us -> 478 us (0.950)
  local copies, waits for them, and re-layouts: 84.6 us -> 46 us
  Pallas kernels: 228 us -> 249 us
    unnamed x181 -> x99, local copies, waits for them, and re-layouts: 57.3 us -> 18.5 us
    ppermute x6, waiting for transfers between devices: 33.8 us -> 19.3 us  [hop(): lax.ppermute(rising, 'row', [(0, 1), (1, 2), (2, 3)])]
    pallas_call x6, Pallas kernels: 21.3 us -> 33.7 us  [sort_rows(): pl.pallas_call(functools.partial(sort_kernel, pieces=pieces), grid_spec=p...]
    ppermute x6, waiting for transfers between devices: 0.02 us -> 7.87 us  [hop(): lax.ppermute(falling, 'row', [(1, 0), (2, 1), (3, 2)])]
  transfers between devices with their start and end apart: 53 -> 53, of which waited for: 15 -> 19; matrix products, arithmetic and copies ran while one was open for 12% -> 13% of each run, Pallas kernels for 46% -> 52%
where the time goes in v3:
time: 478 us; the launch traced here: 473 us
  Pallas kernels  249 us (52%)
  starting transfers between devices  73.5 us (15%)
  waiting for transfers between devices  60.6 us (13%)
  local copies, waits for them, and re-layouts  46 us (10%)
  other arithmetic  27.7 us (6%)
  between operations  15.7 us (3%)
    pallas_call x3, Pallas kernels, grad_in(): pl.pallas_call(functools.partial(grad_in_kernel, slots=slots, choices=cho...  66.3 us
    pallas_call x1, Pallas kernels, scan_backward(): pl.pallas_call(bwd_kernel, grid=(steps,), in_specs=[tok(rank), full(dtw),...  38.2 us
    pallas_call x6, Pallas kernels, sort_rows(): pl.pallas_call(functools.partial(sort_kernel, pieces=pieces), grid_spec=p...  33.7 us
    pallas_call x2, Pallas kernels, apply(): pl.pallas_call(functools.partial(apply_kernel, turned=turned), grid=(span...  31.3 us
    ppermute x6, starting transfers between devices, hop(): lax.ppermute(rising, 'row', [(0, 1), (1, 2), (2, 3)])  30.3 us
    ppermute x29, waiting for transfers between devices, cross(): lax.ppermute(array, 'wide', [(i, i ^ k) for i in range(lax.axis_size('wid...  28.8 us
    pallas_call x1, Pallas kernels, grad_out(): pl.pallas_call(functools.partial(grad_out_kernel, slots=slots, choices=ch...  23.1 us
    pallas_call x1, Pallas kernels, enter(): pl.pallas_call(enter_kernel, grid=(span // block,), in_specs=[pl.BlockSpe...  21.2 us
  transfers between devices with their start and end apart: 53, of which 19 were waited for; matrix products, arithmetic and copies ran while one was open for 13% of the time, Pallas kernels for 52%

profile of v3, /device:TPU:0, one launch (start us, length us, event | category | flops | bytes accessed | tf_op | source)
XLA Modules:
  0.0 472.8 jit_solution(18397196389741650158)
XLA Ops:
  20.7 12.1 %copy.61 = bf16[3,2048,2,512]{3,1,0,2:T(8,128)(2,1)} copy(bf16[3,2048,2,512]{3,2,1,0:T(2,128)(2,1)} %param.17) | data formatting | bytes 25165824 | tf_op args[3]
  38.7 7.6 %collective-permute-done.5 = bf16[72,2048]{1,0:T(8,128)(2,1)S(1)} collective-permute-done((bf16[72,2048]{1,0:T(8,128)(2,1)S(1)}, bf16[72,2048]{1,0:T(8,128)(2,1)S(1)}, u32[]{:S(2)}, u32[]{:S(2)}) %collective-permute-start.5) | collective-permute-done | bytes 294944 | tf_op jit(solution)/shard_map/ppermute | solution.py:572
  53.9 3.8 shard_map.237
  62.6 21.2 %shard_map.238 = (f32[1024,512]{1,0:T(8,128)}, f32[1024,512]{1,0:T(8,128)}, f32[1024,512]{1,0:T(8,128)}, bf16[1024,512]{1,0:T(8,128)(2,1)}, f32[1024,160]{1,0:T(8,128)}) custom-call(bf16[8,144,2048]{2,1,0:T(8,128)(2,1)} %copy-done.3, bf16[1024,128]{1,0:T(8,128)(2,1)} %fusion.16.masks, bf16[2,3,2048,512]{3,2,1,0:T(8,128)(2,1)} %bitcast.80, ...), custom_call_target="tpu_custom_call" | custom-call | tf_op jit(solution)/shard_map/pallas_call | solution.py:408
  88.2 3.7 collective-permute-done.14
  99.6 3.7 shard_map.239
  103.3 12.2 %shard_map.240.dgated = f32[1024,512]{1,0:T(8,128)} custom-call(s32[1]{0:T(128)} %bitcast.13.place, bf16[1024,128]{1,0:T(8,128)(2,1)} %fusion.16.masks, bf16[128,2048]{1,0:T(8,128)(2,1)} %refs_0_.2, bf16[128,2048]{1,0:T(8,128)(2,1)} %copy-done.23, bf16[128,2048]{1,0:T(8,128)(2,1)} %copy-done.14, bf16[128,2048]{1,0:T(8,128)(2,1)} %copy-done.24, ...), custom_call_target="tpu_custom_call" | custom-call | tf_op jit(solution)/shard_map/pallas_call | solution.py:544
  128.4 16.0 %shard_map.241 = (bf16[1024,512]{1,0:T(8,128)(2,1)}, bf16[1024,512]{1,0:T(8,128)(2,1)}, bf16[1024,512]{1,0:T(8,128)(2,1)}, f32[4,16,512]{2,1,0:T(8,128)}) custom-call(bf16[1024,128]{1,0:T(8,128)(2,1)} %slice.124.lr, bf16[128,512]{1,0:T(8,128)(2,1)} %constant_dynamic-slice_fusion.21.dtw, f32[1,512]{1,0:T(1,128)} %bitcast.115, ...), custom_call_target="tpu_custom_call" | custom-call | tf_op jit(solution)/shard_map/pallas_call | solution.py:250
  144.4 5.4 %shard_map.242.refs_3_.refs_4_ = bf16[1024,1024]{1,0:T(8,128)(2,1)} custom-call(s32[1]{0:T(128)} %constant.131.clone.1.start, s32[1,1024]{1,0:T(1,128)} %bitcast.109, bf16[1024,512]{1,0:T(8,128)(2,1)} %get-tuple-element.159.refs_0_, bf16[1024,512]{1,0:T(8,128)(2,1)} %get-tuple-element.149.refs_1_), custom_call_target="tpu_custom_call" | custom-call | tf_op jit(solution)/shard_map/pallas_call | solution.py:513
  154.0 5.9 %collective-permute-start.23 = (bf16[1024,1024]{1,0:T(8,128)(2,1)}, bf16[1024,1024]{1,0:T(8,128)(2,1)}, u32[]{:S(2)}, u32[]{:S(2)}) collective-permute-start(bf16[1024,1024]{1,0:T(8,128)(2,1)} %shard_map.242.refs_3_.refs_4_), channel_id=1, source_target_pairs={{0,8},{8,16},{16,24},{1,9},{9,17},{17,25},{2,10},{10,18},{18,26},{... | collective-permute-start | bytes 6291464 | tf_op jit(solution)/shard_map/ppermute | solution.py:633
  160.0 38.2 %shard_map.243 = (bf16[1024,512]{1,0:T(8,128)(2,1)}, f32[1024,512]{1,0:T(8,128)}, f32[1024,128]{1,0:T(8,128)}, f32[4,16,256]{2,1,0:T(8,128)}, f32[4,16,256]{2,1,...) custom-call(bf16[1024,128]{1,0:T(8,128)(2,1)} %slice.124.lr, ...), custom_call_target="tpu_custom_call" | custom-call | tf_op jit(solution)/shard_map/pallas_call | solution.py:350
  210.0 5.3 %collective-permute-start.30 = (bf16[1024,1024]{1,0:T(8,128)(2,1)}, bf16[1024,1024]{1,0:T(8,128)(2,1)}, u32[]{:S(2)}, u32[]{:S(2)}) collective-permute-start(bf16[1024,1024]{1,0:T(8,128)(2,1)} %collective-permute-done.23.refs_4_.refs_5_), channel_id=1, source_target_pairs={{0,8},{8,16},{16,24},{1,9},{9,17},{17,25},{2,10},{10,18},{18,26},{... | collective-permute-start | bytes 6291464 | tf_op jit(solution)/shard_map/ppermute | solution.py:633
  221.3 11.5 %shard_map.244 = bf16[1024,2048]{1,0:T(8,128)(2,1)} custom-call(bf16[1024,128]{1,0:T(8,128)(2,1)} %fusion.16.masks, bf16[1024,512]{1,0:T(8,128)(2,1)} %get-tuple-element.159.refs_0_, bf16[1,3,512,2048]{3,2,1,0:T(8,128)(2,1)} %bitcast.85), custom_call_target="tpu_custom_call" | custom-call | tf_op jit(solution)/shard_map/pallas_call | solution.py:433
  233.5 5.8 %collective-permute-done.27 = bf16[512,160]{1,0:T(8,128)(2,1)S(1)} collective-permute-done((bf16[512,160]{1,0:T(8,128)(2,1)S(1)}, bf16[512,160]{1,0:T(8,128)(2,1)S(1)}, u32[]{:S(2)}, u32[]{:S(2)}) %collective-permute-start.27) | collective-permute-done | bytes 163872 | tf_op jit(solution)/shard_map/ppermute | solution.py:572
  239.3 5.3 %collective-permute-done.26 = bf16[512,160]{1,0:T(8,128)(2,1)} collective-permute-done((bf16[512,160]{1,0:T(8,128)(2,1)S(1)}, bf16[512,160]{1,0:T(8,128)(2,1)}, u32[]{:S(2)}, u32[]{:S(2)}) %collective-permute-start.26) | collective-permute-done | bytes 163872 | tf_op jit(solution)/shard_map/ppermute | solution.py:572
  248.3 7.2 %shard_map.245 = (bf16[1024,512]{1,0:T(8,128)(2,1)}, f32[4,512]{1,0:T(4,128)}, f32[1,512]{1,0:T(1,128)}, f32[512,160]{1,0:T(8,128)}) custom-call(f32[1024,512]{1,0:T(8,128)} %get-tuple-element.162.dval, bf16[1024,160]{1,0:T(8,128)(2,1)} %fusion.14.dsmall, bf16[512,160]{1,0:T(8,128)(2,1)} %pad_maximum_fusion.3.xp, f32[1024,512]{1,0:T(8,128)} %get-tuple-element.166.pre_act, ...), custom_call_target="tpu_custom_call" | custom-call | tf_op jit(solution)/shard_map/pallas_call | solution.py:484
  255.4 4.0 shard_map.246.refs_3_
  260.7 6.4 %collective-permute-start.32 = (bf16[1024,512]{1,0:T(8,128)(2,1)}, bf16[1024,512]{1,0:T(8,128)(2,1)}, u32[]{:S(2)}, u32[]{:S(2)}) collective-permute-start(bf16[1024,512]{1,0:T(8,128)(2,1)} %shard_map.246.refs_3_), channel_id=1, source_target_pairs={{0,8},{8,16},{16,24},{1,9},{9,17},{17,25},{2,10},{10,18},{18,26},{... | collective-permute-start | bytes 3145736 | tf_op jit(solution)/shard_map/ppermute | solution.py:633
  267.1 19.8 %shard_map.247 = bf16[1024,2048]{1,0:T(8,128)(2,1)} custom-call(bf16[1024,128]{1,0:T(8,128)(2,1)} %fusion.16.masks, bf16[1024,512]{1,0:T(8,128)(2,1)} %get-tuple-element.169.refs_0_, bf16[1024,512]{1,0:T(8,128)(2,1)} %get-tuple-element.149.refs_1_, bf16[2,3,2048,512]{3,2,1,0:T(8,128)(2,1)} %bitcast.81), custom_call_target="tpu_custom_call" | custom-call | tf_op jit(solution)/shard_map/pallas_call | solution.py:433
  289.6 4.5 collective-permute-start.40
  296.2 5.6 %collective-permute-start.42 = (bf16[1024,512]{1,0:T(8,128)(2,1)}, bf16[1024,512]{1,0:T(8,128)(2,1)}, u32[]{:S(2)}, u32[]{:S(2)}) collective-permute-start(bf16[1024,512]{1,0:T(8,128)(2,1)} %collective-permute-done.32.refs_4_), channel_id=1, source_target_pairs={{0,8},{8,16},{16,24},{1,9},{9,17},{17,25},{2,10},{10,18},{18,26},{... | collective-permute-start | bytes 3145736 | tf_op jit(solution)/shard_map/ppermute | solution.py:633
  304.8 8.6 %shard_map.248 = bf16[1024,2048]{1,0:T(8,128)(2,1)} custom-call(s32[1]{0:T(128)} %constant.131.clone.1.start, s32[1,1024]{1,0:T(1,128)} %copy-done.30, bf16[144,2048]{1,0:T(8,128)(2,1)} %copy-done.4, bf16[144,2048]{1,0:T(8,128)(2,1)} %copy-done.19, bf16[144,2048]{1,0:T(8,128)(2,1)} %copy-done.11, bf16[144,2048]{1,0:T(8,128)(2,1)} %copy-done.20, ...), custom_call_target="tpu_custom_call" | custom-call | tf_op jit(solution)/shard_map/pallas_call | solution.py:513
  313.4 8.3 %shard_map.249 = bf16[1024,2048]{1,0:T(8,128)(2,1)} custom-call(s32[1]{0:T(128)} %constant.131.clone.1.start, s32[1,1024]{1,0:T(1,128)} %copy-done.30, bf16[128,2048]{1,0:T(8,128)(2,1)} %refs_0_.2, bf16[128,2048]{1,0:T(8,128)(2,1)} %copy-done.23, bf16[128,2048]{1,0:T(8,128)(2,1)} %copy-done.14, bf16[128,2048]{1,0:T(8,128)(2,1)} %copy-done.24, ...), custom_call_target="tpu_custom_call" | custom-call | tf_op jit(solution)/shard_map/pallas_call | solution.py:513
  321.7 20.0 %shard_map.250.refs_8_ = f32[3,2048,512]{2,1,0:T(8,128)} custom-call(s32[3,4]{1,0:T(4,128)} %bitcast.111, s32[3]{0:T(128)} %pad_add_fusion.4.picks, bf16[8,1,128,2048]{3,2,1,0:T(8,128)(2,1)} %bitcast.82, bf16[8,3,128,2048]{3,2,1,0:T(8,128)(2,1)} %bitcast.72, bf16[8,3,128,2048]{3,2,1,0:T(8,128)(2,1)} %bitcast.73, ...), custom_call_target="tpu_custom_call" | custom-call | tf_op jit(solution)/shard_map/pallas_call | solution.py:153
  341.7 3.1 collective-permute-start.39
  344.8 18.1 %collective-permute-done.42.refs_6_ = bf16[1024,512]{1,0:T(8,128)(2,1)} collective-permute-done((bf16[1024,512]{1,0:T(8,128)(2,1)}, bf16[1024,512]{1,0:T(8,128)(2,1)}, u32[]{:S(2)}, u32[]{:S(2)}) %collective-permute-start.42) | collective-permute-done | bytes 1048608 | tf_op jit(solution)/shard_map/ppermute | solution.py:633
  362.9 4.5 collective-permute-done.43.refs_7_
  367.4 20.0 %shard_map.251.refs_7_ = f32[3,2048,512]{2,1,0:T(8,128)} custom-call(s32[3,4]{1,0:T(4,128)} %bitcast.112, s32[3]{0:T(128)} %pad_add_fusion.4.picks, bf16[8,1,128,2048]{3,2,1,0:T(8,128)(2,1)} %bitcast.83, bf16[8,3,128,2048]{3,2,1,0:T(8,128)(2,1)} %bitcast.74, bf16[8,3,128,2048]{3,2,1,0:T(8,128)(2,1)} %bitcast.75, bf16[1024,512]{1,0:T(8,128)(2,1)} %shard_map.246.refs_3_, ...), custom_call_target="tpu_custom_call" | custom-call | tf_op jit(solution)/shard_map/pallas_call | solution.py:153
  396.8 23.1 %shard_map.252 = f32[3,512,2048]{2,1,0:T(8,128)} custom-call(s32[4,4]{1,0:T(4,128)} %pad_add_fusion.bounds, s32[4]{0:T(128)} %fusion.21.picks, bf16[8,1,128,2048]{3,2,1,0:T(8,128)(2,1)} %bitcast.86, bf16[8,3,128,2048]{3,2,1,0:T(8,128)(2,1)} %bitcast.77, bf16[8,3,128,2048]{3,2,1,0:T(8,128)(2,1)} %bitcast.78, bf16[8,3,128,2048]{3,2,1,0:T(8,128)(2,1)} %bitcast.79, ...), custom_call_target="tpu_custom_call" | custom-call | tf_op jit(solution)/shard_map/pallas_call | solution.py:190
  429.0 26.4 %shard_map.253 = f32[3,16384,128]{2,1,0:T(8,128)} custom-call(s32[1,4]{1,0:T(1,128)} %slice.88.bounds, s32[2]{0:T(128)} %pad_add_fusion.3.picks, bf16[8,3,128,2048]{3,2,1,0:T(8,128)(2,1)} %bitcast.76, bf16[1024,512]{1,0:T(8,128)(2,1)} %collective-permute-done.33.refs_5_.refs_1_, bf16[1024,512]{1,0:T(8,128)(2,1)} %collective-permute-done.44.refs_2_, ...), custom_call_target="tpu_custom_call" | custom-call | tf_op jit(solution)/shard_map/pallas_call | solution.py:153
  459.3 2.9 collective-permute-start.38
  462.2 2.7 fusion.7
  (295 shorter events, 114.3 us)
Async XLA Ops:
  7.2 142.6 %all-gather.9.cloned.1.call-start = ((), (), s32[]{:S(2)}) async-start(), calls=%async_computation.4 | async-start | bytes 2621440 | tf_op jit(solution)/shard_map/all_gather | solution.py:773
  11.2 25.3 %collective-permute-start.2 = (bf16[144,2048]{1,0:T(8,128)(2,1)S(1)}, bf16[144,2048]{1,0:T(8,128)(2,1)S(1)}, u32[]{:S(2)}, u32[]{:S(2)}) collective-permute-start(bf16[144,2048]{1,0:T(8,128)(2,1)S(1)} %fusion.15.refs_0_), channel_id=1, source_target_pairs={{0,1},{1,0},{2,3},{3,2},{4,5},{5,4},{6,7},{7,6},{8,9},{9,8},{10,11... | collective-permute-start | bytes 1769480 | tf_op jit(solution)/shard_map/ppermute | solution.py:572
  11.7 24.8 %collective-permute-start.1 = (bf16[144,2048]{1,0:T(8,128)(2,1)S(1)}, bf16[144,2048]{1,0:T(8,128)(2,1)S(1)}, u32[]{:S(2)}, u32[]{:S(2)}) collective-permute-start(bf16[144,2048]{1,0:T(8,128)(2,1)S(1)} %fusion.15.refs_0_), channel_id=1, source_target_pairs={{0,4},{1,5},{2,6},{3,7},{4,0},{5,1},{6,2},{7,3},{8,12},{9,13},{10,... | collective-permute-start | bytes 1769480 | tf_op jit(solution)/shard_map/ppermute | solution.py:572
  14.3 22.2 %collective-permute-start = (bf16[144,2048]{1,0:T(8,128)(2,1)S(1)}, bf16[144,2048]{1,0:T(8,128)(2,1)S(1)}, u32[]{:S(2)}, u32[]{:S(2)}) collective-permute-start(bf16[144,2048]{1,0:T(8,128)(2,1)S(1)} %fusion.15.refs_0_), channel_id=1, source_target_pairs={{0,2},{1,3},{2,0},{3,1},{4,6},{5,7},{6,4},{7,5},{8,10},{9,11},{10,... | collective-permute-start | bytes 1769480 | tf_op jit(solution)/shard_map/ppermute | solution.py:572
  57.7 146.0 %all-gather.11.cloned.1.call-start = ((), (), s32[]{:S(2)}) async-start(), calls=%async_computation.5 | async-start | bytes 2621440 | tf_op jit(solution)/shard_map/all_gather | solution.py:791
  58.3 25.5 %collective-permute-start.10 = (bf16[128,2048]{1,0:T(8,128)(2,1)S(1)}, bf16[128,2048]{1,0:T(8,128)(2,1)S(1)}, u32[]{:S(2)}, u32[]{:S(2)}) collective-permute-start(bf16[128,2048]{1,0:T(8,128)(2,1)S(1)} %copy-done.8), channel_id=1, source_target_pairs={{0,1},{1,0},{2,3},{3,2},{4,5},{5,4},{6,7},{7,6},{8,9},{9,8},{10,11... | collective-permute-start | bytes 1572872 | tf_op jit(solution)/shard_map/ppermute | solution.py:572
  58.5 25.3 %collective-permute-start.9 = (bf16[128,2048]{1,0:T(8,128)(2,1)S(1)}, bf16[128,2048]{1,0:T(8,128)(2,1)S(1)}, u32[]{:S(2)}, u32[]{:S(2)}) collective-permute-start(bf16[128,2048]{1,0:T(8,128)(2,1)S(1)} %copy-done.8), channel_id=1, source_target_pairs={{0,4},{1,5},{2,6},{3,7},{4,0},{5,1},{6,2},{7,3},{8,12},{9,13},{10,... | collective-permute-start | bytes 1572872 | tf_op jit(solution)/shard_map/ppermute | solution.py:572
  58.8 25.0 %collective-permute-start.8 = (bf16[128,2048]{1,0:T(8,128)(2,1)S(1)}, bf16[128,2048]{1,0:T(8,128)(2,1)S(1)}, u32[]{:S(2)}, u32[]{:S(2)}) collective-permute-start(bf16[128,2048]{1,0:T(8,128)(2,1)S(1)} %copy-done.8), channel_id=1, source_target_pairs={{0,2},{1,3},{2,0},{3,1},{4,6},{5,7},{6,4},{7,5},{8,10},{9,11},{10,... | collective-permute-start | bytes 1572872 | tf_op jit(solution)/shard_map/ppermute | solution.py:572
  95.3 20.2 %collective-permute-start.19 = (bf16[512,160]{1,0:T(8,128)(2,1)}, bf16[512,160]{1,0:T(8,128)(2,1)S(1)}, u32[]{:S(2)}, u32[]{:S(2)}) collective-permute-start(bf16[512,160]{1,0:T(8,128)(2,1)} %fusion.18), channel_id=1, source_target_pairs={{0,6},{1,7},{2,4},{3,5},{4,2},{5,3},{6,0},{7,1},{8,14},{9,15},{10,... | collective-permute-start | bytes 491528 | tf_op jit(solution)/shard_map/ppermute | solution.py:572
  97.8 17.7 %collective-permute-start.18 = (bf16[512,160]{1,0:T(8,128)(2,1)}, bf16[512,160]{1,0:T(8,128)(2,1)}, u32[]{:S(2)}, u32[]{:S(2)}) collective-permute-start(bf16[512,160]{1,0:T(8,128)(2,1)} %fusion.18), channel_id=1, source_target_pairs={{0,4},{1,5},{2,6},{3,7},{4,0},{5,1},{6,2},{7,3},{8,12},{9,13},{10,... | collective-permute-start | bytes 491528 | tf_op jit(solution)/shard_map/ppermute | solution.py:572
  115.5 171.4 %all-gather.13.cloned.1.call-start = ((), (), s32[]{:S(2)}) async-start(), calls=%async_computation.6 | async-start | bytes 14155776 | tf_op jit(solution)/shard_map/all_gather | solution.py:802
  152.7 192.1 %all-gather.15.cloned.1.call-start = ((), (), s32[]{:S(2)}) async-start(), calls=%async_computation.7 | async-start | bytes 14155776 | tf_op jit(solution)/shard_map/all_gather | solution.py:809
  152.7 53.4 %collective-permute-start.24 = (bf16[1024,1024]{1,0:T(8,128)(2,1)}, bf16[1024,1024]{1,0:T(8,128)(2,1)S(1)}, u32[]{:S(2)}, u32[]{:S(2)}) collective-permute-start(bf16[1024,1024]{1,0:T(8,128)(2,1)} %shard_map.242.refs_3_.refs_4_), channel_id=1, source_target_pairs={{8,0},{16,8},{24,16},{9,1},{17,9},{25,17},{10,2},{18,10},{26,18},{... | collective-permute-start | bytes 6291464 | tf_op jit(solution)/shard_map/ppermute | solution.py:634
  154.0 52.2 %collective-permute-start.23 = (bf16[1024,1024]{1,0:T(8,128)(2,1)}, bf16[1024,1024]{1,0:T(8,128)(2,1)}, u32[]{:S(2)}, u32[]{:S(2)}) collective-permute-start(bf16[1024,1024]{1,0:T(8,128)(2,1)} %shard_map.242.refs_3_.refs_4_), channel_id=1, source_target_pairs={{0,8},{8,16},{16,24},{1,9},{9,17},{17,25},{2,10},{10,18},{18,26},{... | collective-permute-start | bytes 6291464 | tf_op jit(solution)/shard_map/ppermute | solution.py:633
  209.8 183.8 %reduce-scatter.5.cloned.1.call-start = ((), (), s32[]{:S(2)}) async-start(), calls=%async_computation.3 | async-start | bytes 4718592 | tf_op jit(solution)/shard_map/reduce_scatter | solution.py:624
  210.0 79.0 %collective-permute-start.30 = (bf16[1024,1024]{1,0:T(8,128)(2,1)}, bf16[1024,1024]{1,0:T(8,128)(2,1)}, u32[]{:S(2)}, u32[]{:S(2)}) collective-permute-start(bf16[1024,1024]{1,0:T(8,128)(2,1)} %collective-permute-done.23.refs_4_.refs_5_), channel_id=1, source_target_pairs={{0,8},{8,16},{16,24},{1,9},{9,17},{17,25},{2,10},{10,18},{18,26},{... | collective-permute-start | bytes 6291464 | tf_op jit(solution)/shard_map/ppermute | solution.py:633
  215.3 73.7 %collective-permute-start.31 = (bf16[1024,1024]{1,0:T(8,128)(2,1)S(1)}, bf16[1024,1024]{1,0:T(8,128)(2,1)}, u32[]{:S(2)}, u32[]{:S(2)}) collective-permute-start(bf16[1024,1024]{1,0:T(8,128)(2,1)S(1)} %collective-permute-done.24.refs_5_.refs_6_.refs_9_.refs_4_), channel_id=1, source_target_pairs={{8,0},{16,8},{24,16},{9,1},{17,9},{25,17},{10,2},{18,10},{26,18},{... | collective-permute-start | bytes 6291464 | tf_op jit(solution)/shard_map/ppermute | solution.py:634
  220.1 19.2 %collective-permute-start.27 = (bf16[512,160]{1,0:T(8,128)(2,1)S(1)}, bf16[512,160]{1,0:T(8,128)(2,1)S(1)}, u32[]{:S(2)}, u32[]{:S(2)}) collective-permute-start(bf16[512,160]{1,0:T(8,128)(2,1)S(1)} %convert_element_type.114), channel_id=1, source_target_pairs={{0,4},{1,5},{2,6},{3,7},{4,0},{5,1},{6,2},{7,3},{8,12},{9,13},{10,... | collective-permute-start | bytes 491528 | tf_op jit(solution)/shard_map/ppermute | solution.py:572
  220.7 23.9 %collective-permute-start.26 = (bf16[512,160]{1,0:T(8,128)(2,1)S(1)}, bf16[512,160]{1,0:T(8,128)(2,1)}, u32[]{:S(2)}, u32[]{:S(2)}) collective-permute-start(bf16[512,160]{1,0:T(8,128)(2,1)S(1)} %convert_element_type.114), channel_id=1, source_target_pairs={{0,2},{1,3},{2,0},{3,1},{4,6},{5,7},{6,4},{7,5},{8,10},{9,11},{10,... | collective-permute-start | bytes 491528 | tf_op jit(solution)/shard_map/ppermute | solution.py:572
  259.4 28.4 %collective-permute-start.33 = (bf16[1024,512]{1,0:T(8,128)(2,1)}, bf16[1024,512]{1,0:T(8,128)(2,1)}, u32[]{:S(2)}, u32[]{:S(2)}) collective-permute-start(bf16[1024,512]{1,0:T(8,128)(2,1)} %shard_map.246.refs_3_), channel_id=1, source_target_pairs={{8,0},{16,8},{24,16},{9,1},{17,9},{25,17},{10,2},{18,10},{26,18},{... | collective-permute-start | bytes 3145736 | tf_op jit(solution)/shard_map/ppermute | solution.py:634
  260.7 28.3 %collective-permute-start.32 = (bf16[1024,512]{1,0:T(8,128)(2,1)}, bf16[1024,512]{1,0:T(8,128)(2,1)}, u32[]{:S(2)}, u32[]{:S(2)}) collective-permute-start(bf16[1024,512]{1,0:T(8,128)(2,1)} %shard_map.246.refs_3_), channel_id=1, source_target_pairs={{0,8},{8,16},{16,24},{1,9},{9,17},{17,25},{2,10},{10,18},{18,26},{... | collective-permute-start | bytes 3145736 | tf_op jit(solution)/shard_map/ppermute | solution.py:633
  289.1 173.1 %reduce-scatter.3.cloned.1.call-start = ((), (), s32[]{:S(2)}) async-start(), calls=%async_computation.2 | async-start | bytes 4718592 | tf_op jit(solution)/shard_map/reduce_scatter | solution.py:624
  289.6 77.8 %collective-permute-start.40 = (bf16[1024,1024]{1,0:T(8,128)(2,1)}, bf16[1024,1024]{1,0:T(8,128)(2,1)S(1)}, u32[]{:S(2)}, u32[]{:S(2)}) collective-permute-start(bf16[1024,1024]{1,0:T(8,128)(2,1)} %collective-permute-done.30.refs_6_.refs_7_), channel_id=1, source_target_pairs={{0,8},{8,16},{16,24},{1,9},{9,17},{17,25},{2,10},{10,18},{18,26},{... | collective-permute-start | bytes 6291464 | tf_op jit(solution)/shard_map/ppermute | solution.py:633
  294.2 73.3 %collective-permute-start.41 = (bf16[1024,1024]{1,0:T(8,128)(2,1)}, bf16[1024,1024]{1,0:T(8,128)(2,1)}, u32[]{:S(2)}, u32[]{:S(2)}) collective-permute-start(bf16[1024,1024]{1,0:T(8,128)(2,1)} %collective-permute-done.31.refs_7_.refs_8_), channel_id=1, source_target_pairs={{8,0},{16,8},{24,16},{9,1},{17,9},{25,17},{10,2},{18,10},{26,18},{... | collective-permute-start | bytes 6291464 | tf_op jit(solution)/shard_map/ppermute | solution.py:634
  296.2 66.7 %collective-permute-start.42 = (bf16[1024,512]{1,0:T(8,128)(2,1)}, bf16[1024,512]{1,0:T(8,128)(2,1)}, u32[]{:S(2)}, u32[]{:S(2)}) collective-permute-start(bf16[1024,512]{1,0:T(8,128)(2,1)} %collective-permute-done.32.refs_4_), channel_id=1, source_target_pairs={{0,8},{8,16},{16,24},{1,9},{9,17},{17,25},{2,10},{10,18},{18,26},{... | collective-permute-start | bytes 3145736 | tf_op jit(solution)/shard_map/ppermute | solution.py:633
  301.8 65.6 %collective-permute-start.43 = (bf16[1024,512]{1,0:T(8,128)(2,1)}, bf16[1024,512]{1,0:T(8,128)(2,1)}, u32[]{:S(2)}, u32[]{:S(2)}) collective-permute-start(bf16[1024,512]{1,0:T(8,128)(2,1)} %collective-permute-done.33.refs_5_.refs_1_), channel_id=1, source_target_pairs={{8,0},{16,8},{24,16},{9,1},{17,9},{25,17},{10,2},{18,10},{26,18},{... | collective-permute-start | bytes 3145736 | tf_op jit(solution)/shard_map/ppermute | solution.py:634
  341.7 45.7 %collective-permute-start.39 = (bf16[1244,128]{1,0:T(8,128)(2,1)S(1)}, bf16[1244,128]{1,0:T(8,128)(2,1)S(1)}, u32[]{:S(2)}, u32[]{:S(2)}) collective-permute-start(bf16[1244,128]{1,0:T(8,128)(2,1)S(1)} %convert_element_type.123), channel_id=1, source_target_pairs={{0,8},{8,0},{16,24},{24,16},{1,9},{9,1},{17,25},{25,17},{2,10},{10... | collective-permute-start | bytes 955400 | tf_op jit(solution)/shard_map/ppermute | solution.py:668
  387.5 34.0 %collective-permute-start.46 = (bf16[1244,128]{1,0:T(8,128)(2,1)S(1)}, bf16[1244,128]{1,0:T(8,128)(2,1)S(1)}, u32[]{:S(2)}, u32[]{:S(2)}) collective-permute-start(bf16[1244,128]{1,0:T(8,128)(2,1)S(1)} %fusion.17), channel_id=1, source_target_pairs={{0,16},{8,24},{16,0},{24,8},{1,17},{9,25},{17,1},{25,9},{2,18},{10... | collective-permute-start | bytes 955400 | tf_op jit(solution)/shard_map/ppermute | solution.py:668
  389.5 39.5 %collective-permute-start.44 = (bf16[1024,512]{1,0:T(8,128)(2,1)}, bf16[1024,512]{1,0:T(8,128)(2,1)}, u32[]{:S(2)}, u32[]{:S(2)}) collective-permute-start(bf16[1024,512]{1,0:T(8,128)(2,1)} %collective-permute-done.42.refs_6_), channel_id=1, source_target_pairs={{0,8},{8,16},{16,24},{1,9},{9,17},{17,25},{2,10},{10,18},{18,26},{... | collective-permute-start | bytes 3145736 | tf_op jit(solution)/shard_map/ppermute | solution.py:633
  392.0 37.0 %collective-permute-start.45 = (bf16[1024,512]{1,0:T(8,128)(2,1)}, bf16[1024,512]{1,0:T(8,128)(2,1)}, u32[]{:S(2)}, u32[]{:S(2)}) collective-permute-start(bf16[1024,512]{1,0:T(8,128)(2,1)} %collective-permute-done.43.refs_7_), channel_id=1, source_target_pairs={{8,0},{16,8},{24,16},{9,1},{17,9},{25,17},{10,2},{18,10},{26,18},{... | collective-permute-start | bytes 3145736 | tf_op jit(solution)/shard_map/ppermute | solution.py:634
  394.9 25.0 %collective-permute-start.34 = (f32[2048]{0:T(1024)S(1)}, f32[2048]{0:T(1024)S(1)}, u32[]{:S(2)}, u32[]{:S(2)}) collective-permute-start(f32[2048]{0:T(1024)S(1)} %get-tuple-element.275), channel_id=1, source_target_pairs={{0,1},{1,0},{2,3},{3,2},{4,5},{5,4},{6,7},{7,6},{8,9},{9,8},{10,11... | collective-permute-start | bytes 24584 | tf_op jit(solution)/shard_map/ppermute | solution.py:572
  423.7 31.7 %collective-permute-start.36 = (f32[2048]{0:T(1024)S(1)}, f32[2048]{0:T(1024)S(1)}, u32[]{:S(2)}, u32[]{:S(2)}) collective-permute-start(f32[2048]{0:T(1024)S(1)} %add.206), channel_id=1, source_target_pairs={{0,4},{1,5},{2,6},{3,7},{4,0},{5,1},{6,2},{7,3},{8,12},{9,13},{10,... | collective-permute-start | bytes 24584 | tf_op jit(solution)/shard_map/ppermute | solution.py:572
  (60 other events, 784.8 us)
Sparse Core Ops, SparseCore 0:
  57.9 46.2 all-gather.8
  115.6 48.8 all-gather.10
  166.4 85.5 all-gather.12
  253.8 72.1 all-gather.14
  329.8 51.3 reduce-scatter.4
  384.7 51.3 reduce-scatter.2
